TPU v7x, 128 devices: a whole 4x4x4 slice. The times are simulated.
128 devices in a mesh: dp: 128 (over z, y, x, core).
Axes of the slice: x: 4, y: 4, z: 4, core: 2. Of those that a mesh axis runs over, the one named last changes fastest.
Arguments:
- embeddings: bfloat16 [131072, 1024], P('dp')
- partners: int32 [128, 13], P('dp'), may hold values from 0 to 127, as said below
- pair_count: int32 [128], P('dp'), may hold values from 1 to 13, as said below
Outputs:
- soft_cosine: float32 [131072], P('dp')
Inputs may be any that keep to these rules, and one draw needn't show every extreme that they name: Entry 0 of partners[h] is h; the live entries of partners[h] are distinct blocks from h to min(h + 16, 127), so each unordered pair of blocks stands once; entries past pair_count[h] are arbitrary blocks in that range and are not pairs. `pair_count`: at most 13 live pairs for one block; some block has exactly 13.
All inputs are finite; a program needn't handle non-finite values.
Results may differ from a plain program's by a relative error of at most 0.00043.
Values may be sent and summed in bfloat16 or wider, within the bound.
No kernel may reach another device: no remote copies, remote signals or barrier semaphores. Data moves between devices by JAX's collectives and lax.ppermute only.
A program may use at most 128 MiB of HBM per device.

v0:
```python
import jax
import jax.numpy as jnp
from jax import lax
from jax.sharding import PartitionSpec as P

WIN = 16


SCALE = 256.0
FLOOR = -1e30


def shifted(value, axis, steps):
    count = lax.axis_size(axis)
    initial, last = (max(0, -steps), min(count, count - steps))
    return lax.ppermute(value, axis, [(source, source + steps) for source in range(initial, last)])


def normalize(embeddings):
    values = embeddings.astype(jnp.float32)
    return (values * lax.rsqrt(jnp.sum(values * values, -1, keepdims=True) + 1e-06)).astype(
        jnp.bfloat16
    )


def merge(first_m, first_s, second_m, second_s):
    top = jnp.maximum(first_m, second_m)
    return (top, first_s * jnp.exp(first_m - top) + second_s * jnp.exp(second_m - top))


def products(left, right):
    return (
        lax.dot_general(left, right, (((1,), (1,)), ((), ())), preferred_element_type=jnp.float32)
        * SCALE
    )


def body(embeddings, partners, pair_count):
    unit = normalize(embeddings)
    rows = unit.shape[0]
    mine = lax.axis_index("dp")
    slots = partners[0]
    live = jnp.arange(slots.shape[0]) < pair_count[0]
    eye = jnp.arange(rows)[:, None] == jnp.arange(rows)[None, :]
    own_scores = jnp.where(eye, FLOOR, products(unit, unit))
    row_m = jnp.max(own_scores, 1)
    row_s = jnp.sum(jnp.exp(own_scores - row_m[:, None]), 1)
    empty_m = jnp.full((rows,), FLOOR, jnp.float32)
    empty_s = jnp.zeros((rows,), jnp.float32)

    def pair_stats(other):
        scores = products(unit, other)
        part_m = jnp.max(scores, 1)
        part_s = jnp.sum(jnp.exp(scores - part_m[:, None]), 1)
        col_m = jnp.max(scores, 0)
        col_s = jnp.sum(jnp.exp(scores - col_m[None, :]), 0)
        return (part_m, part_s, col_m, col_s)

    def skipped(other):
        return (empty_m, empty_s, empty_m, empty_s)

    for offset in range(1, WIN + 1):
        other = shifted(unit, "dp", -offset)
        present = jnp.any(live & (slots == mine + offset))
        part_m, part_s, col_m, col_s = lax.cond(present, pair_stats, skipped, other)
        row_m, row_s = merge(row_m, row_s, part_m, part_s)
        back_m, back_s = shifted((col_m, col_s), "dp", offset)
        row_m, row_s = merge(row_m, row_s, back_m, back_s)
    return (row_m + jnp.log(row_s)) / SCALE


def solution(mesh):
    placed = (P("dp", None), P("dp", None), P("dp"))
    return jax.shard_map(body, mesh=mesh, in_specs=placed, out_specs=P("dp"), check_vma=False)
```

profile of v0, /device:TPU:34, one launch (start us, length us, event | category | flops | bytes accessed | tf_op | source)
XLA Modules:
  0.0 1027.9 jit_solution(543566094756527849)
XLA Ops:
  0.0 2.1 fusion
  2.1 2.0 fusion.1
  4.1 4.6 collective-permute-start.30
  8.8 1.9 collective-permute-start.28
  10.7 3.2 collective-permute-start.26
  13.9 1.9 collective-permute-start.24
  15.8 2.6 collective-permute-start.22
  18.4 126.4 %collective-permute-done.30 = bf16[1024,1024]{1,0:T(8,128)(2,1)S(1)} collective-permute-done((bf16[1024,1024]{1,0:T(8,128)(2,1)S(1)}, bf16[1024,1024]{1,0:T(8,128)(2,1)S(1)}, u32[]{:S(2)}, u32[]{:S(2)}) %collective-permute-start.30) | collective-permute-done | bytes 2097184 | tf_op jit(solution)/shard_map/ppermute | solution.py:16
  144.8 73.1 %collective-permute-start.20 = (bf16[1024,1024]{1,0:T(8,128)(2,1)S(1)}, bf16[1024,1024]{1,0:T(8,128)(2,1)}, u32[]{:S(2)}, u32[]{:S(2)}) collective-permute-start(bf16[1024,1024]{1,0:T(8,128)(2,1)S(1)} %fusion.1), channel_id=1, source_target_pairs={{11,0},{12,1},{13,2},{14,3},{15,4},{16,5},{17,6},{18,7},{19,8},{20... | collective-permute-start | bytes 6291464 | tf_op jit(solution)/shard_map/ppermute | solution.py:16
  217.9 64.2 %collective-permute-start.18 = (bf16[1024,1024]{1,0:T(8,128)(2,1)S(1)}, bf16[1024,1024]{1,0:T(8,128)(2,1)S(1)}, u32[]{:S(2)}, u32[]{:S(2)}) collective-permute-start(bf16[1024,1024]{1,0:T(8,128)(2,1)S(1)} %fusion.1), channel_id=1, source_target_pairs={{10,0},{11,1},{12,2},{13,3},{14,4},{15,5},{16,6},{17,7},{18,8},{19... | collective-permute-start | bytes 6291464 | tf_op jit(solution)/shard_map/ppermute | solution.py:16
  282.1 1.9 collective-permute-start.16
  284.0 132.6 %collective-permute-start.14 = (bf16[1024,1024]{1,0:T(8,128)(2,1)S(1)}, bf16[1024,1024]{1,0:T(8,128)(2,1)S(1)}, u32[]{:S(2)}, u32[]{:S(2)}) collective-permute-start(bf16[1024,1024]{1,0:T(8,128)(2,1)S(1)} %fusion.1), channel_id=1, source_target_pairs={{8,0},{9,1},{10,2},{11,3},{12,4},{13,5},{14,6},{15,7},{16,8},{17,9... | collective-permute-start | bytes 6291464 | tf_op jit(solution)/shard_map/ppermute | solution.py:16
  416.7 1.9 collective-permute-start.12
  418.7 8.1 collective-permute-start.10
  426.8 1.9 collective-permute-start.8
  428.7 96.5 %collective-permute-done.16 = bf16[1024,1024]{1,0:T(8,128)(2,1)S(1)} collective-permute-done((bf16[1024,1024]{1,0:T(8,128)(2,1)S(1)}, bf16[1024,1024]{1,0:T(8,128)(2,1)S(1)}, u32[]{:S(2)}, u32[]{:S(2)}) %collective-permute-start.16) | collective-permute-done | bytes 2097184 | tf_op jit(solution)/shard_map/ppermute | solution.py:16
  525.2 78.5 %collective-permute-start.6 = (bf16[1024,1024]{1,0:T(8,128)(2,1)S(1)}, bf16[1024,1024]{1,0:T(8,128)(2,1)}, u32[]{:S(2)}, u32[]{:S(2)}) collective-permute-start(bf16[1024,1024]{1,0:T(8,128)(2,1)S(1)} %fusion.1), channel_id=1, source_target_pairs={{4,0},{5,1},{6,2},{7,3},{8,4},{9,5},{10,6},{11,7},{12,8},{13,9},{1... | collective-permute-start | bytes 6291464 | tf_op jit(solution)/shard_map/ppermute | solution.py:16
  603.7 85.1 %collective-permute-start.4 = (bf16[1024,1024]{1,0:T(8,128)(2,1)S(1)}, bf16[1024,1024]{1,0:T(8,128)(2,1)}, u32[]{:S(2)}, u32[]{:S(2)}) collective-permute-start(bf16[1024,1024]{1,0:T(8,128)(2,1)S(1)} %fusion.1), channel_id=1, source_target_pairs={{3,0},{4,1},{5,2},{6,3},{7,4},{8,5},{9,6},{10,7},{11,8},{12,9},{13... | collective-permute-start | bytes 6291464 | tf_op jit(solution)/shard_map/ppermute | solution.py:16
  688.9 11.0 %collective-permute-start.2 = (bf16[1024,1024]{1,0:T(8,128)(2,1)S(1)}, bf16[1024,1024]{1,0:T(8,128)(2,1)}, u32[]{:S(2)}, u32[]{:S(2)}) collective-permute-start(bf16[1024,1024]{1,0:T(8,128)(2,1)S(1)} %fusion.1), channel_id=1, source_target_pairs={{2,0},{3,1},{4,2},{5,3},{6,4},{7,5},{8,6},{9,7},{10,8},{11,9},{12,... | collective-permute-start | bytes 6291464 | tf_op jit(solution)/shard_map/ppermute | solution.py:16
  701.2 11.0 %collective-permute-start = (bf16[1024,1024]{1,0:T(8,128)(2,1)S(1)}, bf16[1024,1024]{1,0:T(8,128)(2,1)}, u32[]{:S(2)}, u32[]{:S(2)}) collective-permute-start(bf16[1024,1024]{1,0:T(8,128)(2,1)S(1)} %fusion.1), channel_id=1, source_target_pairs={{1,0},{2,1},{3,2},{4,3},{5,4},{6,5},{7,6},{8,7},{9,8},{10,9},{11,1... | collective-permute-start | bytes 6291464 | tf_op jit(solution)/shard_map/ppermute | solution.py:16
  715.7 5.0 collective-permute-start.31
  720.8 3.5 collective-permute-start.47
  726.1 7.4 conditional.30
  726.6 4.6 multiply_reduce_fusion.28
  731.2 2.2 exponential_reduce_fusion.28
  734.7 6.9 conditional.28
  734.7 4.6 multiply_reduce_fusion.24
  739.3 2.2 exponential_reduce_fusion.24
  741.5 10.9 %collective-permute-done.4 = bf16[1024,1024]{1,0:T(8,128)(2,1)} collective-permute-done((bf16[1024,1024]{1,0:T(8,128)(2,1)S(1)}, bf16[1024,1024]{1,0:T(8,128)(2,1)}, u32[]{:S(2)}, u32[]{:S(2)}) %collective-permute-start.4) | collective-permute-done | bytes 2097184 | tf_op jit(solution)/shard_map/ppermute | solution.py:16
  752.4 2.6 collective-permute-start.29
  755.0 24.3 %collective-permute-done.2 = bf16[1024,1024]{1,0:T(8,128)(2,1)} collective-permute-done((bf16[1024,1024]{1,0:T(8,128)(2,1)S(1)}, bf16[1024,1024]{1,0:T(8,128)(2,1)}, u32[]{:S(2)}, u32[]{:S(2)}) %collective-permute-start.2) | collective-permute-done | bytes 2097184 | tf_op jit(solution)/shard_map/ppermute | solution.py:16
  779.3 20.7 %collective-permute-start.46 = (f32[1024]{0:T(1024)S(1)}, f32[1024]{0:T(1024)S(1)}, u32[]{:S(2)}, u32[]{:S(2)}) collective-permute-start(f32[1024]{0:T(1024)S(1)} %get-tuple-element.226), channel_id=1, source_target_pairs={{0,15},{1,16},{2,17},{3,18},{4,19},{5,20},{6,21},{7,22},{8,23},{9,... | collective-permute-start | bytes 12296 | tf_op jit(solution)/shard_map/ppermute | solution.py:16
  801.7 5.3 collective-permute-start.27
  807.1 5.0 collective-permute-start.45
  812.0 4.4 collective-permute-start.25
  817.6 7.1 conditional.27
  817.8 4.6 multiply_reduce_fusion.22
  822.5 2.2 exponential_reduce_fusion.22
  827.8 6.6 collective-permute-start.23
  836.4 5.8 collective-permute-start.21
  842.3 10.3 %collective-permute-start.42 = (f32[1024]{0:T(1024)S(1)}, f32[1024]{0:T(1024)S(1)}, u32[]{:S(2)}, u32[]{:S(2)}) collective-permute-start(f32[1024]{0:T(1024)S(1)} %get-tuple-element.218), channel_id=1, source_target_pairs={{0,11},{1,12},{2,13},{3,14},{4,15},{5,16},{6,17},{7,18},{8,19},{9,... | collective-permute-start | bytes 12296 | tf_op jit(solution)/shard_map/ppermute | solution.py:16
  862.0 11.3 %collective-permute-start.17 = (f32[1024]{0:T(1024)}, f32[1024]{0:T(1024)S(1)}, u32[]{:S(2)}, u32[]{:S(2)}) collective-permute-start(f32[1024]{0:T(1024)} %get-tuple-element.182), channel_id=1, source_target_pairs={{0,9},{1,10},{2,11},{3,12},{4,13},{5,14},{6,15},{7,16},{8,17},{9,1... | collective-permute-start | bytes 12296 | tf_op jit(solution)/shard_map/ppermute | solution.py:16
  879.5 7.3 conditional.21
  879.9 4.6 multiply_reduce_fusion.10
  884.5 2.2 exponential_reduce_fusion.10
  886.8 1.9 collective-permute-start.39
  888.7 3.1 collective-permute-start.13
  895.7 7.9 collective-permute-start.37
  905.4 6.9 conditional.20
  905.4 4.6 multiply_reduce_fusion.8
  910.1 2.2 exponential_reduce_fusion.8
  912.3 6.9 conditional.19
  912.3 4.6 multiply_reduce_fusion.6
  917.0 2.2 exponential_reduce_fusion.6
  924.5 9.5 collective-permute-start.7
  933.9 10.2 collective-permute-start.35
  944.1 10.2 collective-permute-start.5
  954.3 4.3 fusion.2
  962.5 19.9 %collective-permute-start.34 = (f32[1024]{0:T(1024)S(1)}, f32[1024]{0:T(1024)S(1)}, u32[]{:S(2)}, u32[]{:S(2)}) collective-permute-start(f32[1024]{0:T(1024)S(1)} %get-tuple-element.202), channel_id=1, source_target_pairs={{0,3},{1,4},{2,5},{3,6},{4,7},{5,8},{6,9},{7,10},{8,11},{9,12},{10... | collective-permute-start | bytes 12296 | tf_op jit(solution)/shard_map/ppermute | solution.py:16
  982.4 10.2 collective-permute-start.3
  992.6 10.2 collective-permute-start.33
  1002.8 10.2 collective-permute-start.1
  1013.0 10.2 collective-permute-start.32
  1023.2 3.0 exponential_reduce_fusion.32
  (127 shorter events, 49.3 us)
Async XLA Ops:
  0.0 712.9 %copy-start = (s32[1,13]{1,0:T(1,128)S(1)}, s32[1,13]{1,0:T(1,128)}, u32[]{:S(2)}) copy-start(s32[1,13]{1,0:T(1,128)} %param.36) | copy-start | bytes 160
  4.1 140.7 %collective-permute-start.30 = (bf16[1024,1024]{1,0:T(8,128)(2,1)S(1)}, bf16[1024,1024]{1,0:T(8,128)(2,1)S(1)}, u32[]{:S(2)}, u32[]{:S(2)}) collective-permute-start(bf16[1024,1024]{1,0:T(8,128)(2,1)S(1)} %fusion.1), channel_id=1, source_target_pairs={{16,0},{17,1},{18,2},{19,3},{20,4},{21,5},{22,6},{23,7},{24,8},{25... | collective-permute-start | bytes 6291464 | tf_op jit(solution)/shard_map/ppermute | solution.py:16
  8.8 209.1 %collective-permute-start.28 = (bf16[1024,1024]{1,0:T(8,128)(2,1)S(1)}, bf16[1024,1024]{1,0:T(8,128)(2,1)S(1)}, u32[]{:S(2)}, u32[]{:S(2)}) collective-permute-start(bf16[1024,1024]{1,0:T(8,128)(2,1)S(1)} %fusion.1), channel_id=1, source_target_pairs={{15,0},{16,1},{17,2},{18,3},{19,4},{20,5},{21,6},{22,7},{23,8},{24... | collective-permute-start | bytes 6291464 | tf_op jit(solution)/shard_map/ppermute | solution.py:16
  10.7 271.4 %collective-permute-start.26 = (bf16[1024,1024]{1,0:T(8,128)(2,1)S(1)}, bf16[1024,1024]{1,0:T(8,128)(2,1)S(1)}, u32[]{:S(2)}, u32[]{:S(2)}) collective-permute-start(bf16[1024,1024]{1,0:T(8,128)(2,1)S(1)} %fusion.1), channel_id=1, source_target_pairs={{14,0},{15,1},{16,2},{17,3},{18,4},{19,5},{20,6},{21,7},{22,8},{23... | collective-permute-start | bytes 6291464 | tf_op jit(solution)/shard_map/ppermute | solution.py:16
  13.9 270.2 %collective-permute-start.24 = (bf16[1024,1024]{1,0:T(8,128)(2,1)S(1)}, bf16[1024,1024]{1,0:T(8,128)(2,1)S(1)}, u32[]{:S(2)}, u32[]{:S(2)}) collective-permute-start(bf16[1024,1024]{1,0:T(8,128)(2,1)S(1)} %fusion.1), channel_id=1, source_target_pairs={{13,0},{14,1},{15,2},{16,3},{17,4},{18,5},{19,6},{20,7},{21,8},{22... | collective-permute-start | bytes 6291464 | tf_op jit(solution)/shard_map/ppermute | solution.py:16
  15.8 400.9 %collective-permute-start.22 = (bf16[1024,1024]{1,0:T(8,128)(2,1)S(1)}, bf16[1024,1024]{1,0:T(8,128)(2,1)}, u32[]{:S(2)}, u32[]{:S(2)}) collective-permute-start(bf16[1024,1024]{1,0:T(8,128)(2,1)S(1)} %fusion.1), channel_id=1, source_target_pairs={{12,0},{13,1},{14,2},{15,3},{16,4},{17,5},{18,6},{19,7},{20,8},{21... | collective-permute-start | bytes 6291464 | tf_op jit(solution)/shard_map/ppermute | solution.py:16
  144.8 137.3 %copy-start.9 = (bf16[1024,1024]{1,0:T(8,128)(2,1)}, bf16[1024,1024]{1,0:T(8,128)(2,1)S(1)}, u32[]{:S(2)}) copy-start(bf16[1024,1024]{1,0:T(8,128)(2,1)S(1)} %collective-permute-done.30) | copy-start | bytes 6291460
  144.8 273.9 %collective-permute-start.20 = (bf16[1024,1024]{1,0:T(8,128)(2,1)S(1)}, bf16[1024,1024]{1,0:T(8,128)(2,1)}, u32[]{:S(2)}, u32[]{:S(2)}) collective-permute-start(bf16[1024,1024]{1,0:T(8,128)(2,1)S(1)} %fusion.1), channel_id=1, source_target_pairs={{11,0},{12,1},{13,2},{14,3},{15,4},{16,5},{17,6},{18,7},{19,8},{20... | collective-permute-start | bytes 6291464 | tf_op jit(solution)/shard_map/ppermute | solution.py:16
  217.8 66.2 %copy-start.8 = (bf16[1024,1024]{1,0:T(8,128)(2,1)}, bf16[1024,1024]{1,0:T(8,128)(2,1)S(1)}, u32[]{:S(2)}) copy-start(bf16[1024,1024]{1,0:T(8,128)(2,1)S(1)} %collective-permute-done.28) | copy-start | bytes 6291460
  217.9 208.9 %collective-permute-start.18 = (bf16[1024,1024]{1,0:T(8,128)(2,1)S(1)}, bf16[1024,1024]{1,0:T(8,128)(2,1)S(1)}, u32[]{:S(2)}, u32[]{:S(2)}) collective-permute-start(bf16[1024,1024]{1,0:T(8,128)(2,1)S(1)} %fusion.1), channel_id=1, source_target_pairs={{10,0},{11,1},{12,2},{13,3},{14,4},{15,5},{16,6},{17,7},{18,8},{19... | collective-permute-start | bytes 6291464 | tf_op jit(solution)/shard_map/ppermute | solution.py:16
  282.1 136.6 %copy-start.7 = (bf16[1024,1024]{1,0:T(8,128)(2,1)}, bf16[1024,1024]{1,0:T(8,128)(2,1)S(1)}, u32[]{:S(2)}) copy-start(bf16[1024,1024]{1,0:T(8,128)(2,1)S(1)} %collective-permute-done.26) | copy-start | bytes 6291460
  282.1 243.1 %collective-permute-start.16 = (bf16[1024,1024]{1,0:T(8,128)(2,1)S(1)}, bf16[1024,1024]{1,0:T(8,128)(2,1)S(1)}, u32[]{:S(2)}, u32[]{:S(2)}) collective-permute-start(bf16[1024,1024]{1,0:T(8,128)(2,1)S(1)} %fusion.1), channel_id=1, source_target_pairs={{9,0},{10,1},{11,2},{12,3},{13,4},{14,5},{15,6},{16,7},{17,8},{18,... | collective-permute-start | bytes 6291464 | tf_op jit(solution)/shard_map/ppermute | solution.py:16
  284.0 132.7 %copy-start.6 = (bf16[1024,1024]{1,0:T(8,128)(2,1)}, bf16[1024,1024]{1,0:T(8,128)(2,1)S(1)}, u32[]{:S(2)}) copy-start(bf16[1024,1024]{1,0:T(8,128)(2,1)S(1)} %collective-permute-done.24) | copy-start | bytes 6291460
  284.0 319.7 %collective-permute-start.14 = (bf16[1024,1024]{1,0:T(8,128)(2,1)S(1)}, bf16[1024,1024]{1,0:T(8,128)(2,1)S(1)}, u32[]{:S(2)}, u32[]{:S(2)}) collective-permute-start(bf16[1024,1024]{1,0:T(8,128)(2,1)S(1)} %fusion.1), channel_id=1, source_target_pairs={{8,0},{9,1},{10,2},{11,3},{12,4},{13,5},{14,6},{15,7},{16,8},{17,9... | collective-permute-start | bytes 6291464 | tf_op jit(solution)/shard_map/ppermute | solution.py:16
  416.7 272.1 %collective-permute-start.12 = (bf16[1024,1024]{1,0:T(8,128)(2,1)S(1)}, bf16[1024,1024]{1,0:T(8,128)(2,1)S(1)}, u32[]{:S(2)}, u32[]{:S(2)}) collective-permute-start(bf16[1024,1024]{1,0:T(8,128)(2,1)S(1)} %fusion.1), channel_id=1, source_target_pairs={{7,0},{8,1},{9,2},{10,3},{11,4},{12,5},{13,6},{14,7},{15,8},{16,9}... | collective-permute-start | bytes 6291464 | tf_op jit(solution)/shard_map/ppermute | solution.py:16
  418.7 281.2 %collective-permute-start.10 = (bf16[1024,1024]{1,0:T(8,128)(2,1)S(1)}, bf16[1024,1024]{1,0:T(8,128)(2,1)S(1)}, u32[]{:S(2)}, u32[]{:S(2)}) collective-permute-start(bf16[1024,1024]{1,0:T(8,128)(2,1)S(1)} %fusion.1), channel_id=1, source_target_pairs={{6,0},{7,1},{8,2},{9,3},{10,4},{11,5},{12,6},{13,7},{14,8},{15,9},... | collective-permute-start | bytes 6291464 | tf_op jit(solution)/shard_map/ppermute | solution.py:16
  426.8 285.4 %copy-start.5 = (bf16[1024,1024]{1,0:T(8,128)(2,1)}, bf16[1024,1024]{1,0:T(8,128)(2,1)S(1)}, u32[]{:S(2)}) copy-start(bf16[1024,1024]{1,0:T(8,128)(2,1)S(1)} %collective-permute-done.18) | copy-start | bytes 6291460
  426.8 288.9 %collective-permute-start.8 = (bf16[1024,1024]{1,0:T(8,128)(2,1)S(1)}, bf16[1024,1024]{1,0:T(8,128)(2,1)}, u32[]{:S(2)}, u32[]{:S(2)}) collective-permute-start(bf16[1024,1024]{1,0:T(8,128)(2,1)S(1)} %fusion.1), channel_id=1, source_target_pairs={{5,0},{6,1},{7,2},{8,3},{9,4},{10,5},{11,6},{12,7},{13,8},{14,9},{... | collective-permute-start | bytes 6291464 | tf_op jit(solution)/shard_map/ppermute | solution.py:16
  525.2 187.0 %copy-start.4 = (bf16[1024,1024]{1,0:T(8,128)(2,1)}, bf16[1024,1024]{1,0:T(8,128)(2,1)S(1)}, u32[]{:S(2)}) copy-start(bf16[1024,1024]{1,0:T(8,128)(2,1)S(1)} %collective-permute-done.16) | copy-start | bytes 6291460
  525.2 195.5 %collective-permute-start.6 = (bf16[1024,1024]{1,0:T(8,128)(2,1)S(1)}, bf16[1024,1024]{1,0:T(8,128)(2,1)}, u32[]{:S(2)}, u32[]{:S(2)}) collective-permute-start(bf16[1024,1024]{1,0:T(8,128)(2,1)S(1)} %fusion.1), channel_id=1, source_target_pairs={{4,0},{5,1},{6,2},{7,3},{8,4},{9,5},{10,6},{11,7},{12,8},{13,9},{1... | collective-permute-start | bytes 6291464 | tf_op jit(solution)/shard_map/ppermute | solution.py:16
  603.7 108.5 %copy-start.3 = (bf16[1024,1024]{1,0:T(8,128)(2,1)}, bf16[1024,1024]{1,0:T(8,128)(2,1)S(1)}, u32[]{:S(2)}) copy-start(bf16[1024,1024]{1,0:T(8,128)(2,1)S(1)} %collective-permute-done.14) | copy-start | bytes 6291460
  603.7 148.7 %collective-permute-start.4 = (bf16[1024,1024]{1,0:T(8,128)(2,1)S(1)}, bf16[1024,1024]{1,0:T(8,128)(2,1)}, u32[]{:S(2)}, u32[]{:S(2)}) collective-permute-start(bf16[1024,1024]{1,0:T(8,128)(2,1)S(1)} %fusion.1), channel_id=1, source_target_pairs={{3,0},{4,1},{5,2},{6,3},{7,4},{8,5},{9,6},{10,7},{11,8},{12,9},{13... | collective-permute-start | bytes 6291464 | tf_op jit(solution)/shard_map/ppermute | solution.py:16
  688.9 23.3 %copy-start.2 = (bf16[1024,1024]{1,0:T(8,128)(2,1)}, bf16[1024,1024]{1,0:T(8,128)(2,1)S(1)}, u32[]{:S(2)}) copy-start(bf16[1024,1024]{1,0:T(8,128)(2,1)S(1)} %collective-permute-done.12) | copy-start | bytes 6291460
  688.9 90.4 %collective-permute-start.2 = (bf16[1024,1024]{1,0:T(8,128)(2,1)S(1)}, bf16[1024,1024]{1,0:T(8,128)(2,1)}, u32[]{:S(2)}, u32[]{:S(2)}) collective-permute-start(bf16[1024,1024]{1,0:T(8,128)(2,1)S(1)} %fusion.1), channel_id=1, source_target_pairs={{2,0},{3,1},{4,2},{5,3},{6,4},{7,5},{8,6},{9,7},{10,8},{11,9},{12,... | collective-permute-start | bytes 6291464 | tf_op jit(solution)/shard_map/ppermute | solution.py:16
  699.9 1.3 copy-start.1
  701.2 100.5 %collective-permute-start = (bf16[1024,1024]{1,0:T(8,128)(2,1)S(1)}, bf16[1024,1024]{1,0:T(8,128)(2,1)}, u32[]{:S(2)}, u32[]{:S(2)}) collective-permute-start(bf16[1024,1024]{1,0:T(8,128)(2,1)S(1)} %fusion.1), channel_id=1, source_target_pairs={{1,0},{2,1},{3,2},{4,3},{5,4},{6,5},{7,6},{8,7},{9,8},{10,9},{11,1... | collective-permute-start | bytes 6291464 | tf_op jit(solution)/shard_map/ppermute | solution.py:16
  715.7 91.3 %collective-permute-start.31 = (f32[1024]{0:T(1024)}, f32[1024]{0:T(1024)S(1)}, u32[]{:S(2)}, u32[]{:S(2)}) collective-permute-start(f32[1024]{0:T(1024)} %get-tuple-element.196), channel_id=1, source_target_pairs={{0,16},{1,17},{2,18},{3,19},{4,20},{5,21},{6,22},{7,23},{8,24},{9,... | collective-permute-start | bytes 12296 | tf_op jit(solution)/shard_map/ppermute | solution.py:16
  720.8 91.3 %collective-permute-start.47 = (f32[1024]{0:T(1024)S(1)}, f32[1024]{0:T(1024)S(1)}, u32[]{:S(2)}, u32[]{:S(2)}) collective-permute-start(f32[1024]{0:T(1024)S(1)} %get-tuple-element.228), channel_id=1, source_target_pairs={{0,16},{1,17},{2,18},{3,19},{4,20},{5,21},{6,22},{7,23},{8,24},{9,... | collective-permute-start | bytes 12296 | tf_op jit(solution)/shard_map/ppermute | solution.py:16
  752.4 73.5 %collective-permute-start.29 = (f32[1024]{0:T(1024)}, f32[1024]{0:T(1024)S(1)}, u32[]{:S(2)}, u32[]{:S(2)}) collective-permute-start(f32[1024]{0:T(1024)} %get-tuple-element.194), channel_id=1, source_target_pairs={{0,15},{1,16},{2,17},{3,18},{4,19},{5,20},{6,21},{7,22},{8,23},{9,... | collective-permute-start | bytes 12296 | tf_op jit(solution)/shard_map/ppermute | solution.py:16
  779.3 48.6 %collective-permute-start.46 = (f32[1024]{0:T(1024)S(1)}, f32[1024]{0:T(1024)S(1)}, u32[]{:S(2)}, u32[]{:S(2)}) collective-permute-start(f32[1024]{0:T(1024)S(1)} %get-tuple-element.226), channel_id=1, source_target_pairs={{0,15},{1,16},{2,17},{3,18},{4,19},{5,20},{6,21},{7,22},{8,23},{9,... | collective-permute-start | bytes 12296 | tf_op jit(solution)/shard_map/ppermute | solution.py:16
  801.7 32.8 %collective-permute-start.27 = (f32[1024]{0:T(1024)}, f32[1024]{0:T(1024)S(1)}, u32[]{:S(2)}, u32[]{:S(2)}) collective-permute-start(f32[1024]{0:T(1024)} %get-tuple-element.192), channel_id=1, source_target_pairs={{0,14},{1,15},{2,16},{3,17},{4,18},{5,19},{6,20},{7,21},{8,22},{9,... | collective-permute-start | bytes 12296 | tf_op jit(solution)/shard_map/ppermute | solution.py:16
  807.1 29.4 %collective-permute-start.45 = (f32[1024]{0:T(1024)S(1)}, f32[1024]{0:T(1024)S(1)}, u32[]{:S(2)}, u32[]{:S(2)}) collective-permute-start(f32[1024]{0:T(1024)S(1)} %get-tuple-element.224), channel_id=1, source_target_pairs={{0,14},{1,15},{2,16},{3,17},{4,18},{5,19},{6,20},{7,21},{8,22},{9,... | collective-permute-start | bytes 12296 | tf_op jit(solution)/shard_map/ppermute | solution.py:16
  812.0 30.2 %collective-permute-start.25 = (f32[1024]{0:T(1024)}, f32[1024]{0:T(1024)S(1)}, u32[]{:S(2)}, u32[]{:S(2)}) collective-permute-start(f32[1024]{0:T(1024)} %get-tuple-element.190), channel_id=1, source_target_pairs={{0,13},{1,14},{2,15},{3,16},{4,17},{5,18},{6,19},{7,20},{8,21},{9,... | collective-permute-start | bytes 12296 | tf_op jit(solution)/shard_map/ppermute | solution.py:16
  825.9 32.2 %collective-permute-start.44 = (f32[1024]{0:T(1024)S(1)}, f32[1024]{0:T(1024)S(1)}, u32[]{:S(2)}, u32[]{:S(2)}) collective-permute-start(f32[1024]{0:T(1024)S(1)} %get-tuple-element.222), channel_id=1, source_target_pairs={{0,13},{1,14},{2,15},{3,16},{4,17},{5,18},{6,19},{7,20},{8,21},{9,... | collective-permute-start | bytes 12296 | tf_op jit(solution)/shard_map/ppermute | solution.py:16
  827.8 32.2 %collective-permute-start.23 = (f32[1024]{0:T(1024)}, f32[1024]{0:T(1024)S(1)}, u32[]{:S(2)}, u32[]{:S(2)}) collective-permute-start(f32[1024]{0:T(1024)} %get-tuple-element.188), channel_id=1, source_target_pairs={{0,12},{1,13},{2,14},{3,15},{4,16},{5,17},{6,18},{7,19},{8,20},{9,... | collective-permute-start | bytes 12296 | tf_op jit(solution)/shard_map/ppermute | solution.py:16
  834.5 27.5 %collective-permute-start.43 = (f32[1024]{0:T(1024)S(1)}, f32[1024]{0:T(1024)S(1)}, u32[]{:S(2)}, u32[]{:S(2)}) collective-permute-start(f32[1024]{0:T(1024)S(1)} %get-tuple-element.220), channel_id=1, source_target_pairs={{0,12},{1,13},{2,14},{3,15},{4,16},{5,17},{6,18},{7,19},{8,20},{9,... | collective-permute-start | bytes 12296 | tf_op jit(solution)/shard_map/ppermute | solution.py:16
  836.4 36.8 %collective-permute-start.21 = (f32[1024]{0:T(1024)}, f32[1024]{0:T(1024)S(1)}, u32[]{:S(2)}, u32[]{:S(2)}) collective-permute-start(f32[1024]{0:T(1024)} %get-tuple-element.186), channel_id=1, source_target_pairs={{0,11},{1,12},{2,13},{3,14},{4,15},{5,16},{6,17},{7,18},{8,19},{9,... | collective-permute-start | bytes 12296 | tf_op jit(solution)/shard_map/ppermute | solution.py:16
  842.3 32.9 %collective-permute-start.42 = (f32[1024]{0:T(1024)S(1)}, f32[1024]{0:T(1024)S(1)}, u32[]{:S(2)}, u32[]{:S(2)}) collective-permute-start(f32[1024]{0:T(1024)S(1)} %get-tuple-element.218), channel_id=1, source_target_pairs={{0,11},{1,12},{2,13},{3,14},{4,15},{5,16},{6,17},{7,18},{8,19},{9,... | collective-permute-start | bytes 12296 | tf_op jit(solution)/shard_map/ppermute | solution.py:16
  858.1 28.7 %collective-permute-start.19 = (f32[1024]{0:T(1024)}, f32[1024]{0:T(1024)S(1)}, u32[]{:S(2)}, u32[]{:S(2)}) collective-permute-start(f32[1024]{0:T(1024)} %get-tuple-element.184), channel_id=1, source_target_pairs={{0,10},{1,11},{2,12},{3,13},{4,14},{5,15},{6,16},{7,17},{8,18},{9,... | collective-permute-start | bytes 12296 | tf_op jit(solution)/shard_map/ppermute | solution.py:16
  860.1 28.7 %collective-permute-start.41 = (f32[1024]{0:T(1024)S(1)}, f32[1024]{0:T(1024)S(1)}, u32[]{:S(2)}, u32[]{:S(2)}) collective-permute-start(f32[1024]{0:T(1024)S(1)} %get-tuple-element.216), channel_id=1, source_target_pairs={{0,10},{1,11},{2,12},{3,13},{4,14},{5,15},{6,16},{7,17},{8,18},{9,... | collective-permute-start | bytes 12296 | tf_op jit(solution)/shard_map/ppermute | solution.py:16
  862.0 29.9 %collective-permute-start.17 = (f32[1024]{0:T(1024)}, f32[1024]{0:T(1024)S(1)}, u32[]{:S(2)}, u32[]{:S(2)}) collective-permute-start(f32[1024]{0:T(1024)} %get-tuple-element.182), channel_id=1, source_target_pairs={{0,9},{1,10},{2,11},{3,12},{4,13},{5,14},{6,15},{7,16},{8,17},{9,1... | collective-permute-start | bytes 12296 | tf_op jit(solution)/shard_map/ppermute | solution.py:16
  873.3 20.5 %collective-permute-start.40 = (f32[1024]{0:T(1024)S(1)}, f32[1024]{0:T(1024)S(1)}, u32[]{:S(2)}, u32[]{:S(2)}) collective-permute-start(f32[1024]{0:T(1024)S(1)} %get-tuple-element.214), channel_id=1, source_target_pairs={{0,9},{1,10},{2,11},{3,12},{4,13},{5,14},{6,15},{7,16},{8,17},{9,1... | collective-permute-start | bytes 12296 | tf_op jit(solution)/shard_map/ppermute | solution.py:16
  875.2 20.5 %collective-permute-start.15 = (f32[1024]{0:T(1024)}, f32[1024]{0:T(1024)S(1)}, u32[]{:S(2)}, u32[]{:S(2)}) collective-permute-start(f32[1024]{0:T(1024)} %get-tuple-element.180), channel_id=1, source_target_pairs={{0,8},{1,9},{2,10},{3,11},{4,12},{5,13},{6,14},{7,15},{8,16},{9,17... | collective-permute-start | bytes 12296 | tf_op jit(solution)/shard_map/ppermute | solution.py:16
  886.8 33.8 %collective-permute-start.39 = (f32[1024]{0:T(1024)S(1)}, f32[1024]{0:T(1024)S(1)}, u32[]{:S(2)}, u32[]{:S(2)}) collective-permute-start(f32[1024]{0:T(1024)S(1)} %get-tuple-element.212), channel_id=1, source_target_pairs={{0,8},{1,9},{2,10},{3,11},{4,12},{5,13},{6,14},{7,15},{8,16},{9,17... | collective-permute-start | bytes 12296 | tf_op jit(solution)/shard_map/ppermute | solution.py:16
  888.7 33.8 %collective-permute-start.13 = (f32[1024]{0:T(1024)}, f32[1024]{0:T(1024)S(1)}, u32[]{:S(2)}, u32[]{:S(2)}) collective-permute-start(f32[1024]{0:T(1024)} %get-tuple-element.178), channel_id=1, source_target_pairs={{0,7},{1,8},{2,9},{3,10},{4,11},{5,12},{6,13},{7,14},{8,15},{9,16}... | collective-permute-start | bytes 12296 | tf_op jit(solution)/shard_map/ppermute | solution.py:16
  891.9 32.6 %collective-permute-start.38 = (f32[1024]{0:T(1024)S(1)}, f32[1024]{0:T(1024)S(1)}, u32[]{:S(2)}, u32[]{:S(2)}) collective-permute-start(f32[1024]{0:T(1024)S(1)} %get-tuple-element.210), channel_id=1, source_target_pairs={{0,7},{1,8},{2,9},{3,10},{4,11},{5,12},{6,13},{7,14},{8,15},{9,16}... | collective-permute-start | bytes 12296 | tf_op jit(solution)/shard_map/ppermute | solution.py:16
  893.8 40.1 %collective-permute-start.11 = (f32[1024]{0:T(1024)}, f32[1024]{0:T(1024)S(1)}, u32[]{:S(2)}, u32[]{:S(2)}) collective-permute-start(f32[1024]{0:T(1024)} %get-tuple-element.176), channel_id=1, source_target_pairs={{0,6},{1,7},{2,8},{3,9},{4,10},{5,11},{6,12},{7,13},{8,14},{9,15},... | collective-permute-start | bytes 12296 | tf_op jit(solution)/shard_map/ppermute | solution.py:16
  895.7 48.4 %collective-permute-start.37 = (f32[1024]{0:T(1024)S(1)}, f32[1024]{0:T(1024)S(1)}, u32[]{:S(2)}, u32[]{:S(2)}) collective-permute-start(f32[1024]{0:T(1024)S(1)} %get-tuple-element.208), channel_id=1, source_target_pairs={{0,6},{1,7},{2,8},{3,9},{4,10},{5,11},{6,12},{7,13},{8,14},{9,15},... | collective-permute-start | bytes 12296 | tf_op jit(solution)/shard_map/ppermute | solution.py:16
  920.6 41.9 %collective-permute-start.9 = (f32[1024]{0:T(1024)}, f32[1024]{0:T(1024)S(1)}, u32[]{:S(2)}, u32[]{:S(2)}) collective-permute-start(f32[1024]{0:T(1024)} %get-tuple-element.174), channel_id=1, source_target_pairs={{0,5},{1,6},{2,7},{3,8},{4,9},{5,10},{6,11},{7,12},{8,13},{9,14},{... | collective-permute-start | bytes 12296 | tf_op jit(solution)/shard_map/ppermute | solution.py:16
  922.5 59.9 %collective-permute-start.36 = (f32[1024]{0:T(1024)S(1)}, f32[1024]{0:T(1024)S(1)}, u32[]{:S(2)}, u32[]{:S(2)}) collective-permute-start(f32[1024]{0:T(1024)S(1)} %get-tuple-element.206), channel_id=1, source_target_pairs={{0,5},{1,6},{2,7},{3,8},{4,9},{5,10},{6,11},{7,12},{8,13},{9,14},{... | collective-permute-start | bytes 12296 | tf_op jit(solution)/shard_map/ppermute | solution.py:16
  924.5 68.1 %collective-permute-start.7 = (f32[1024]{0:T(1024)}, f32[1024]{0:T(1024)S(1)}, u32[]{:S(2)}, u32[]{:S(2)}) collective-permute-start(f32[1024]{0:T(1024)} %get-tuple-element.172), channel_id=1, source_target_pairs={{0,4},{1,5},{2,6},{3,7},{4,8},{5,9},{6,10},{7,11},{8,12},{9,13},{1... | collective-permute-start | bytes 12296 | tf_op jit(solution)/shard_map/ppermute | solution.py:16
  933.9 68.9 %collective-permute-start.35 = (f32[1024]{0:T(1024)S(1)}, f32[1024]{0:T(1024)S(1)}, u32[]{:S(2)}, u32[]{:S(2)}) collective-permute-start(f32[1024]{0:T(1024)S(1)} %get-tuple-element.204), channel_id=1, source_target_pairs={{0,4},{1,5},{2,6},{3,7},{4,8},{5,9},{6,10},{7,11},{8,12},{9,13},{1... | collective-permute-start | bytes 12296 | tf_op jit(solution)/shard_map/ppermute | solution.py:16
  944.1 68.8 %collective-permute-start.5 = (f32[1024]{0:T(1024)}, f32[1024]{0:T(1024)S(1)}, u32[]{:S(2)}, u32[]{:S(2)}) collective-permute-start(f32[1024]{0:T(1024)} %get-tuple-element.170), channel_id=1, source_target_pairs={{0,3},{1,4},{2,5},{3,6},{4,7},{5,8},{6,9},{7,10},{8,11},{9,12},{10... | collective-permute-start | bytes 12296 | tf_op jit(solution)/shard_map/ppermute | solution.py:16
  962.5 63.6 %collective-permute-start.34 = (f32[1024]{0:T(1024)S(1)}, f32[1024]{0:T(1024)S(1)}, u32[]{:S(2)}, u32[]{:S(2)}) collective-permute-start(f32[1024]{0:T(1024)S(1)} %get-tuple-element.202), channel_id=1, source_target_pairs={{0,3},{1,4},{2,5},{3,6},{4,7},{5,8},{6,9},{7,10},{8,11},{9,12},{10... | collective-permute-start | bytes 12296 | tf_op jit(solution)/shard_map/ppermute | solution.py:16
  982.4 43.7 %collective-permute-start.3 = (f32[1024]{0:T(1024)}, f32[1024]{0:T(1024)S(1)}, u32[]{:S(2)}, u32[]{:S(2)}) collective-permute-start(f32[1024]{0:T(1024)} %get-tuple-element.168), channel_id=1, source_target_pairs={{0,2},{1,3},{2,4},{3,5},{4,6},{5,7},{6,8},{7,9},{8,10},{9,11},{10,... | collective-permute-start | bytes 12296 | tf_op jit(solution)/shard_map/ppermute | solution.py:16
  992.6 33.6 %collective-permute-start.33 = (f32[1024]{0:T(1024)S(1)}, f32[1024]{0:T(1024)S(1)}, u32[]{:S(2)}, u32[]{:S(2)}) collective-permute-start(f32[1024]{0:T(1024)S(1)} %get-tuple-element.200), channel_id=1, source_target_pairs={{0,2},{1,3},{2,4},{3,5},{4,6},{5,7},{6,8},{7,9},{8,10},{9,11},{10,... | collective-permute-start | bytes 12296 | tf_op jit(solution)/shard_map/ppermute | solution.py:16
  1002.8 23.4 %collective-permute-start.1 = (f32[1024]{0:T(1024)}, f32[1024]{0:T(1024)S(1)}, u32[]{:S(2)}, u32[]{:S(2)}) collective-permute-start(f32[1024]{0:T(1024)} %get-tuple-element.166), channel_id=1, source_target_pairs={{0,1},{1,2},{2,3},{3,4},{4,5},{5,6},{6,7},{7,8},{8,9},{9,10},{10,1... | collective-permute-start | bytes 12296 | tf_op jit(solution)/shard_map/ppermute | solution.py:16
  1013.0 13.2 %collective-permute-start.32 = (f32[1024]{0:T(1024)S(1)}, f32[1024]{0:T(1024)S(1)}, u32[]{:S(2)}, u32[]{:S(2)}) collective-permute-start(f32[1024]{0:T(1024)S(1)} %get-tuple-element.198), channel_id=1, source_target_pairs={{0,1},{1,2},{2,3},{3,4},{4,5},{5,6},{6,7},{7,8},{8,9},{9,10},{10,1... | collective-permute-start | bytes 12296 | tf_op jit(solution)/shard_map/ppermute | solution.py:16
where the time goes:
time: 1040 us; the launch traced here: 1030 us
  starting transfers between devices  687 us (66%)
  waiting for transfers between devices  260 us (25%)
  matrix products  32.2 us (3%)
  other arithmetic  23 us (2%)
  local copies, waits for them, and re-layouts  13.2 us (1%)
  between operations  11.4 us (1%)
    ppermute x48, starting transfers between devices, shifted(): lax.ppermute(value, axis, [(source, source + steps) for source in range(i...  687 us
    ppermute x48, waiting for transfers between devices, shifted(): lax.ppermute(value, axis, [(source, source + steps) for source in range(i...  260 us
    dot_general x7, matrix products, products(): lax.dot_general(left, right, (((1,), (1,)), ((), ())), preferred_element_...  32.2 us
  transfers between devices with their start and end apart: 48, of which 5 were waited for; matrix products, arithmetic and copies ran while one was open for 6% of the time, Pallas kernels for 0%

commit v1 on v0

v1 whole, which is shorter than its diff:
```python
import functools

import jax
import jax.numpy as jnp
from jax import lax
from jax.experimental import pallas as pl
from jax.experimental.pallas import tpu as pltpu
from jax.sharding import PartitionSpec as P

SCALE = 256.0
LOG2E = 1.4426950408889634
LN2 = 0.6931471805599453
GAIN = SCALE * LOG2E
PLAIN = 78.0 / SCALE
FLOOR = -1e30
MASKED = -1e27
B = 1024
D = 1024
CH = 256
G = 32
COUNT = 128
RING = 8


def around(dx):
    moves = []
    for d in range(COUNT):
        core, x, rest = d % 2, (d // 2) % 4, d // RING
        moves.append((d, rest * RING + ((x + dx) % 4) * 2 + core))
    return moves


def along(steps, flip=0):
    return [(d, (d + steps) ^ flip) for d in range(COUNT) if 0 <= d + steps < COUNT]


def send(value, moves):
    return lax.ppermute(value, "dp", moves)


def unit_kernel(x_ref, o_ref):
    for g in range(x_ref.shape[0] // G):
        v = x_ref[g * G : (g + 1) * G, :].astype(jnp.float32)
        size = jnp.sum(v * v, -1, keepdims=True)
        o_ref[g * G : (g + 1) * G, :] = (v * lax.rsqrt(size + 1e-06)).astype(jnp.bfloat16)


def normalize(embeddings):
    return pl.pallas_call(
        unit_kernel,
        grid=(B // CH,),
        in_specs=[pl.BlockSpec((CH, D), lambda i: (i, 0))],
        out_specs=pl.BlockSpec((CH, D), lambda i: (i, 0)),
        out_shape=jax.ShapeDtypeStruct((B, D), jnp.bfloat16),
        name="unit_rows",
    )(embeddings)


def lanes(value, op):
    return functools.reduce(op, [value[:, q * 128 : (q + 1) * 128] for q in range(value.shape[1] // 128)])


def rows8(value, op):
    return functools.reduce(op, [value[q * 8 : (q + 1) * 8, :] for q in range(value.shape[0] // 8)])


def fold(m, s, f, axis):
    top = jnp.max(m, axis, keepdims=True)
    plain = jnp.sum(f, axis, keepdims=True)
    top = jnp.maximum(top, jnp.where(plain > 0.0, 0.0, FLOOR))
    total = jnp.sum(s * jnp.exp2(m - top), axis, keepdims=True)
    total = total + plain * jnp.exp2(jnp.minimum(-top, 0.0))
    return jnp.maximum(top + jnp.log2(total), FLOOR)


def log2_add(a, b):
    top = jnp.maximum(a, b)
    return top + jnp.log2(jnp.exp2(a - top) + jnp.exp2(b - top))


def stage_kernel(plan, live, prev, *refs):
    nl, nr, lefts, rights, own_first = plan
    blocks, refs = refs[: len(lefts) + len(rights)], refs[len(lefts) + len(rights) :]
    row_out, col_out = refs[:2]
    (lbuf, rbuf, sc, row_t, col_t, chk, row_f, row_m, row_s, col_f, col_m, col_s, waited, lsem, rsem) = refs[2:]

    def copies(side, slot):
        pieces = lefts if side == 0 else rights
        base = 0 if side == 0 else len(lefts)
        buf, sem = (lbuf, lsem) if side == 0 else (rbuf, rsem)
        made = []
        for i, (s, row, count) in enumerate(pieces):
            if s == slot:
                made.append(
                    pltpu.make_async_copy(blocks[base + i], buf.at[slot, row : row + count, :], sem.at[slot])
                )
        return made

    def used(flags):
        return functools.reduce(jnp.logical_or, [f > 0 for f in flags])

    need_l = [used([live[q * nr + r] for r in range(nr)]) for q in range(nl)]
    need_r = [used([live[q * nr + r] for q in range(nl)]) for r in range(nr)]
    for q in range(nl):

        @pl.when(need_l[q])
        def _(q=q):
            for c in copies(0, q):
                c.start()

    for r in range(nr):
        waited[r] = 0

        @pl.when(need_r[r])
        def _(r=r):
            for c in copies(1, r):
                c.start()

    col_f[...] = jnp.zeros_like(col_f)
    col_s[...] = jnp.zeros_like(col_s)
    col_m[...] = jnp.full_like(col_m, FLOOR)

    def pair(q, r, diag):
        def dot(i):
            sc[i * CH : (i + 1) * CH, :] = lax.dot_general(
                lbuf[q, i * CH : (i + 1) * CH, :],
                rbuf[r],
                (((1,), (1,)), ((), ())),
                preferred_element_type=jnp.float32,
            )

        def sums(i):
            cols = jnp.zeros((8, B), jnp.float32)
            size = jnp.zeros((8, 128), jnp.float32)
            for g in range(CH // G):
                at = i * CH + g * G
                v = sc[at : at + G, :]
                if diag:
                    r_at = lax.broadcasted_iota(jnp.int32, (G, B), 0) + at
                    c_at = lax.broadcasted_iota(jnp.int32, (G, B), 1)
                    eye = r_at == c_at
                    absv = jnp.where(eye, 0.0, jnp.abs(v))
                    v = jnp.where(eye, MASKED, v)
                    sc[at : at + G, :] = v
                else:
                    absv = jnp.abs(v)
                e = jnp.exp2(v * GAIN)
                row_t[at : at + G, :] = lanes(e, jnp.add)
                if not diag:
                    cols = cols + rows8(e, jnp.add)
                size = jnp.maximum(size, rows8(lanes(absv, jnp.maximum), jnp.maximum))
            if not diag:
                col_t[...] = cols if i == 0 else col_t[...] + cols
            chk[...] = size if i == 0 else jnp.maximum(chk[...], size)

        n = B // CH
        dot(0)
        for i in range(n):
            if i + 1 < n:
                dot(i + 1)
            sums(i)
        plain = jnp.max(chk[...]) <= PLAIN

        @pl.when(plain)
        def _():
            row_f[...] += row_t[...]
            if not diag:
                col_f[r] += col_t[...]

        @pl.when(jnp.logical_not(plain))
        def _():
            def group(g, _):
                at = pl.multiple_of(g * G, G)
                w = sc[pl.ds(at, G), :] * GAIN
                old = row_m[pl.ds(at, G), :]
                top = jnp.maximum(old, lanes(w, jnp.maximum))
                total = row_s[pl.ds(at, G), :] * jnp.exp2(old - top)
                for k in range(B // 128):
                    total = total + jnp.exp2(w[:, k * 128 : (k + 1) * 128] - top)
                row_m[pl.ds(at, G), :] = top
                row_s[pl.ds(at, G), :] = total
                if not diag:
                    old = col_m[r]
                    top = jnp.maximum(old, rows8(w, jnp.maximum))
                    total = col_s[r] * jnp.exp2(old - top)
                    for k in range(G // 8):
                        total = total + jnp.exp2(w[k * 8 : (k + 1) * 8, :] - top)
                    col_m[r] = top
                    col_s[r] = total
                return 0

            lax.fori_loop(0, B // G, group, 0)

    def arrive(r):
        @pl.when(waited[r] == 0)
        def _():
            for s in range(nr):

                @pl.when(r == s)
                def _(s=s):
                    for c in copies(1, s):
                        c.wait()

            waited[r] = 1

    for q in range(nl):
        row_f[...] = jnp.zeros_like(row_f)
        row_s[...] = jnp.zeros_like(row_s)
        row_m[...] = jnp.full_like(row_m, FLOOR)

        @pl.when(need_l[q])
        def _(q=q):
            for c in copies(0, q):
                c.wait()

        first = 0
        if own_first and q == 0:
            arrive(0)
            pair(0, 0, True)
            first = 1

        def step(r, _, q=q):
            @pl.when(live[q * nr + r] > 0)
            def _():
                arrive(r)
                pair(q, r, False)

            return 0

        lax.fori_loop(first, nr, step, 0)
        row_out[q : q + 1, :] = fold(row_m[...].T, row_s[...].T, row_f[...].T, 0)
    for r in range(nr):
        col_out[r : r + 1, :] = log2_add(fold(col_m[r], col_s[r], col_f[r], 0), prev[r : r + 1, :])


def stage(name, live, prev, lefts, rights, own_first=False):
    nl, nr = len(lefts), len(rights)
    flat, tables = [], []
    for side in (lefts, rights):
        table = []
        for slot, pieces in enumerate(side):
            for array, row in pieces:
                flat.append(array)
                table.append((slot, row, array.shape[0]))
        tables.append(tuple(table))
    plan = (nl, nr, tables[0], tables[1], own_first)
    f32 = jnp.float32
    return pl.pallas_call(
        functools.partial(stage_kernel, plan),
        out_shape=[jax.ShapeDtypeStruct((nl, B), f32), jax.ShapeDtypeStruct((nr, B), f32)],
        in_specs=[pl.BlockSpec(memory_space=pltpu.SMEM), pl.BlockSpec(memory_space=pltpu.VMEM)]
        + [pl.BlockSpec(memory_space=pl.ANY)] * len(flat),
        out_specs=[pl.BlockSpec(memory_space=pltpu.VMEM)] * 2,
        scratch_shapes=[
            pltpu.VMEM((nl, B, D), jnp.bfloat16),
            pltpu.VMEM((nr, B, D), jnp.bfloat16),
            pltpu.VMEM((B, B), f32),
            pltpu.VMEM((B, 128), f32),
            pltpu.VMEM((8, B), f32),
            pltpu.VMEM((8, 128), f32),
            pltpu.VMEM((B, 128), f32),
            pltpu.VMEM((B, 128), f32),
            pltpu.VMEM((B, 128), f32),
            pltpu.VMEM((nr, 8, B), f32),
            pltpu.VMEM((nr, 8, B), f32),
            pltpu.VMEM((nr, 8, B), f32),
            pltpu.SMEM((nr,), jnp.int32),
            pltpu.SemaphoreType.DMA((nl,)),
            pltpu.SemaphoreType.DMA((nr,)),
        ],
        compiler_params=pltpu.CompilerParams(vmem_limit_bytes=40 * 2**20),
        cost_estimate=pl.CostEstimate(
            flops=2 * B * B * D * max(1, nl * nr // 4), bytes_accessed=2 * B * D * (nl + nr), transcendentals=0
        ),
        name=name,
    )(live, prev, *flat)


def body(embeddings, partners, pair_count):
    unit = normalize(embeddings)
    me = lax.axis_index("dp")
    column = me % RING
    ring = me - column
    chip, core = column // 2, column % 2

    slots = partners[0]
    meta = jnp.where(jnp.arange(slots.shape[0]) < pair_count[0], slots, -1)[None, :]
    half = B // 2
    top, low = unit[:half], unit[half:]

    meta_a, meta_b = send(meta, around(1)), send(meta, around(-1))
    meta_c = send(meta, around(2))
    a_top = send(top, around(1))
    b_low = send(low, around(-1))
    sib = send(unit, along(0, 1))
    c_own = send(unit, along(-RING))
    a_low = send(low, around(1))
    b_top = send(top, around(-1))
    d_top = send(top, along(-2 * RING))
    over = []
    for d in range(COUNT):
        y = (d // RING) % 4
        over.append((d, d - y * RING + ((y + 1) % 4) * RING))
    relay = dict(over)
    d_mid = send(low, over)
    d_low = send(d_mid, [(relay[d], d - 2 * RING) for d in range(2 * RING, COUNT)])
    f_top = send(a_top, around(1))
    f_low = send(b_low, around(-1))
    c_sib = send(c_own, along(0, 1))
    d_own = jnp.concatenate([d_top, d_low], 0)
    d_sib = send(d_own, along(0, 1))

    other = 1 - core
    targets = [
        ring + chip * 2 + core,
        ring + chip * 2 + other,
        ring + RING + chip * 2 + core,
        ring + RING + chip * 2 + other,
        ring + 2 * RING + chip * 2 + core,
        ring + 2 * RING + chip * 2 + other,
    ]
    targets = jnp.stack(targets).astype(jnp.int32)
    lists = jnp.concatenate([meta, meta_a, meta_b, meta_c], 0)
    live = jnp.any(lists[:, None, :] == targets[None, :, None], -1).astype(jnp.int32)

    blocks = [[(unit, 0)], [(sib, 0)], [(c_own, 0)], [(c_sib, 0)], [(d_own, 0)], [(d_sib, 0)]]
    none = jnp.full((6, B), FLOOR, jnp.float32)
    row_0, col_0 = stage("own_ring", live[0, :2], none[:2], [blocks[0]], blocks[:2], own_first=True)
    left_a = [(a_top, 0), (a_low, half)]
    left_b = [(b_top, 0), (b_low, half)]
    left_c = [(f_top, 0), (f_low, half)]
    prev = jnp.concatenate([col_0, none[:4]], 0)
    live_1 = jnp.concatenate([live[:1].at[:, :2].set(0), live[1:3]], 0).reshape(-1)
    row_1, col_1 = stage("near", live_1, prev, [blocks[0], left_a, left_b], blocks)
    row_2, col_2 = stage("far", live[3], col_1, [left_c], blocks)

    got = [row_0[0], row_1[0], col_2[0]]
    got.append(send(row_1[1], around(-1)))
    got.append(send(row_1[2], around(1)))
    got.append(send(row_2[0], around(2)))
    got.append(send(col_2[1], along(0, 1)))
    for k in range(2):
        for flip in range(2):
            moves = along((k + 1) * RING, flip)
            back = send(col_2[2 + 2 * k + flip], moves)
            got.append(jnp.where(me >= (k + 1) * RING, back, FLOOR))
    got = jnp.stack(got)
    best = jnp.max(got, 0)
    return (best + jnp.log2(jnp.sum(jnp.exp2(got - best), 0))) * (LN2 / SCALE)


def solution(mesh):
    placed = (P("dp", None), P("dp", None), P("dp"))
    return jax.shard_map(body, mesh=mesh, in_specs=placed, out_specs=P("dp"), check_vma=False)
```

time: 1040 us -> 219 us (0.21)
  the two profiles are of different devices: /device:TPU:34 before, /device:TPU:8 now
where the time goes in v1:
time: 219 us; the launch traced here: 218 us
  waiting for transfers between devices  116 us (53%)
  starting transfers between devices  67.3 us (31%)
  Pallas kernels  24.4 us (11%)
  local copies, waits for them, and re-layouts  6.67 us (3%)
  other arithmetic  2.45 us (1%)
    ppermute x24, waiting for transfers between devices, send(): return lax.ppermute(value, 'dp', moves)  116 us
    ppermute x24, starting transfers between devices, send(): return lax.ppermute(value, 'dp', moves)  67.3 us
    pallas_call x3, Pallas kernels, stage(): pl.pallas_call(functools.partial(stage_kernel, plan), out_shape=[jax.Shap...  20.3 us
  transfers between devices with their start and end apart: 24, of which 10 were waited for; matrix products, arithmetic and copies ran while one was open for 2% of the time, Pallas kernels for 8%

profile of v1, /device:TPU:8, one launch (start us, length us, event | category | flops | bytes accessed | tf_op | source)
XLA Modules:
  0.0 217.7 jit_solution(5667866381916629533)
XLA Ops:
  0.0 4.1 %unit_rows.1.refs_0_.refs_1_.refs_5_.refs_2_ = bf16[1024,1024]{1,0:T(8,128)(2,1)} custom-call(bf16[1024,1024]{1,0:T(8,128)(2,1)} %x_ref.1), custom_call_target="tpu_custom_call" | custom-call | tf_op jit(solution)/shard_map/unit_rows/pallas_call | solution.py:49
  4.1 2.8 %fusion = (bf16[512,1024]{1,0:T(8,128)(2,1)S(1)}, bf16[512,1024]{1,0:T(8,128)(2,1)}) fusion(bf16[1024,1024]{1,0:T(8,128)(2,1)} %unit_rows.1.refs_0_.refs_1_.refs_5_.refs_2_), kind=kLoop, calls=%fused_computation.18 | loop fusion | bytes 4194304 | tf_op jit(solution)/shard_map/slice | solution.py:289
  7.0 1.6 collective-permute-start.11
  8.5 2.3 %collective-permute-start.8 = (bf16[1024,1024]{1,0:T(8,128)(2,1)S(1)}, bf16[1024,1024]{1,0:T(8,128)(2,1)}, u32[]{:S(2)}, u32[]{:S(2)}) collective-permute-start(bf16[1024,1024]{1,0:T(8,128)(2,1)S(1)} %copy-done), channel_id=1, source_target_pairs={{8,0},{9,1},{10,2},{11,3},{12,4},{13,5},{14,6},{15,7},{16,8},{17,9... | collective-permute-start | bytes 6291464 | tf_op jit(solution)/shard_map/ppermute | solution.py:38
  10.9 1.3 collective-permute-start.10
  12.2 19.7 %collective-permute-done.11 = bf16[512,1024]{1,0:T(8,128)(2,1)S(1)} collective-permute-done((bf16[512,1024]{1,0:T(8,128)(2,1)S(1)}, bf16[512,1024]{1,0:T(8,128)(2,1)S(1)}, u32[]{:S(2)}, u32[]{:S(2)}) %collective-permute-start.11) | collective-permute-done | bytes 1048608 | tf_op jit(solution)/shard_map/ppermute | solution.py:38
  31.9 1.3 collective-permute-start.12
  33.1 0.1 collective-permute-start.3
  33.2 1.6 collective-permute-start.4
  35.5 45.2 %collective-permute-done.10 = bf16[512,1024]{1,0:T(8,128)(2,1)S(1)} collective-permute-done((bf16[512,1024]{1,0:T(8,128)(2,1)}, bf16[512,1024]{1,0:T(8,128)(2,1)S(1)}, u32[]{:S(2)}, u32[]{:S(2)}) %collective-permute-start.10) | collective-permute-done | bytes 1048608 | tf_op jit(solution)/shard_map/ppermute | solution.py:38
  80.7 3.0 %collective-permute-start.2 = (s32[1,13]{1,0:T(1,128)S(1)}, s32[1,13]{1,0:T(1,128)S(1)}, u32[]{:S(2)}, u32[]{:S(2)}) collective-permute-start(s32[1,13]{1,0:T(1,128)S(1)} %compare_select_fusion), channel_id=1, source_target_pairs={{0,4},{1,5},{2,6},{3,7},{4,0},{5,1},{6,2},{7,3},{8,12},{9,13},{10,... | collective-permute-start | bytes 164 | tf_op jit(solution)/shard_map/ppermute | solution.py:38
  83.7 1.1 constant_dynamic-update-slice_fusion.1
  84.9 0.0 collective-permute-done.12
  84.9 1.1 collective-permute-start.1
  86.0 1.1 constant_dynamic-update-slice_fusion.refs_9_.refs_6_
  87.1 0.0 collective-permute-done.2
  87.1 0.9 collective-permute-start
  87.9 0.5 collective-permute-done.1
  88.4 0.6 collective-permute-start.5
  89.0 0.0 collective-permute-done.8.refs_7_.refs_4_
  89.0 0.0 collective-permute-start.9
  89.0 2.9 %collective-permute-done = s32[1,13]{1,0:T(1,128)S(1)} collective-permute-done((s32[1,13]{1,0:T(1,128)S(1)}, s32[1,13]{1,0:T(1,128)S(1)}, u32[]{:S(2)}, u32[]{:S(2)}) %collective-permute-start) | collective-permute-done | bytes 84 | tf_op jit(solution)/shard_map/ppermute | solution.py:38
  91.9 0.0 collective-permute-start.13
  91.9 0.0 collective-permute-done.4.refs_1_
  91.9 0.3 collective-permute-start.7
  92.2 19.9 %collective-permute-done.5.refs_2_ = bf16[512,1024]{1,0:T(8,128)(2,1)S(1)} collective-permute-done((bf16[512,1024]{1,0:T(8,128)(2,1)S(1)}, bf16[512,1024]{1,0:T(8,128)(2,1)S(1)}, u32[]{:S(2)}, u32[]{:S(2)}) %collective-permute-start.5) | collective-permute-done | bytes 1048608 | tf_op jit(solution)/shard_map/ppermute | solution.py:38
  112.0 1.0 copy-done.1
  113.0 1.1 collective-permute-start.6
  114.2 0.1 stack.54
  114.2 0.6 compare_reduce_fusion.1
  114.9 0.3 compare_reduce_fusion
  115.2 0.1 slice.70
  115.2 0.2 slice_reduce_fusion
  115.4 0.8 select_dynamic-update-slice_fusion
  116.2 1.8 collective-permute-done.7.refs_4_
  117.9 0.0 collective-permute-start.14
  118.0 0.0 collective-permute-done.3.refs_2_.refs_6_.refs_3_
  118.0 3.2 %collective-permute-start.15 = (bf16[512,1024]{1,0:T(8,128)(2,1)}, bf16[512,1024]{1,0:T(8,128)(2,1)}, u32[]{:S(2)}, u32[]{:S(2)}) collective-permute-start(bf16[512,1024]{1,0:T(8,128)(2,1)} %collective-permute-done.7.refs_4_), channel_id=1, source_target_pairs={{0,6},{1,7},{2,0},{3,1},{4,2},{5,3},{6,4},{7,5},{8,14},{9,15},{10,... | collective-permute-start | bytes 3145736 | tf_op jit(solution)/shard_map/ppermute | solution.py:38
  121.2 0.1 pad_add_fusion
  121.3 0.1 copy.5
  121.4 0.1 reshape.57.live
  121.5 5.6 %own_ring.1 = (f32[1,1024]{1,0:T(1,128)S(1)}, f32[2,1024]{1,0:T(2,128)S(1)}) custom-call(s32[2]{0:T(128)S(1)} %get-tuple-element.45.live, f32[2,1024]{1,0:T(2,128)S(1)} %slice.68.prev, bf16[1024,1024]{1,0:T(8,128)(2,1)S(1)} %copy-done, bf16[1024,1024]{1,0:T(8,128)(2,1)S(1)} %copy-done, bf16[1024,1024]{1,0:T(8,128)(2,1)} %collective-permute-done.3.refs_2_.refs_6_.refs_3_), custom_call_target="tpu_custom_call" | custom-call | flops 2147483648 | bytes 6291456 | tf_op jit(solution)/shard_map/own_ring/pallas_call | solution.py:248
  127.1 13.3 %collective-permute-done.6.refs_3_ = bf16[512,1024]{1,0:T(8,128)(2,1)} collective-permute-done((bf16[512,1024]{1,0:T(8,128)(2,1)}, bf16[512,1024]{1,0:T(8,128)(2,1)}, u32[]{:S(2)}, u32[]{:S(2)}) %collective-permute-start.6) | collective-permute-done | bytes 1048608 | tf_op jit(solution)/shard_map/ppermute | solution.py:38
  140.4 0.0 collective-permute-done.9.refs_8_.refs_5_
  140.4 0.0 collective-permute-done.13.refs_10_.refs_7_
  140.4 12.9 %near.1 = (f32[3,1024]{1,0:T(4,128)S(1)}, f32[6,1024]{1,0:T(8,128)S(1)}) custom-call(s32[18]{0:T(128)S(1)} %reshape.57.live, f32[6,1024]{1,0:T(8,128)S(1)} %concatenate.16.prev, bf16[1024,1024]{1,0:T(8,128)(2,1)S(1)} %copy-done, bf16[512,1024]{1,0:T(8,128)(2,1)} %collective-permute-done.4.refs_1_, bf16[512,1024]{1,0:T(8,128)(2,1)S(1)} %copy-done.2, ...), custom_call_target="tpu_custom_call" | custom-call | flops 8589934592 | bytes 18874368 | tf_op jit(solution)/shard_map/near/pallas_call | solution.py:248
  153.3 0.0 collective-permute-done.14.refs_0_
  153.3 9.2 %collective-permute-done.15.refs_1_ = bf16[512,1024]{1,0:T(8,128)(2,1)} collective-permute-done((bf16[512,1024]{1,0:T(8,128)(2,1)}, bf16[512,1024]{1,0:T(8,128)(2,1)}, u32[]{:S(2)}, u32[]{:S(2)}) %collective-permute-start.15) | collective-permute-done | bytes 1048608 | tf_op jit(solution)/shard_map/ppermute | solution.py:38
  162.5 1.8 far.1
  164.4 29.8 %collective-permute-start.23 = (f32[1024]{0:T(1024)S(1)}, f32[1024]{0:T(1024)S(1)}, u32[]{:S(2)}, u32[]{:S(2)}) collective-permute-start(f32[1024]{0:T(1024)S(1)} %bitcast.49), channel_id=1, source_target_pairs={{0,17},{1,16},{2,19},{3,18},{4,21},{5,20},{6,23},{7,22},{8,25},{9,... | collective-permute-start | bytes 12296 | tf_op jit(solution)/shard_map/ppermute | solution.py:38
  194.2 1.3 collective-permute-start.22
  195.5 2.3 %collective-permute-start.21 = (f32[1024]{0:T(1024)S(1)}, f32[1024]{0:T(1024)S(1)}, u32[]{:S(2)}, u32[]{:S(2)}) collective-permute-start(f32[1024]{0:T(1024)S(1)} %bitcast.47), channel_id=1, source_target_pairs={{0,9},{1,8},{2,11},{3,10},{4,13},{5,12},{6,15},{7,14},{8,17},{9,16... | collective-permute-start | bytes 12296 | tf_op jit(solution)/shard_map/ppermute | solution.py:38
  197.8 11.8 %collective-permute-start.20 = (f32[1024]{0:T(1024)S(1)}, f32[1024]{0:T(1024)S(1)}, u32[]{:S(2)}, u32[]{:S(2)}) collective-permute-start(f32[1024]{0:T(1024)S(1)} %bitcast.46), channel_id=1, source_target_pairs={{0,8},{1,9},{2,10},{3,11},{4,12},{5,13},{6,14},{7,15},{8,16},{9,17... | collective-permute-start | bytes 12296 | tf_op jit(solution)/shard_map/ppermute | solution.py:38
  209.6 0.2 collective-permute-start.19
  209.8 0.1 collective-permute-start.18
  209.9 3.4 %collective-permute-start.17 = (f32[1024]{0:T(1024)S(1)}, f32[1024]{0:T(1024)S(1)}, u32[]{:S(2)}, u32[]{:S(2)}) collective-permute-start(f32[1024]{0:T(1024)S(1)} %bitcast.51), channel_id=1, source_target_pairs={{0,2},{1,3},{2,4},{3,5},{4,6},{5,7},{6,0},{7,1},{8,10},{9,11},{10,... | collective-permute-start | bytes 12296 | tf_op jit(solution)/shard_map/ppermute | solution.py:38
  213.3 0.0 collective-permute-done.21
  213.3 0.0 collective-permute-start.16
  213.4 0.0 collective-permute-done.20
  213.4 1.6 collective-permute-done.18
  215.0 0.0 collective-permute-done.17
  215.0 1.9 collective-permute-done.16
  217.0 0.1 stack.63
  217.1 0.6 add_multiply_fusion
  (23 shorter events, 0.2 us)
Async XLA Ops:
  4.1 4.4 %copy-start = (bf16[1024,1024]{1,0:T(8,128)(2,1)S(1)}, bf16[1024,1024]{1,0:T(8,128)(2,1)}, u32[]{:S(2)}) copy-start(bf16[1024,1024]{1,0:T(8,128)(2,1)} %unit_rows.1.refs_0_.refs_1_.refs_5_.refs_2_) | copy-start | bytes 6291460
  4.1 31.3 %copy-start.3 = (s32[1,13]{1,0:T(1,128)S(1)}, s32[1,13]{1,0:T(1,128)}, u32[]{:S(2)}) copy-start(s32[1,13]{1,0:T(1,128)} %param.6) | copy-start | bytes 160
  7.0 24.9 %collective-permute-start.11 = (bf16[512,1024]{1,0:T(8,128)(2,1)S(1)}, bf16[512,1024]{1,0:T(8,128)(2,1)S(1)}, u32[]{:S(2)}, u32[]{:S(2)}) collective-permute-start(bf16[512,1024]{1,0:T(8,128)(2,1)S(1)} %get-tuple-element.31), channel_id=1, source_target_pairs={{0,8},{1,9},{2,10},{3,11},{4,12},{5,13},{6,14},{7,15},{8,16},{9,17... | collective-permute-start | bytes 3145736 | tf_op jit(solution)/shard_map/ppermute | solution.py:38
  8.5 80.5 %collective-permute-start.8 = (bf16[1024,1024]{1,0:T(8,128)(2,1)S(1)}, bf16[1024,1024]{1,0:T(8,128)(2,1)}, u32[]{:S(2)}, u32[]{:S(2)}) collective-permute-start(bf16[1024,1024]{1,0:T(8,128)(2,1)S(1)} %copy-done), channel_id=1, source_target_pairs={{8,0},{9,1},{10,2},{11,3},{12,4},{13,5},{14,6},{15,7},{16,8},{17,9... | collective-permute-start | bytes 6291464 | tf_op jit(solution)/shard_map/ppermute | solution.py:38
  10.9 69.8 %collective-permute-start.10 = (bf16[512,1024]{1,0:T(8,128)(2,1)}, bf16[512,1024]{1,0:T(8,128)(2,1)S(1)}, u32[]{:S(2)}, u32[]{:S(2)}) collective-permute-start(bf16[512,1024]{1,0:T(8,128)(2,1)} %get-tuple-element.32), channel_id=1, source_target_pairs={{16,0},{17,1},{18,2},{19,3},{20,4},{21,5},{22,6},{23,7},{24,8},{25... | collective-permute-start | bytes 3145736 | tf_op jit(solution)/shard_map/ppermute | solution.py:38
  31.9 53.0 %collective-permute-start.12 = (bf16[512,1024]{1,0:T(8,128)(2,1)S(1)}, bf16[512,1024]{1,0:T(8,128)(2,1)S(1)}, u32[]{:S(2)}, u32[]{:S(2)}) collective-permute-start(bf16[512,1024]{1,0:T(8,128)(2,1)S(1)} %collective-permute-done.11), channel_id=1, source_target_pairs={{24,0},{25,1},{26,2},{27,3},{28,4},{29,5},{30,6},{31,7},{0,8},{1,9... | collective-permute-start | bytes 3145736 | tf_op jit(solution)/shard_map/ppermute | solution.py:38
  33.1 84.8 %collective-permute-start.3 = (bf16[1024,1024]{1,0:T(8,128)(2,1)S(1)}, bf16[1024,1024]{1,0:T(8,128)(2,1)}, u32[]{:S(2)}, u32[]{:S(2)}) collective-permute-start(bf16[1024,1024]{1,0:T(8,128)(2,1)S(1)} %copy-done), channel_id=1, source_target_pairs={{0,1},{1,0},{2,3},{3,2},{4,5},{5,4},{6,7},{7,6},{8,9},{9,8},{10,11... | collective-permute-start | bytes 6291464 | tf_op jit(solution)/shard_map/ppermute | solution.py:38
  33.2 58.6 %collective-permute-start.4 = (bf16[512,1024]{1,0:T(8,128)(2,1)}, bf16[512,1024]{1,0:T(8,128)(2,1)}, u32[]{:S(2)}, u32[]{:S(2)}) collective-permute-start(bf16[512,1024]{1,0:T(8,128)(2,1)} %get-tuple-element.32), channel_id=1, source_target_pairs={{0,2},{1,3},{2,4},{3,5},{4,6},{5,7},{6,0},{7,1},{8,10},{9,11},{10,... | collective-permute-start | bytes 3145736 | tf_op jit(solution)/shard_map/ppermute | solution.py:38
  80.7 6.4 %collective-permute-start.2 = (s32[1,13]{1,0:T(1,128)S(1)}, s32[1,13]{1,0:T(1,128)S(1)}, u32[]{:S(2)}, u32[]{:S(2)}) collective-permute-start(s32[1,13]{1,0:T(1,128)S(1)} %compare_select_fusion), channel_id=1, source_target_pairs={{0,4},{1,5},{2,6},{3,7},{4,0},{5,1},{6,2},{7,3},{8,12},{9,13},{10,... | collective-permute-start | bytes 164 | tf_op jit(solution)/shard_map/ppermute | solution.py:38
  84.9 3.5 %collective-permute-start.1 = (s32[1,13]{1,0:T(1,128)S(1)}, s32[1,13]{1,0:T(1,128)S(1)}, u32[]{:S(2)}, u32[]{:S(2)}) collective-permute-start(s32[1,13]{1,0:T(1,128)S(1)} %compare_select_fusion), channel_id=1, source_target_pairs={{0,6},{1,7},{2,0},{3,1},{4,2},{5,3},{6,4},{7,5},{8,14},{9,15},{10,... | collective-permute-start | bytes 164 | tf_op jit(solution)/shard_map/ppermute | solution.py:38
  87.1 4.8 %collective-permute-start = (s32[1,13]{1,0:T(1,128)S(1)}, s32[1,13]{1,0:T(1,128)S(1)}, u32[]{:S(2)}, u32[]{:S(2)}) collective-permute-start(s32[1,13]{1,0:T(1,128)S(1)} %compare_select_fusion), channel_id=1, source_target_pairs={{0,2},{1,3},{2,4},{3,5},{4,6},{5,7},{6,0},{7,1},{8,10},{9,11},{10,... | collective-permute-start | bytes 164 | tf_op jit(solution)/shard_map/ppermute | solution.py:38
  88.4 23.6 %collective-permute-start.5 = (bf16[512,1024]{1,0:T(8,128)(2,1)S(1)}, bf16[512,1024]{1,0:T(8,128)(2,1)S(1)}, u32[]{:S(2)}, u32[]{:S(2)}) collective-permute-start(bf16[512,1024]{1,0:T(8,128)(2,1)S(1)} %get-tuple-element.31), channel_id=1, source_target_pairs={{0,2},{1,3},{2,4},{3,5},{4,6},{5,7},{6,0},{7,1},{8,10},{9,11},{10,... | collective-permute-start | bytes 3145736 | tf_op jit(solution)/shard_map/ppermute | solution.py:38
  89.0 51.4 %collective-permute-start.9 = (bf16[1024,1024]{1,0:T(8,128)(2,1)}, bf16[1024,1024]{1,0:T(8,128)(2,1)}, u32[]{:S(2)}, u32[]{:S(2)}) collective-permute-start(bf16[1024,1024]{1,0:T(8,128)(2,1)} %collective-permute-done.8.refs_7_.refs_4_), channel_id=1, source_target_pairs={{0,1},{1,0},{2,3},{3,2},{4,5},{5,4},{6,7},{7,6},{8,9},{9,8},{10,11... | collective-permute-start | bytes 6291464 | tf_op jit(solution)/shard_map/ppermute | solution.py:38
  91.9 48.5 %collective-permute-start.13 = (bf16[1024,1024]{1,0:T(8,128)(2,1)}, bf16[1024,1024]{1,0:T(8,128)(2,1)}, u32[]{:S(2)}, u32[]{:S(2)}) collective-permute-start(bf16[1024,1024]{1,0:T(8,128)(2,1)} %constant_dynamic-update-slice_fusion.refs_9_.refs_6_), channel_id=1, source_target_pairs={{0,1},{1,0},{2,3},{3,2},{4,5},{5,4},{6,7},{7,6},{8,9},{9,8},{10,11... | collective-permute-start | bytes 6291464 | tf_op jit(solution)/shard_map/ppermute | solution.py:38
  91.9 26.1 %collective-permute-start.7 = (bf16[512,1024]{1,0:T(8,128)(2,1)S(1)}, bf16[512,1024]{1,0:T(8,128)(2,1)}, u32[]{:S(2)}, u32[]{:S(2)}) collective-permute-start(bf16[512,1024]{1,0:T(8,128)(2,1)S(1)} %get-tuple-element.31), channel_id=1, source_target_pairs={{0,6},{1,7},{2,0},{3,1},{4,2},{5,3},{6,4},{7,5},{8,14},{9,15},{10,... | collective-permute-start | bytes 3145736 | tf_op jit(solution)/shard_map/ppermute | solution.py:38
  112.0 1.0 copy-start.1
  113.0 27.4 %collective-permute-start.6 = (bf16[512,1024]{1,0:T(8,128)(2,1)}, bf16[512,1024]{1,0:T(8,128)(2,1)}, u32[]{:S(2)}, u32[]{:S(2)}) collective-permute-start(bf16[512,1024]{1,0:T(8,128)(2,1)} %get-tuple-element.32), channel_id=1, source_target_pairs={{0,6},{1,7},{2,0},{3,1},{4,2},{5,3},{6,4},{7,5},{8,14},{9,15},{10,... | collective-permute-start | bytes 3145736 | tf_op jit(solution)/shard_map/ppermute | solution.py:38
  117.9 35.4 %collective-permute-start.14 = (bf16[512,1024]{1,0:T(8,128)(2,1)}, bf16[512,1024]{1,0:T(8,128)(2,1)S(1)}, u32[]{:S(2)}, u32[]{:S(2)}) collective-permute-start(bf16[512,1024]{1,0:T(8,128)(2,1)} %collective-permute-done.4.refs_1_), channel_id=1, source_target_pairs={{0,2},{1,3},{2,4},{3,5},{4,6},{5,7},{6,0},{7,1},{8,10},{9,11},{10,... | collective-permute-start | bytes 3145736 | tf_op jit(solution)/shard_map/ppermute | solution.py:38
  118.0 44.6 %collective-permute-start.15 = (bf16[512,1024]{1,0:T(8,128)(2,1)}, bf16[512,1024]{1,0:T(8,128)(2,1)}, u32[]{:S(2)}, u32[]{:S(2)}) collective-permute-start(bf16[512,1024]{1,0:T(8,128)(2,1)} %collective-permute-done.7.refs_4_), channel_id=1, source_target_pairs={{0,6},{1,7},{2,0},{3,1},{4,2},{5,3},{6,4},{7,5},{8,14},{9,15},{10,... | collective-permute-start | bytes 3145736 | tf_op jit(solution)/shard_map/ppermute | solution.py:38
  121.4 19.0 %copy-start.2 = (bf16[512,1024]{1,0:T(8,128)(2,1)S(1)}, bf16[512,1024]{1,0:T(8,128)(2,1)}, u32[]{:S(2)}) copy-start(bf16[512,1024]{1,0:T(8,128)(2,1)} %copy-done.1) | copy-start | bytes 3145732
  164.4 45.4 %collective-permute-start.23 = (f32[1024]{0:T(1024)S(1)}, f32[1024]{0:T(1024)S(1)}, u32[]{:S(2)}, u32[]{:S(2)}) collective-permute-start(f32[1024]{0:T(1024)S(1)} %bitcast.49), channel_id=1, source_target_pairs={{0,17},{1,16},{2,19},{3,18},{4,21},{5,20},{6,23},{7,22},{8,25},{9,... | collective-permute-start | bytes 12296 | tf_op jit(solution)/shard_map/ppermute | solution.py:38
  194.2 15.7 %collective-permute-start.22 = (f32[1024]{0:T(1024)S(1)}, f32[1024]{0:T(1024)S(1)}, u32[]{:S(2)}, u32[]{:S(2)}) collective-permute-start(f32[1024]{0:T(1024)S(1)} %bitcast.48), channel_id=1, source_target_pairs={{0,16},{1,17},{2,18},{3,19},{4,20},{5,21},{6,22},{7,23},{8,24},{9,... | collective-permute-start | bytes 12296 | tf_op jit(solution)/shard_map/ppermute | solution.py:38
  195.5 17.9 %collective-permute-start.21 = (f32[1024]{0:T(1024)S(1)}, f32[1024]{0:T(1024)S(1)}, u32[]{:S(2)}, u32[]{:S(2)}) collective-permute-start(f32[1024]{0:T(1024)S(1)} %bitcast.47), channel_id=1, source_target_pairs={{0,9},{1,8},{2,11},{3,10},{4,13},{5,12},{6,15},{7,14},{8,17},{9,16... | collective-permute-start | bytes 12296 | tf_op jit(solution)/shard_map/ppermute | solution.py:38
  197.8 15.6 %collective-permute-start.20 = (f32[1024]{0:T(1024)S(1)}, f32[1024]{0:T(1024)S(1)}, u32[]{:S(2)}, u32[]{:S(2)}) collective-permute-start(f32[1024]{0:T(1024)S(1)} %bitcast.46), channel_id=1, source_target_pairs={{0,8},{1,9},{2,10},{3,11},{4,12},{5,13},{6,14},{7,15},{8,16},{9,17... | collective-permute-start | bytes 12296 | tf_op jit(solution)/shard_map/ppermute | solution.py:38
  209.6 3.8 %collective-permute-start.19 = (f32[1024]{0:T(1024)S(1)}, f32[1024]{0:T(1024)S(1)}, u32[]{:S(2)}, u32[]{:S(2)}) collective-permute-start(f32[1024]{0:T(1024)S(1)} %bitcast.45), channel_id=1, source_target_pairs={{0,1},{1,0},{2,3},{3,2},{4,5},{5,4},{6,7},{7,6},{8,9},{9,8},{10,11... | collective-permute-start | bytes 12296 | tf_op jit(solution)/shard_map/ppermute | solution.py:38
  209.8 5.2 %collective-permute-start.18 = (f32[1024]{0:T(1024)S(1)}, f32[1024]{0:T(1024)S(1)}, u32[]{:S(2)}, u32[]{:S(2)}) collective-permute-start(f32[1024]{0:T(1024)S(1)} %bitcast.26), channel_id=1, source_target_pairs={{0,4},{1,5},{2,6},{3,7},{4,0},{5,1},{6,2},{7,3},{8,12},{9,13},{10,... | collective-permute-start | bytes 12296 | tf_op jit(solution)/shard_map/ppermute | solution.py:38
  209.9 5.1 %collective-permute-start.17 = (f32[1024]{0:T(1024)S(1)}, f32[1024]{0:T(1024)S(1)}, u32[]{:S(2)}, u32[]{:S(2)}) collective-permute-start(f32[1024]{0:T(1024)S(1)} %bitcast.51), channel_id=1, source_target_pairs={{0,2},{1,3},{2,4},{3,5},{4,6},{5,7},{6,0},{7,1},{8,10},{9,11},{10,... | collective-permute-start | bytes 12296 | tf_op jit(solution)/shard_map/ppermute | solution.py:38
  213.3 3.6 %collective-permute-start.16 = (f32[1024]{0:T(1024)S(1)}, f32[1024]{0:T(1024)S(1)}, u32[]{:S(2)}, u32[]{:S(2)}) collective-permute-start(f32[1024]{0:T(1024)S(1)} %bitcast.50), channel_id=1, source_target_pairs={{0,6},{1,7},{2,0},{3,1},{4,2},{5,3},{6,4},{7,5},{8,14},{9,15},{10,... | collective-permute-start | bytes 12296 | tf_op jit(solution)/shard_map/ppermute | solution.py:38

commit v2 on v1

--- a/solution.py
+++ b/solution.py
@@ -20,6 +20,7 @@
 G = 32
 COUNT = 128
 RING = 8
+HALVES = B // 2 // CH
 
 
 def around(dx):
@@ -38,20 +39,39 @@
     return lax.ppermute(value, "dp", moves)
 
 
-def unit_kernel(x_ref, o_ref):
-    for g in range(x_ref.shape[0] // G):
-        v = x_ref[g * G : (g + 1) * G, :].astype(jnp.float32)
+def unit_kernel(x_ref, o_ref, top_ref, low_ref):
+    i = pl.program_id(0)
+    for g in range(CH // G):
+        at = slice(g * G, (g + 1) * G)
+        v = x_ref[at, :].astype(jnp.float32)
         size = jnp.sum(v * v, -1, keepdims=True)
-        o_ref[g * G : (g + 1) * G, :] = (v * lax.rsqrt(size + 1e-06)).astype(jnp.bfloat16)
+        o_ref[at, :] = (v * lax.rsqrt(size + 1e-06)).astype(jnp.bfloat16)
+
+    @pl.when(i < HALVES)
+    def _():
+        top_ref[...] = o_ref[...]
+
+    @pl.when(i >= HALVES)
+    def _():
+        low_ref[...] = o_ref[...]
 
 
 def normalize(embeddings):
+    bf16 = jnp.bfloat16
     return pl.pallas_call(
         unit_kernel,
         grid=(B // CH,),
         in_specs=[pl.BlockSpec((CH, D), lambda i: (i, 0))],
-        out_specs=pl.BlockSpec((CH, D), lambda i: (i, 0)),
-        out_shape=jax.ShapeDtypeStruct((B, D), jnp.bfloat16),
+        out_specs=[
+            pl.BlockSpec((CH, D), lambda i: (i, 0)),
+            pl.BlockSpec((CH, D), lambda i: (jnp.minimum(i, HALVES - 1), 0)),
+            pl.BlockSpec((CH, D), lambda i: (jnp.maximum(i - HALVES, 0), 0)),
+        ],
+        out_shape=[
+            jax.ShapeDtypeStruct((B, D), bf16),
+            jax.ShapeDtypeStruct((B // 2, D), bf16),
+            jax.ShapeDtypeStruct((B // 2, D), bf16),
+        ],
         name="unit_rows",
     )(embeddings)
 
@@ -78,7 +98,7 @@
     return top + jnp.log2(jnp.exp2(a - top) + jnp.exp2(b - top))
 
 
-def stage_kernel(plan, live, prev, *refs):
+def stage_kernel(plan, live, row_prev, col_prev, *refs):
     nl, nr, lefts, rights, own_first = plan
     blocks, refs = refs[: len(lefts) + len(rights)], refs[len(lefts) + len(rights) :]
     row_out, col_out = refs[:2]
@@ -228,12 +248,22 @@
             return 0
 
         lax.fori_loop(first, nr, step, 0)
-        row_out[q : q + 1, :] = fold(row_m[...].T, row_s[...].T, row_f[...].T, 0)
+        row_out[q : q + 1, :] = row_prev[q : q + 1, :]
+
+        @pl.when(need_l[q])
+        def _(q=q):
+            found = fold(row_m[...].T, row_s[...].T, row_f[...].T, 0)
+            row_out[q : q + 1, :] = log2_add(found, row_prev[q : q + 1, :])
+
     for r in range(nr):
-        col_out[r : r + 1, :] = log2_add(fold(col_m[r], col_s[r], col_f[r], 0), prev[r : r + 1, :])
-
-
-def stage(name, live, prev, lefts, rights, own_first=False):
+        col_out[r : r + 1, :] = col_prev[r : r + 1, :]
+
+        @pl.when(need_r[r])
+        def _(r=r):
+            col_out[r : r + 1, :] = log2_add(fold(col_m[r], col_s[r], col_f[r], 0), col_prev[r : r + 1, :])
+
+
+def stage(name, live, row_prev, col_prev, lefts, rights, own_first=False):
     nl, nr = len(lefts), len(rights)
     flat, tables = [], []
     for side in (lefts, rights):
@@ -248,7 +278,8 @@
     return pl.pallas_call(
         functools.partial(stage_kernel, plan),
         out_shape=[jax.ShapeDtypeStruct((nl, B), f32), jax.ShapeDtypeStruct((nr, B), f32)],
-        in_specs=[pl.BlockSpec(memory_space=pltpu.SMEM), pl.BlockSpec(memory_space=pltpu.VMEM)]
+        in_specs=[pl.BlockSpec(memory_space=pltpu.SMEM)]
+        + [pl.BlockSpec(memory_space=pltpu.VMEM)] * 2
         + [pl.BlockSpec(memory_space=pl.ANY)] * len(flat),
         out_specs=[pl.BlockSpec(memory_space=pltpu.VMEM)] * 2,
         scratch_shapes=[
@@ -273,80 +304,90 @@
             flops=2 * B * B * D * max(1, nl * nr // 4), bytes_accessed=2 * B * D * (nl + nr), transcendentals=0
         ),
         name=name,
-    )(live, prev, *flat)
+    )(live, row_prev, col_prev, *flat)
+
+
+def last_kernel(own_ref, ring_ref, back_ref, o_ref):
+    got = jnp.concatenate([own_ref[...], ring_ref[...], back_ref[...]], 0)
+    best = jnp.max(got, 0, keepdims=True)
+    total = jnp.sum(jnp.exp2(got - best), 0, keepdims=True)
+    o_ref[...] = (best + jnp.log2(total)) * (LN2 / SCALE)
 
 
 def body(embeddings, partners, pair_count):
-    unit = normalize(embeddings)
+    unit, top, low = normalize(embeddings)
     me = lax.axis_index("dp")
     column = me % RING
     ring = me - column
     chip, core = column // 2, column % 2
+    half = B // 2
+    none = jnp.full((1, B), FLOOR, jnp.float32)
+
+    sib = send(unit, along(0, 1))
+    a = send(unit, around(1))
+    b = send(unit, around(-1))
+    c_own = send(unit, along(-RING))
+    over = [(d, d - d % 32 + (d + RING) % 32) for d in range(COUNT)]
+    relay = dict(over)
+    mid = send(low, over)
+    mine = [(unit, 0)]
+    self_row, _ = stage("own", jnp.ones((1,), jnp.int32), none, none, [mine], [mine], own_first=True)
+    mid, a, b, c_own, sib, _ = lax.optimization_barrier((mid, a, b, c_own, sib, self_row))
+    d_low = send(mid, [(relay[d], d - 2 * RING) for d in range(2 * RING, COUNT)])
+    blocks = [mine, [(sib, 0)], [(c_own, 0)]]
 
     slots = partners[0]
     meta = jnp.where(jnp.arange(slots.shape[0]) < pair_count[0], slots, -1)[None, :]
-    half = B // 2
-    top, low = unit[:half], unit[half:]
-
-    meta_a, meta_b = send(meta, around(1)), send(meta, around(-1))
-    meta_c = send(meta, around(2))
-    a_top = send(top, around(1))
-    b_low = send(low, around(-1))
-    sib = send(unit, along(0, 1))
-    c_own = send(unit, along(-RING))
-    a_low = send(low, around(1))
-    b_top = send(top, around(-1))
-    d_top = send(top, along(-2 * RING))
-    over = []
-    for d in range(COUNT):
-        y = (d // RING) % 4
-        over.append((d, d - y * RING + ((y + 1) % 4) * RING))
-    relay = dict(over)
-    d_mid = send(low, over)
-    d_low = send(d_mid, [(relay[d], d - 2 * RING) for d in range(2 * RING, COUNT)])
-    f_top = send(a_top, around(1))
-    f_low = send(b_low, around(-1))
+    meta, _ = lax.optimization_barrier((meta, self_row))
+    groups = [[r * RING + x * 2 + k for x in range(4)] for r in range(COUNT // RING) for k in range(2)]
+    lists = lax.all_gather(meta, "dp", axis_index_groups=groups, tiled=True)
+    lists = jnp.stack([lists[(chip + k) % 4] for k in (0, -1, 1, 2)])
+
+    f_top = send(a[:half], around(1))
+    f_low = send(b[half:], around(-1))
     c_sib = send(c_own, along(0, 1))
-    d_own = jnp.concatenate([d_top, d_low], 0)
-    d_sib = send(d_own, along(0, 1))
-
-    other = 1 - core
-    targets = [
-        ring + chip * 2 + core,
-        ring + chip * 2 + other,
-        ring + RING + chip * 2 + core,
-        ring + RING + chip * 2 + other,
-        ring + 2 * RING + chip * 2 + core,
-        ring + 2 * RING + chip * 2 + other,
-    ]
-    targets = jnp.stack(targets).astype(jnp.int32)
-    lists = jnp.concatenate([meta, meta_a, meta_b, meta_c], 0)
+    late, _ = lax.optimization_barrier((top, c_own))
+    d_top = send(late, along(-2 * RING))
+    d_low_sib = send(d_low, along(0, 1))
+
+    column_of = [chip * 2 + core, chip * 2 + 1 - core]
+    targets = jnp.stack([ring + k * RING + c for k in range(3) for c in column_of]).astype(jnp.int32)
     live = jnp.any(lists[:, None, :] == targets[None, :, None], -1).astype(jnp.int32)
-
-    blocks = [[(unit, 0)], [(sib, 0)], [(c_own, 0)], [(c_sib, 0)], [(d_own, 0)], [(d_sib, 0)]]
-    none = jnp.full((6, B), FLOOR, jnp.float32)
-    row_0, col_0 = stage("own_ring", live[0, :2], none[:2], [blocks[0]], blocks[:2], own_first=True)
-    left_a = [(a_top, 0), (a_low, half)]
-    left_b = [(b_top, 0), (b_low, half)]
-    left_c = [(f_top, 0), (f_low, half)]
-    prev = jnp.concatenate([col_0, none[:4]], 0)
-    live_1 = jnp.concatenate([live[:1].at[:, :2].set(0), live[1:3]], 0).reshape(-1)
-    row_1, col_1 = stage("near", live_1, prev, [blocks[0], left_a, left_b], blocks)
-    row_2, col_2 = stage("far", live[3], col_1, [left_c], blocks)
-
-    got = [row_0[0], row_1[0], col_2[0]]
-    got.append(send(row_1[1], around(-1)))
-    got.append(send(row_1[2], around(1)))
-    got.append(send(row_2[0], around(2)))
-    got.append(send(col_2[1], along(0, 1)))
+    live = live.at[0, 0].set(0)
+
+    blocks.append([(c_sib, 0)])
+    left = [mine, [(a, 0)], [(b, 0)]]
+    row_prev = jnp.concatenate([self_row, none, none], 0)
+    col_prev = jnp.concatenate([none] * 4, 0)
+    row, col = stage("near", live[:3, :4].reshape(-1), row_prev, col_prev, left, blocks)
+    d_top, f_top, f_low, row = lax.optimization_barrier((d_top, f_top, f_low, row))
+    d_top_sib = send(d_top, along(0, 1))
+    blocks.append([(d_top, 0), (d_low, half)])
+    blocks.append([(d_top_sib, 0), (d_low_sib, half)])
+    left.append([(f_top, 0), (f_low, half)])
+    row_prev = jnp.concatenate([row, none], 0)
+    col_prev = jnp.concatenate([col, none, none], 0)
+    live_far = live.at[:3, :4].set(0)
+    row, col = stage("far", live_far.reshape(-1), row_prev, col_prev, left, blocks)
+
+    back = []
     for k in range(2):
         for flip in range(2):
-            moves = along((k + 1) * RING, flip)
-            back = send(col_2[2 + 2 * k + flip], moves)
-            got.append(jnp.where(me >= (k + 1) * RING, back, FLOOR))
-    got = jnp.stack(got)
-    best = jnp.max(got, 0)
-    return (best + jnp.log2(jnp.sum(jnp.exp2(got - best), 0))) * (LN2 / SCALE)
+            moved = send(col[2 + 2 * k + flip], along((k + 1) * RING, flip))
+            back.append(jnp.where(me >= (k + 1) * RING, moved, FLOOR))
+    ring_part = jnp.full((RING, B), FLOOR, jnp.float32)
+    for q, dx in ((1, -1), (2, 1), (3, 2)):
+        ring_part = lax.dynamic_update_slice(ring_part, row[q : q + 1], (((chip + dx) % 4) * 2 + core, 0))
+    ring_part = lax.dynamic_update_slice(ring_part, col[1:2], (chip * 2 + 1 - core, 0))
+    groups = [[r * RING + k for k in range(RING)] for r in range(COUNT // RING)]
+    ring_got = lax.all_to_all(ring_part, "dp", 0, 0, axis_index_groups=groups, tiled=True)
+    own = jnp.concatenate([row[:1], col[:1]], 0)
+    out = pl.pallas_call(
+        last_kernel,
+        out_shape=jax.ShapeDtypeStruct((1, B), jnp.float32),
+        name="last_sum",
+    )(own, ring_got, jnp.stack(back))
+    return out.reshape(B)
 
 
 def solution(mesh):

time: 219 us -> 187 us (0.85)
  waiting for transfers between devices: 116 us -> 43.9 us
  blocking collectives: 0 us -> 28.2 us
  starting transfers between devices: 67.3 us -> 79.7 us
  local copies, waits for them, and re-layouts: 6.67 us -> 16.1 us
  Pallas kernels: 24.4 us -> 15 us
    ppermute x24 -> x16, waiting for transfers between devices: 116 us -> 39.8 us  [send(): return lax.ppermute(value, 'dp', moves)]
    all_gather x0 -> x1, blocking collectives: none -> 28.2 us  [body(): lists = lax.all_gather(meta, 'dp', axis_index_groups=groups, tiled=True)]
    pallas_call x3, Pallas kernels: 20.3 us -> 8.83 us  [stage(): pl.pallas_call(functools.partial(stage_kernel, plan), out_shape=[jax.Shap...]
    ppermute x24 -> x16, starting transfers between devices: 67.3 us -> 76.4 us  [send(): return lax.ppermute(value, 'dp', moves)]
    unnamed x9 -> x19, local copies, waits for them, and re-layouts: 2.12 us -> 10.2 us
    all_to_all x0 -> x1, waiting for transfers between devices: none -> 4.06 us  [body(): lax.all_to_all(ring_part, 'dp', 0, 0, axis_index_groups=groups, tiled=True)]
    all_to_all x0 -> x1, starting transfers between devices: none -> 3.33 us  [body(): lax.all_to_all(ring_part, 'dp', 0, 0, axis_index_groups=groups, tiled=True)]
    dynamic_update_slice x0 -> x4, local copies, waits for them, and re-layouts: none -> 2.36 us  [the longest x3 1.77 us: body(): lax.dynamic_update_slice(ring_part, row[q:q + 1], ((chip + dx) % 4 * 2 +...]
  transfers between devices with their start and end apart: 24 -> 17, of which waited for: 10 -> 5; matrix products, arithmetic and copies ran while one was open for 2% -> 4% of each run, Pallas kernels for 8% -> 4%
where the time goes in v2:
time: 187 us; the launch traced here: 185 us
  starting transfers between devices  79.7 us (43%)
  waiting for transfers between devices  43.9 us (23%)
  blocking collectives  28.2 us (15%)
  local copies, waits for them, and re-layouts  16.1 us (9%)
  Pallas kernels  15 us (8%)
    ppermute x16, starting transfers between devices, send(): return lax.ppermute(value, 'dp', moves)  76.4 us
    ppermute x16, waiting for transfers between devices, send(): return lax.ppermute(value, 'dp', moves)  39.8 us
    all_gather x1, blocking collectives, body(): lists = lax.all_gather(meta, 'dp', axis_index_groups=groups, tiled=True)  28.2 us
    unnamed x19, local copies, waits for them, and re-layouts  10.2 us
    pallas_call x3, Pallas kernels, stage(): pl.pallas_call(functools.partial(stage_kernel, plan), out_shape=[jax.Shap...  8.83 us
    pallas_call x1, Pallas kernels, normalize(): pl.pallas_call(unit_kernel, grid=(B // CH,), in_specs=[pl.BlockSpec((CH,...  4.78 us
    all_to_all x1, waiting for transfers between devices, body(): lax.all_to_all(ring_part, 'dp', 0, 0, axis_index_groups=groups, tiled=True)  4.06 us
  transfers between devices with their start and end apart: 17, of which 5 were waited for; matrix products, arithmetic and copies ran while one was open for 4% of the time, Pallas kernels for 4%

profile of v2, /device:TPU:8, one launch (start us, length us, event | category | flops | bytes accessed | tf_op | source)
XLA Modules:
  0.0 185.3 jit_solution(5563837475560758758)
XLA Ops:
  0.0 4.8 %unit_rows.1 = (bf16[1024,1024]{1,0:T(8,128)(2,1)}, bf16[512,1024]{1,0:T(8,128)(2,1)}, bf16[512,1024]{1,0:T(8,128)(2,1)}) custom-call(bf16[1024,1024]{1,0:T(8,128)(2,1)} %x_ref.1), custom_call_target="tpu_custom_call" | custom-call | tf_op jit(solution)/shard_map/unit_rows/pallas_call | solution.py:61
  4.8 1.5 collective-permute-start.1
  6.3 1.7 collective-permute-start.2
  8.0 2.3 %collective-permute-start.3 = (bf16[1024,1024]{1,0:T(8,128)(2,1)}, bf16[1024,1024]{1,0:T(8,128)(2,1)}, u32[]{:S(2)}, u32[]{:S(2)}) collective-permute-start(bf16[1024,1024]{1,0:T(8,128)(2,1)} %get-tuple-element.48.refs_0_.refs_1_.refs_3_.refs_5_), channel_id=1, source_target_pairs={{8,0},{9,1},{10,2},{11,3},{12,4},{13,5},{14,6},{15,7},{16,8},{17,9... | collective-permute-start | bytes 6291464 | tf_op jit(solution)/shard_map/ppermute | solution.py:39
  10.3 0.1 collective-permute-start.4
  10.4 1.7 collective-permute-start
  12.1 1.6 copy-done.3
  13.7 5.7 %own.1 = (f32[1,1024]{1,0:T(1,128)S(1)}, f32[1,1024]{1,0:T(1,128)}) custom-call(s32[1]{0:T(128)} %constant.122.clone.1.live, f32[1,1024]{1,0:T(1,128)S(1)} %broadcast_in_dim.19.row_prev.col_prev, f32[1,1024]{1,0:T(1,128)S(1)} %broadcast_in_dim.19.row_prev.col_prev, bf16[1024,1024]{1,0:T(8,128)(2,1)S(1)} %copy-done.3, bf16[1024,1024]{1,0:T(8,128)(2,1)S(1)} %copy-done.3), custom_call_target="tpu_custom_call" | custom-call | flops 2147483648 | bytes 4194304 | tf_op jit(solution)/shard_map/own/pallas_call | solution.py:278
  19.5 16.8 %collective-permute-done = bf16[512,1024]{1,0:T(8,128)(2,1)} collective-permute-done((bf16[512,1024]{1,0:T(8,128)(2,1)}, bf16[512,1024]{1,0:T(8,128)(2,1)}, u32[]{:S(2)}, u32[]{:S(2)}) %collective-permute-start) | collective-permute-done | bytes 1048608 | tf_op jit(solution)/shard_map/ppermute | solution.py:39
  36.3 17.3 %collective-permute-done.1.refs_1_ = bf16[1024,1024]{1,0:T(8,128)(2,1)S(1)} collective-permute-done((bf16[1024,1024]{1,0:T(8,128)(2,1)}, bf16[1024,1024]{1,0:T(8,128)(2,1)S(1)}, u32[]{:S(2)}, u32[]{:S(2)}) %collective-permute-start.1) | collective-permute-done | bytes 2097184 | tf_op jit(solution)/shard_map/ppermute | solution.py:39
  53.6 0.0 collective-permute-done.2.refs_2_
  53.6 3.4 %collective-permute-done.3.refs_5_.refs_7_ = bf16[1024,1024]{1,0:T(8,128)(2,1)} collective-permute-done((bf16[1024,1024]{1,0:T(8,128)(2,1)}, bf16[1024,1024]{1,0:T(8,128)(2,1)}, u32[]{:S(2)}, u32[]{:S(2)}) %collective-permute-start.3) | collective-permute-done | bytes 2097184 | tf_op jit(solution)/shard_map/ppermute | solution.py:39
  57.0 0.0 collective-permute-done.4.refs_4_.refs_6_
  57.0 0.0 collective-permute-start.8
  57.0 1.3 collective-permute-start.9
  59.0 0.0 copy-start.8
  59.0 1.3 collective-permute-start.5
  60.3 1.1 slice.77
  61.4 0.3 collective-permute-start.6
  61.7 1.1 slice.78
  62.7 3.0 %collective-permute-start.7 = (bf16[512,1024]{1,0:T(8,128)(2,1)}, bf16[512,1024]{1,0:T(8,128)(2,1)}, u32[]{:S(2)}, u32[]{:S(2)}) collective-permute-start(bf16[512,1024]{1,0:T(8,128)(2,1)} %slice.78), channel_id=1, source_target_pairs={{0,6},{1,7},{2,0},{3,1},{4,2},{5,3},{6,4},{7,5},{8,14},{9,15},{10,... | collective-permute-start | bytes 3145736 | tf_op jit(solution)/shard_map/ppermute | solution.py:39
  65.7 0.1 stack.46
  65.8 28.2 %all-gather = s32[4,1,13]{2,1,0:T(1,128)S(1)} all-gather(s32[1,1,13]{2,1,0:T(1,128)S(1)} %bitcast.46), channel_id=1, replica_groups={{0,2,4,6},{1,3,5,7},{8,10,12,14},{9,11,13,15},{16,18,20,22},{17,19,21,2..., dimensions={0}, use_global_device_ids=true | all-gather | bytes 260 | tf_op jit(solution)/shard_map/all_gather | solution.py:343
  94.0 0.3 compare_reduce_fusion
  94.3 0.1 scatter.6
  94.4 0.1 copy.5
  94.5 0.1 reshape.83.live
  94.5 0.0 collective-permute-done.9.refs_10_
  94.6 0.0 collective-permute-start.11
  94.6 0.0 collective-permute-done.8.refs_6_.refs_8_
  94.6 1.6 copy-done.1
  96.2 1.6 copy-done.4
  97.8 1.6 copy-done.7
  99.4 1.3 near.1
  100.7 0.0 collective-permute-done.5.refs_9_
  100.7 0.0 collective-permute-done.6.refs_3_
  100.7 0.0 collective-permute-done.7.refs_4_
  100.7 11.2 %collective-permute-start.10 = (bf16[512,1024]{1,0:T(8,128)(2,1)}, bf16[512,1024]{1,0:T(8,128)(2,1)}, u32[]{:S(2)}, u32[]{:S(2)}) collective-permute-start(bf16[512,1024]{1,0:T(8,128)(2,1)} %collective-permute-done.5.refs_9_), channel_id=1, source_target_pairs={{0,1},{1,0},{2,3},{3,2},{4,5},{5,4},{6,7},{7,6},{8,9},{9,8},{10,11... | collective-permute-start | bytes 3145736 | tf_op jit(solution)/shard_map/ppermute | solution.py:39
  112.0 0.2 scatter.9
  112.2 0.1 copy.4
  112.3 0.1 reshape.82.live
  112.4 0.0 collective-permute-done.11.refs_12_
  112.4 2.2 %collective-permute-done.10.refs_11_ = bf16[512,1024]{1,0:T(8,128)(2,1)} collective-permute-done((bf16[512,1024]{1,0:T(8,128)(2,1)}, bf16[512,1024]{1,0:T(8,128)(2,1)}, u32[]{:S(2)}, u32[]{:S(2)}) %collective-permute-start.10) | collective-permute-done | bytes 1048608 | tf_op jit(solution)/shard_map/ppermute | solution.py:39
  114.6 1.6 copy-done.2
  116.2 1.6 copy-done.5
  117.8 1.7 far.1
  119.6 12.8 %collective-permute-start.12 = (f32[1024]{0:T(1024)S(1)}, f32[1024]{0:T(1024)S(1)}, u32[]{:S(2)}, u32[]{:S(2)}) collective-permute-start(f32[1024]{0:T(1024)S(1)} %bitcast.45), channel_id=1, source_target_pairs={{0,8},{1,9},{2,10},{3,11},{4,12},{5,13},{6,14},{7,15},{8,16},{9,17... | collective-permute-start | bytes 12296 | tf_op jit(solution)/shard_map/ppermute | solution.py:39
  132.4 3.4 %collective-permute-start.13 = (f32[1024]{0:T(1024)S(1)}, f32[1024]{0:T(1024)S(1)}, u32[]{:S(2)}, u32[]{:S(2)}) collective-permute-start(f32[1024]{0:T(1024)S(1)} %bitcast.44), channel_id=1, source_target_pairs={{0,9},{1,8},{2,11},{3,10},{4,13},{5,12},{6,15},{7,14},{8,17},{9,16... | collective-permute-start | bytes 12296 | tf_op jit(solution)/shard_map/ppermute | solution.py:39
  135.8 34.2 %collective-permute-start.14 = (f32[1024]{0:T(1024)S(1)}, f32[1024]{0:T(1024)S(1)}, u32[]{:S(2)}, u32[]{:S(2)}) collective-permute-start(f32[1024]{0:T(1024)S(1)} %bitcast.43), channel_id=1, source_target_pairs={{0,16},{1,17},{2,18},{3,19},{4,20},{5,21},{6,22},{7,23},{8,24},{9,... | collective-permute-start | bytes 12296 | tf_op jit(solution)/shard_map/ppermute | solution.py:39
  170.0 1.6 collective-permute-start.15
  171.6 0.6 all_to_all.15
  172.3 0.6 bitcast_dynamic-update-slice_fusion.3
  172.9 0.6 bitcast_dynamic-update-slice_fusion.2
  173.4 0.6 bitcast_dynamic-update-slice_fusion.1
  174.0 0.6 bitcast_dynamic-update-slice_fusion
  174.6 3.3 %all-to-all-start = ((f32[8,1,1024]{2,1,0:T(1,128)}), f32[8,1,1024]{2,1,0:T(1,128)S(1)}, u32[]{:S(2)}, u32[]{:S(2)}) async-start(f32[8,1,1024]{2,1,0:T(1,128)} %bitcast_dynamic-update-slice_fusion), calls=%async_computation | async-start | bytes 65536 | tf_op jit(solution)/shard_map/all_to_all | solution.py:383
  178.0 0.6 pad_maximum_fusion.1.own_ref
  178.6 0.0 collective-permute-done.12
  178.6 0.0 collective-permute-done.14
  178.6 0.0 collective-permute-done.15
  178.6 0.6 pad_maximum_fusion.back_ref
  179.3 4.1 %all-to-all-done = f32[8,1,1024]{2,1,0:T(1,128)S(1)} async-done(((f32[8,1,1024]{2,1,0:T(1,128)}), f32[8,1,1024]{2,1,0:T(1,128)S(1)}, u32[]{:S(2)}, u32[]{:S(2)}) %all-to-all-start) | async-done | bytes 32800 | tf_op jit(solution)/shard_map/all_to_all | solution.py:383
  183.3 0.6 copy.8
  183.9 1.4 last_sum.1
  (29 shorter events, 0.1 us)
Async XLA Ops:
  4.8 48.8 %collective-permute-start.1 = (bf16[1024,1024]{1,0:T(8,128)(2,1)}, bf16[1024,1024]{1,0:T(8,128)(2,1)S(1)}, u32[]{:S(2)}, u32[]{:S(2)}) collective-permute-start(bf16[1024,1024]{1,0:T(8,128)(2,1)} %get-tuple-element.48.refs_0_.refs_1_.refs_3_.refs_5_), channel_id=1, source_target_pairs={{0,2},{1,3},{2,4},{3,5},{4,6},{5,7},{6,0},{7,1},{8,10},{9,11},{10,... | collective-permute-start | bytes 6291464 | tf_op jit(solution)/shard_map/ppermute | solution.py:39
  6.3 47.3 %collective-permute-start.2 = (bf16[1024,1024]{1,0:T(8,128)(2,1)}, bf16[1024,1024]{1,0:T(8,128)(2,1)S(1)}, u32[]{:S(2)}, u32[]{:S(2)}) collective-permute-start(bf16[1024,1024]{1,0:T(8,128)(2,1)} %get-tuple-element.48.refs_0_.refs_1_.refs_3_.refs_5_), channel_id=1, source_target_pairs={{0,6},{1,7},{2,0},{3,1},{4,2},{5,3},{6,4},{7,5},{8,14},{9,15},{10,... | collective-permute-start | bytes 6291464 | tf_op jit(solution)/shard_map/ppermute | solution.py:39
  8.0 49.0 %collective-permute-start.3 = (bf16[1024,1024]{1,0:T(8,128)(2,1)}, bf16[1024,1024]{1,0:T(8,128)(2,1)}, u32[]{:S(2)}, u32[]{:S(2)}) collective-permute-start(bf16[1024,1024]{1,0:T(8,128)(2,1)} %get-tuple-element.48.refs_0_.refs_1_.refs_3_.refs_5_), channel_id=1, source_target_pairs={{8,0},{9,1},{10,2},{11,3},{12,4},{13,5},{14,6},{15,7},{16,8},{17,9... | collective-permute-start | bytes 6291464 | tf_op jit(solution)/shard_map/ppermute | solution.py:39
  10.3 46.7 %collective-permute-start.4 = (bf16[1024,1024]{1,0:T(8,128)(2,1)}, bf16[1024,1024]{1,0:T(8,128)(2,1)S(1)}, u32[]{:S(2)}, u32[]{:S(2)}) collective-permute-start(bf16[1024,1024]{1,0:T(8,128)(2,1)} %get-tuple-element.48.refs_0_.refs_1_.refs_3_.refs_5_), channel_id=1, source_target_pairs={{0,1},{1,0},{2,3},{3,2},{4,5},{5,4},{6,7},{7,6},{8,9},{9,8},{10,11... | collective-permute-start | bytes 6291464 | tf_op jit(solution)/shard_map/ppermute | solution.py:39
  10.4 25.9 %collective-permute-start = (bf16[512,1024]{1,0:T(8,128)(2,1)}, bf16[512,1024]{1,0:T(8,128)(2,1)}, u32[]{:S(2)}, u32[]{:S(2)}) collective-permute-start(bf16[512,1024]{1,0:T(8,128)(2,1)} %get-tuple-element.52), channel_id=1, source_target_pairs={{0,8},{1,9},{2,10},{3,11},{4,12},{5,13},{6,14},{7,15},{8,16},{9,17... | collective-permute-start | bytes 3145736 | tf_op jit(solution)/shard_map/ppermute | solution.py:39
  12.1 1.6 copy-start.3
  53.6 9.1 %copy-start = (bf16[1024,1024]{1,0:T(8,128)(2,1)}, bf16[1024,1024]{1,0:T(8,128)(2,1)S(1)}, u32[]{:S(2)}) copy-start(bf16[1024,1024]{1,0:T(8,128)(2,1)S(1)} %collective-permute-done.2.refs_2_) | copy-start | bytes 6291460
  57.0 5.7 %copy-start.6 = (bf16[1024,1024]{1,0:T(8,128)(2,1)}, bf16[1024,1024]{1,0:T(8,128)(2,1)S(1)}, u32[]{:S(2)}) copy-start(bf16[1024,1024]{1,0:T(8,128)(2,1)S(1)} %collective-permute-done.4.refs_4_.refs_6_) | copy-start | bytes 6291460
  57.0 37.5 %collective-permute-start.8 = (bf16[1024,1024]{1,0:T(8,128)(2,1)}, bf16[1024,1024]{1,0:T(8,128)(2,1)}, u32[]{:S(2)}, u32[]{:S(2)}) collective-permute-start(bf16[1024,1024]{1,0:T(8,128)(2,1)} %collective-permute-done.3.refs_5_.refs_7_), channel_id=1, source_target_pairs={{0,1},{1,0},{2,3},{3,2},{4,5},{5,4},{6,7},{7,6},{8,9},{9,8},{10,11... | collective-permute-start | bytes 6291464 | tf_op jit(solution)/shard_map/ppermute | solution.py:39
  57.0 37.5 %collective-permute-start.9 = (bf16[512,1024]{1,0:T(8,128)(2,1)}, bf16[512,1024]{1,0:T(8,128)(2,1)S(1)}, u32[]{:S(2)}, u32[]{:S(2)}) collective-permute-start(bf16[512,1024]{1,0:T(8,128)(2,1)} %collective-permute-done), channel_id=1, source_target_pairs={{24,0},{25,1},{26,2},{27,3},{28,4},{29,5},{30,6},{31,7},{0,8},{1,9... | collective-permute-start | bytes 3145736 | tf_op jit(solution)/shard_map/ppermute | solution.py:39
  59.0 6.7 %copy-start.8 = (s32[1,13]{1,0:T(1,128)S(1)}, s32[1,13]{1,0:T(1,128)}, u32[]{:S(2)}) copy-start(s32[1,13]{1,0:T(1,128)} %param.8) | copy-start | bytes 160
  59.0 41.7 %collective-permute-start.5 = (bf16[512,1024]{1,0:T(8,128)(2,1)}, bf16[512,1024]{1,0:T(8,128)(2,1)}, u32[]{:S(2)}, u32[]{:S(2)}) collective-permute-start(bf16[512,1024]{1,0:T(8,128)(2,1)} %get-tuple-element.54), channel_id=1, source_target_pairs={{16,0},{17,1},{18,2},{19,3},{20,4},{21,5},{22,6},{23,7},{24,8},{25... | collective-permute-start | bytes 3145736 | tf_op jit(solution)/shard_map/ppermute | solution.py:39
  61.4 39.4 %collective-permute-start.6 = (bf16[512,1024]{1,0:T(8,128)(2,1)}, bf16[512,1024]{1,0:T(8,128)(2,1)}, u32[]{:S(2)}, u32[]{:S(2)}) collective-permute-start(bf16[512,1024]{1,0:T(8,128)(2,1)} %slice.77), channel_id=1, source_target_pairs={{0,2},{1,3},{2,4},{3,5},{4,6},{5,7},{6,0},{7,1},{8,10},{9,11},{10,... | collective-permute-start | bytes 3145736 | tf_op jit(solution)/shard_map/ppermute | solution.py:39
  62.7 38.0 %collective-permute-start.7 = (bf16[512,1024]{1,0:T(8,128)(2,1)}, bf16[512,1024]{1,0:T(8,128)(2,1)}, u32[]{:S(2)}, u32[]{:S(2)}) collective-permute-start(bf16[512,1024]{1,0:T(8,128)(2,1)} %slice.78), channel_id=1, source_target_pairs={{0,6},{1,7},{2,0},{3,1},{4,2},{5,3},{6,4},{7,5},{8,14},{9,15},{10,... | collective-permute-start | bytes 3145736 | tf_op jit(solution)/shard_map/ppermute | solution.py:39
  94.6 17.8 %collective-permute-start.11 = (bf16[512,1024]{1,0:T(8,128)(2,1)S(1)}, bf16[512,1024]{1,0:T(8,128)(2,1)}, u32[]{:S(2)}, u32[]{:S(2)}) collective-permute-start(bf16[512,1024]{1,0:T(8,128)(2,1)S(1)} %collective-permute-done.9.refs_10_), channel_id=1, source_target_pairs={{0,1},{1,0},{2,3},{3,2},{4,5},{5,4},{6,7},{7,6},{8,9},{9,8},{10,11... | collective-permute-start | bytes 3145736 | tf_op jit(solution)/shard_map/ppermute | solution.py:39
  94.6 1.6 copy-start.1
  96.2 1.6 copy-start.4
  97.8 1.6 copy-start.7
  100.7 13.8 %collective-permute-start.10 = (bf16[512,1024]{1,0:T(8,128)(2,1)}, bf16[512,1024]{1,0:T(8,128)(2,1)}, u32[]{:S(2)}, u32[]{:S(2)}) collective-permute-start(bf16[512,1024]{1,0:T(8,128)(2,1)} %collective-permute-done.5.refs_9_), channel_id=1, source_target_pairs={{0,1},{1,0},{2,3},{3,2},{4,5},{5,4},{6,7},{7,6},{8,9},{9,8},{10,11... | collective-permute-start | bytes 3145736 | tf_op jit(solution)/shard_map/ppermute | solution.py:39
  114.6 1.6 copy-start.2
  116.2 1.6 copy-start.5
  119.6 59.0 %collective-permute-start.12 = (f32[1024]{0:T(1024)S(1)}, f32[1024]{0:T(1024)S(1)}, u32[]{:S(2)}, u32[]{:S(2)}) collective-permute-start(f32[1024]{0:T(1024)S(1)} %bitcast.45), channel_id=1, source_target_pairs={{0,8},{1,9},{2,10},{3,11},{4,12},{5,13},{6,14},{7,15},{8,16},{9,17... | collective-permute-start | bytes 12296 | tf_op jit(solution)/shard_map/ppermute | solution.py:39
  132.4 46.2 %collective-permute-start.13 = (f32[1024]{0:T(1024)S(1)}, f32[1024]{0:T(1024)S(1)}, u32[]{:S(2)}, u32[]{:S(2)}) collective-permute-start(f32[1024]{0:T(1024)S(1)} %bitcast.44), channel_id=1, source_target_pairs={{0,9},{1,8},{2,11},{3,10},{4,13},{5,12},{6,15},{7,14},{8,17},{9,16... | collective-permute-start | bytes 12296 | tf_op jit(solution)/shard_map/ppermute | solution.py:39
  135.8 42.8 %collective-permute-start.14 = (f32[1024]{0:T(1024)S(1)}, f32[1024]{0:T(1024)S(1)}, u32[]{:S(2)}, u32[]{:S(2)}) collective-permute-start(f32[1024]{0:T(1024)S(1)} %bitcast.43), channel_id=1, source_target_pairs={{0,16},{1,17},{2,18},{3,19},{4,20},{5,21},{6,22},{7,23},{8,24},{9,... | collective-permute-start | bytes 12296 | tf_op jit(solution)/shard_map/ppermute | solution.py:39
  170.0 8.6 %collective-permute-start.15 = (f32[1024]{0:T(1024)S(1)}, f32[1024]{0:T(1024)S(1)}, u32[]{:S(2)}, u32[]{:S(2)}) collective-permute-start(f32[1024]{0:T(1024)S(1)} %bitcast.42), channel_id=1, source_target_pairs={{0,17},{1,16},{2,19},{3,18},{4,21},{5,20},{6,23},{7,22},{8,25},{9,... | collective-permute-start | bytes 12296 | tf_op jit(solution)/shard_map/ppermute | solution.py:39
  174.6 8.7 %all-to-all-start = ((f32[8,1,1024]{2,1,0:T(1,128)}), f32[8,1,1024]{2,1,0:T(1,128)S(1)}, u32[]{:S(2)}, u32[]{:S(2)}) async-start(f32[8,1,1024]{2,1,0:T(1,128)} %bitcast_dynamic-update-slice_fusion), calls=%async_computation | async-start | bytes 65536 | tf_op jit(solution)/shard_map/all_to_all | solution.py:383

commit v3 on v2

--- a/solution.py
+++ b/solution.py
@@ -14,6 +14,7 @@
 PLAIN = 78.0 / SCALE
 FLOOR = -1e30
 MASKED = -1e27
+SCRATCH = 17
 B = 1024
 D = 1024
 CH = 256
@@ -99,10 +100,11 @@
 
 
 def stage_kernel(plan, live, row_prev, col_prev, *refs):
-    nl, nr, lefts, rights, own_first = plan
+    nl, nr, lefts, rights, own_first, last = plan
     blocks, refs = refs[: len(lefts) + len(rights)], refs[len(lefts) + len(rights) :]
-    row_out, col_out = refs[:2]
-    (lbuf, rbuf, sc, row_t, col_t, chk, row_f, row_m, row_s, col_f, col_m, col_s, waited, lsem, rsem) = refs[2:]
+    outs, refs = refs[: -SCRATCH], refs[-SCRATCH:]
+    row_out, col_out = refs[-2:] if last else outs
+    (lbuf, rbuf, sc, row_t, col_t, chk, row_f, row_m, row_s, col_f, col_m, col_s, waited, lsem, rsem) = refs[:-2]
 
     def copies(side, slot):
         pieces = lefts if side == 0 else rights
@@ -262,8 +264,20 @@
         def _(r=r):
             col_out[r : r + 1, :] = log2_add(fold(col_m[r], col_s[r], col_f[r], 0), col_prev[r : r + 1, :])
 
-
-def stage(name, live, row_prev, col_prev, lefts, rights, own_first=False):
+    if last:
+        ring_out = outs[0]
+        ring_out[...] = jnp.full_like(ring_out, FLOOR)
+        chip, core = live[nl * nr], live[nl * nr + 1]
+        mine = chip * 2 + core
+        ring_out[pl.ds(mine, 1), :] = log2_add(row_out[0:1, :], col_out[0:1, :])
+        ring_out[pl.ds(mine + 1 - 2 * core, 1), :] = col_out[1:2, :]
+        for q, dx in ((1, 3), (2, 1), (3, 2)):
+            ring_out[pl.ds((chip + dx) % 4 * 2 + core, 1), :] = row_out[q : q + 1, :]
+        for r in range(2, nr):
+            outs[r - 1][...] = col_out[r : r + 1, :]
+
+
+def stage(name, live, row_prev, col_prev, lefts, rights, own_first=False, last=False):
     nl, nr = len(lefts), len(rights)
     flat, tables = [], []
     for side in (lefts, rights):
@@ -273,15 +287,17 @@
                 flat.append(array)
                 table.append((slot, row, array.shape[0]))
         tables.append(tuple(table))
-    plan = (nl, nr, tables[0], tables[1], own_first)
+    plan = (nl, nr, tables[0], tables[1], own_first, last)
     f32 = jnp.float32
+    shapes = [(RING, B)] + [(1, B)] * (nr - 2) if last else [(nl, B), (nr, B)]
+    shapes = [jax.ShapeDtypeStruct(shape, f32) for shape in shapes]
     return pl.pallas_call(
         functools.partial(stage_kernel, plan),
-        out_shape=[jax.ShapeDtypeStruct((nl, B), f32), jax.ShapeDtypeStruct((nr, B), f32)],
+        out_shape=shapes,
         in_specs=[pl.BlockSpec(memory_space=pltpu.SMEM)]
         + [pl.BlockSpec(memory_space=pltpu.VMEM)] * 2
         + [pl.BlockSpec(memory_space=pl.ANY)] * len(flat),
-        out_specs=[pl.BlockSpec(memory_space=pltpu.VMEM)] * 2,
+        out_specs=[pl.BlockSpec(memory_space=pltpu.VMEM)] * len(shapes),
         scratch_shapes=[
             pltpu.VMEM((nl, B, D), jnp.bfloat16),
             pltpu.VMEM((nr, B, D), jnp.bfloat16),
@@ -298,8 +314,10 @@
             pltpu.SMEM((nr,), jnp.int32),
             pltpu.SemaphoreType.DMA((nl,)),
             pltpu.SemaphoreType.DMA((nr,)),
+            pltpu.VMEM((nl, B), f32),
+            pltpu.VMEM((nr, B), f32),
         ],
-        compiler_params=pltpu.CompilerParams(vmem_limit_bytes=40 * 2**20),
+        compiler_params=pltpu.CompilerParams(vmem_limit_bytes=62 * 2**20),
         cost_estimate=pl.CostEstimate(
             flops=2 * B * B * D * max(1, nl * nr // 4), bytes_accessed=2 * B * D * (nl + nr), transcendentals=0
         ),
@@ -307,8 +325,13 @@
     )(live, row_prev, col_prev, *flat)
 
 
-def last_kernel(own_ref, ring_ref, back_ref, o_ref):
-    got = jnp.concatenate([own_ref[...], ring_ref[...], back_ref[...]], 0)
+def last_kernel(row_ref, ring_ref, *refs):
+    parts, o_ref = refs[:-1], refs[-1]
+    row = row_ref[0]
+    got = [ring_ref[...]]
+    for k, part in enumerate(parts):
+        got.append(jnp.where(row > k // 2, part[...], FLOOR))
+    got = jnp.concatenate(got, 0)
     best = jnp.max(got, 0, keepdims=True)
     total = jnp.sum(jnp.exp2(got - best), 0, keepdims=True)
     o_ref[...] = (best + jnp.log2(total)) * (LN2 / SCALE)
@@ -332,15 +355,16 @@
     mid = send(low, over)
     mine = [(unit, 0)]
     self_row, _ = stage("own", jnp.ones((1,), jnp.int32), none, none, [mine], [mine], own_first=True)
-    mid, a, b, c_own, sib, _ = lax.optimization_barrier((mid, a, b, c_own, sib, self_row))
-    d_low = send(mid, [(relay[d], d - 2 * RING) for d in range(2 * RING, COUNT)])
-    blocks = [mine, [(sib, 0)], [(c_own, 0)]]
-
     slots = partners[0]
     meta = jnp.where(jnp.arange(slots.shape[0]) < pair_count[0], slots, -1)[None, :]
     meta, _ = lax.optimization_barrier((meta, self_row))
     groups = [[r * RING + x * 2 + k for x in range(4)] for r in range(COUNT // RING) for k in range(2)]
-    lists = lax.all_gather(meta, "dp", axis_index_groups=groups, tiled=True)
+    meta = jnp.broadcast_to(meta, (4, meta.shape[1]))
+    lists = lax.all_to_all(meta, "dp", 0, 0, axis_index_groups=groups, tiled=True)
+    mid, lists = lax.optimization_barrier((mid, lists))
+    d_low = send(mid, [(relay[d], d - 2 * RING) for d in range(2 * RING, COUNT)])
+    a, b, c_own, d_low = lax.optimization_barrier((a, b, c_own, d_low))
+    blocks = [mine, [(sib, 0)], [(c_own, 0)]]
     lists = jnp.stack([lists[(chip + k) % 4] for k in (0, -1, 1, 2)])
 
     f_top = send(a[:half], around(1))
@@ -368,25 +392,19 @@
     row_prev = jnp.concatenate([row, none], 0)
     col_prev = jnp.concatenate([col, none, none], 0)
     live_far = live.at[:3, :4].set(0)
-    row, col = stage("far", live_far.reshape(-1), row_prev, col_prev, left, blocks)
-
-    back = []
-    for k in range(2):
-        for flip in range(2):
-            moved = send(col[2 + 2 * k + flip], along((k + 1) * RING, flip))
-            back.append(jnp.where(me >= (k + 1) * RING, moved, FLOOR))
-    ring_part = jnp.full((RING, B), FLOOR, jnp.float32)
-    for q, dx in ((1, -1), (2, 1), (3, 2)):
-        ring_part = lax.dynamic_update_slice(ring_part, row[q : q + 1], (((chip + dx) % 4) * 2 + core, 0))
-    ring_part = lax.dynamic_update_slice(ring_part, col[1:2], (chip * 2 + 1 - core, 0))
+    place = jnp.stack([chip, core]).astype(jnp.int32)
+    live_far = jnp.concatenate([live_far.reshape(-1), place])
+    ring_part, *cols = stage("far", live_far, row_prev, col_prev, left, blocks, last=True)
+
+    back = [send(col, along((k // 2 + 1) * RING, k % 2)) for k, col in enumerate(cols)]
     groups = [[r * RING + k for k in range(RING)] for r in range(COUNT // RING)]
     ring_got = lax.all_to_all(ring_part, "dp", 0, 0, axis_index_groups=groups, tiled=True)
-    own = jnp.concatenate([row[:1], col[:1]], 0)
     out = pl.pallas_call(
         last_kernel,
+        in_specs=[pl.BlockSpec(memory_space=pltpu.SMEM)] + [pl.BlockSpec(memory_space=pltpu.VMEM)] * 5,
         out_shape=jax.ShapeDtypeStruct((1, B), jnp.float32),
         name="last_sum",
-    )(own, ring_got, jnp.stack(back))
+    )((me // RING)[None].astype(jnp.int32), ring_got, *back)
     return out.reshape(B)
 
 

time: 187 us -> 173 us (0.925)
  the two profiles are of different devices: /device:TPU:8 before, /device:TPU:67 now
where the time goes in v3:
time: 173 us
  starting transfers between devices  50.7 us (29%)
  waiting for transfers between devices  45.7 us (26%)
  blocking collectives  36.5 us (21%)
  Pallas kernels  25.7 us (15%)
  local copies, waits for them, and re-layouts  12 us (7%)
    ppermute x16, waiting for transfers between devices, send(): return lax.ppermute(value, 'dp', moves)  45.7 us
    ppermute x16, starting transfers between devices, send(): return lax.ppermute(value, 'dp', moves)  37.4 us
    all_to_all x1, blocking collectives, body(): lax.all_to_all(meta, 'dp', 0, 0, axis_index_groups=groups, tiled=True)  36.5 us
    pallas_call x3, Pallas kernels, stage(): pl.pallas_call(functools.partial(stage_kernel, plan), out_shape=shapes, i...  19.5 us
    all_to_all x1, starting transfers between devices, body(): lax.all_to_all(ring_part, 'dp', 0, 0, axis_index_groups=groups, tiled=True)  13.3 us
    pallas_call x1, Pallas kernels, normalize(): pl.pallas_call(unit_kernel, grid=(B // CH,), in_specs=[pl.BlockSpec((CH,...  4.72 us
  transfers between devices with their start and end apart: 17, of which 5 were waited for; matrix products, arithmetic and copies ran while one was open for 6% of the time, Pallas kernels for 6%

profile of v3, /device:TPU:67, one launch (start us, length us, event | category | flops | bytes accessed | tf_op | source)
XLA Modules:
  0.0 172.5 jit_solution(5147499685415564213)
XLA Ops:
  0.0 4.7 %unit_rows.1 = (bf16[1024,1024]{1,0:T(8,128)(2,1)}, bf16[512,1024]{1,0:T(8,128)(2,1)}, bf16[512,1024]{1,0:T(8,128)(2,1)}) custom-call(bf16[1024,1024]{1,0:T(8,128)(2,1)} %x_ref.1), custom_call_target="tpu_custom_call" | custom-call | tf_op jit(solution)/shard_map/unit_rows/pallas_call | solution.py:62
  4.7 1.3 collective-permute-start
  6.0 2.9 %collective-permute-start.3 = (bf16[1024,1024]{1,0:T(8,128)(2,1)}, bf16[1024,1024]{1,0:T(8,128)(2,1)}, u32[]{:S(2)}, u32[]{:S(2)}) collective-permute-start(bf16[1024,1024]{1,0:T(8,128)(2,1)} %get-tuple-element.53.refs_0_.refs_1_.refs_3_.refs_5_), channel_id=1, source_target_pairs={{8,0},{9,1},{10,2},{11,3},{12,4},{13,5},{14,6},{15,7},{16,8},{17,9... | collective-permute-start | bytes 6291464 | tf_op jit(solution)/shard_map/ppermute | solution.py:40
  8.9 0.3 collective-permute-start.2
  9.2 1.2 collective-permute-start.1
  11.1 0.6 broadcast_in_dim.20.row_prev.col_prev
  11.7 8.3 %own.1 = (f32[1,1024]{1,0:T(1,128)}, f32[1,1024]{1,0:T(1,128)}) custom-call(s32[1]{0:T(128)} %constant.123.clone.1.live, f32[1,1024]{1,0:T(1,128)} %broadcast_in_dim.20.row_prev.col_prev, f32[1,1024]{1,0:T(1,128)} %broadcast_in_dim.20.row_prev.col_prev, bf16[1024,1024]{1,0:T(8,128)(2,1)} %get-tuple-element.53.refs_0_.refs_1_.refs_3_.refs_5_, ...), custom_call_target="tpu_custom_call" | custom-call | flops 2147483648 | bytes 4194304 | tf_op jit(solution)/shard_map/own/pallas_call | solution.py:294
  20.1 0.0 copy-done.5
  20.1 36.5 %all_to_all.20 = s32[4,1,13]{2,1,0:T(1,128)S(1)} all-to-all(s32[4,1,13]{2,1,0:T(1,128)S(1)} %broadcast_in_dim.21), channel_id=1, replica_groups={{0,2,4,6},{1,3,5,7},{8,10,12,14},{9,11,13,15},{16,18,20,22},{17,19,21,2..., dimensions={0} | all-to-all | bytes 416 | tf_op jit(solution)/shard_map/all_to_all | solution.py:363
  56.6 0.0 collective-permute-done
  56.6 2.3 %collective-permute-start.4 = (bf16[512,1024]{1,0:T(8,128)(2,1)}, bf16[512,1024]{1,0:T(8,128)(2,1)}, u32[]{:S(2)}, u32[]{:S(2)}) collective-permute-start(bf16[512,1024]{1,0:T(8,128)(2,1)} %collective-permute-done), channel_id=1, source_target_pairs={{24,0},{25,1},{26,2},{27,3},{28,4},{29,5},{30,6},{31,7},{0,8},{1,9... | collective-permute-start | bytes 3145736 | tf_op jit(solution)/shard_map/ppermute | solution.py:40
  58.9 2.5 %collective-permute-start.8 = (bf16[1024,1024]{1,0:T(8,128)(2,1)}, bf16[1024,1024]{1,0:T(8,128)(2,1)}, u32[]{:S(2)}, u32[]{:S(2)}) collective-permute-start(bf16[1024,1024]{1,0:T(8,128)(2,1)} %get-tuple-element.53.refs_0_.refs_1_.refs_3_.refs_5_), channel_id=1, source_target_pairs={{0,1},{1,0},{2,3},{3,2},{4,5},{5,4},{6,7},{7,6},{8,9},{9,8},{10,11... | collective-permute-start | bytes 6291464 | tf_op jit(solution)/shard_map/ppermute | solution.py:40
  61.4 21.1 %collective-permute-done.4.refs_10_ = bf16[512,1024]{1,0:T(8,128)(2,1)} collective-permute-done((bf16[512,1024]{1,0:T(8,128)(2,1)}, bf16[512,1024]{1,0:T(8,128)(2,1)}, u32[]{:S(2)}, u32[]{:S(2)}) %collective-permute-start.4) | collective-permute-done | bytes 1048608 | tf_op jit(solution)/shard_map/ppermute | solution.py:40
  82.5 0.0 collective-permute-done.3.refs_5_.refs_7_
  82.5 0.0 collective-permute-done.2.refs_2_
  82.5 0.0 collective-permute-done.1.refs_1_
  82.5 3.1 %collective-permute-start.9 = (bf16[1024,1024]{1,0:T(8,128)(2,1)}, bf16[1024,1024]{1,0:T(8,128)(2,1)}, u32[]{:S(2)}, u32[]{:S(2)}) collective-permute-start(bf16[1024,1024]{1,0:T(8,128)(2,1)} %collective-permute-done.3.refs_5_.refs_7_), channel_id=1, source_target_pairs={{0,1},{1,0},{2,3},{3,2},{4,5},{5,4},{6,7},{7,6},{8,9},{9,8},{10,11... | collective-permute-start | bytes 6291464 | tf_op jit(solution)/shard_map/ppermute | solution.py:40
  85.6 1.3 slice.47
  86.9 2.3 %slice.48 = bf16[512,1024]{1,0:T(8,128)(2,1)} slice(bf16[1024,1024]{1,0:T(8,128)(2,1)} %collective-permute-done.2.refs_2_), slice={[512:1024], [0:1024]} | slice | bytes 2097152 | tf_op jit(solution)/shard_map/slice | solution.py:371
  89.2 2.4 %collective-permute-start.7 = (bf16[512,1024]{1,0:T(8,128)(2,1)}, bf16[512,1024]{1,0:T(8,128)(2,1)}, u32[]{:S(2)}, u32[]{:S(2)}) collective-permute-start(bf16[512,1024]{1,0:T(8,128)(2,1)} %slice.48), channel_id=1, source_target_pairs={{0,6},{1,7},{2,0},{3,1},{4,2},{5,3},{6,4},{7,5},{8,14},{9,15},{10,... | collective-permute-start | bytes 3145736 | tf_op jit(solution)/shard_map/ppermute | solution.py:40
  91.6 0.0 collective-permute-start.6
  91.6 3.2 %collective-permute-start.5 = (bf16[512,1024]{1,0:T(8,128)(2,1)}, bf16[512,1024]{1,0:T(8,128)(2,1)}, u32[]{:S(2)}, u32[]{:S(2)}) collective-permute-start(bf16[512,1024]{1,0:T(8,128)(2,1)} %get-tuple-element.60), channel_id=1, source_target_pairs={{16,0},{17,1},{18,2},{19,3},{20,4},{21,5},{22,6},{23,7},{24,8},{25... | collective-permute-start | bytes 3145736 | tf_op jit(solution)/shard_map/ppermute | solution.py:40
  94.9 0.0 copy-done
  94.9 0.6 concatenate.20.row_prev
  95.5 0.1 stack.37
  95.6 0.3 compare_reduce_fusion
  95.9 0.1 scatter.6
  96.0 0.1 copy.6
  96.1 0.7 reshape.81.live
  96.7 0.0 collective-permute-done.8.refs_4_.refs_6_
  96.7 0.6 collective-permute-start.11
  97.3 0.0 collective-permute-done.9.refs_6_.refs_8_
  97.3 0.6 concatenate.21.col_prev
  97.9 2.1 %near.1 = (f32[3,1024]{1,0:T(4,128)}, f32[4,1024]{1,0:T(4,128)}) custom-call(s32[12]{0:T(128)} %reshape.81.live, f32[3,1024]{1,0:T(4,128)} %concatenate.20.row_prev, f32[4,1024]{1,0:T(4,128)} %concatenate.21.col_prev, bf16[1024,1024]{1,0:T(8,128)(2,1)} %get-tuple-element.53.refs_0_.refs_1_.refs_3_.refs_5_, ...), custom_call_target="tpu_custom_call" | custom-call | flops 6442450944 | bytes 14680064 | tf_op jit(solution)/shard_map/near/pallas_call | solution.py:294
  100.1 14.4 %collective-permute-done.7.refs_4_ = bf16[512,1024]{1,0:T(8,128)(2,1)} collective-permute-done((bf16[512,1024]{1,0:T(8,128)(2,1)}, bf16[512,1024]{1,0:T(8,128)(2,1)}, u32[]{:S(2)}, u32[]{:S(2)}) %collective-permute-start.7) | collective-permute-done | bytes 1048608 | tf_op jit(solution)/shard_map/ppermute | solution.py:40
  114.5 1.7 collective-permute-done.6.refs_3_
  116.1 3.6 %collective-permute-done.5.refs_9_ = bf16[512,1024]{1,0:T(8,128)(2,1)} collective-permute-done((bf16[512,1024]{1,0:T(8,128)(2,1)}, bf16[512,1024]{1,0:T(8,128)(2,1)}, u32[]{:S(2)}, u32[]{:S(2)}) %collective-permute-start.5) | collective-permute-done | bytes 1048608 | tf_op jit(solution)/shard_map/ppermute | solution.py:40
  119.7 1.1 collective-permute-start.10
  120.9 0.2 scatter.9
  121.1 0.1 copy.5
  121.2 0.1 reshape.80
  121.3 0.7 pad_add_fusion.1.live
  121.9 1.3 concatenate.22.row_prev
  123.2 1.3 concatenate.23.col_prev
  124.6 0.0 collective-permute-done.11.refs_12_
  124.6 0.0 collective-permute-done.10.refs_11_
  124.6 9.1 %far.1 = (f32[8,1024]{1,0:T(8,128)}, f32[1,1024]{1,0:T(1,128)}, f32[1,1024]{1,0:T(1,128)}, f32[1,1024]{1,0:T(1,128)}, f32[1,1024]{1,0:T(1,128)}) custom-call(s32[26]{0:T(128)} %pad_add_fusion.1.live, f32[4,1024]{1,0:T(4,128)} %concatenate.22.row_prev, f32[6,1024]{1,0:T(8,128)} %concatenate.23.col_prev, ...), custom_call_target="tpu_custom_call" | custom-call | flops 12884901888 | bytes 20971520 | tf_op jit(solution)/shard_map/far/pallas_call | solution.py:294
  133.7 1.4 copy.7
  135.1 13.3 %all-to-all-start.1 = ((f32[8,1,1024]{2,1,0:T(1,128)}), f32[8,1,1024]{2,1,0:T(1,128)S(1)}, u32[]{:S(2)}, u32[]{:S(2)}) async-start(f32[8,1,1024]{2,1,0:T(1,128)} %copy.7), calls=%async_computation.1 | async-start | bytes 65536 | tf_op jit(solution)/shard_map/all_to_all | solution.py:401
  148.4 1.9 %collective-permute-start.12 = (f32[1,1024]{1,0:T(1,128)}, f32[1,1024]{1,0:T(1,128)S(1)}, u32[]{:S(2)}, u32[]{:S(2)}) collective-permute-start(f32[1,1024]{1,0:T(1,128)} %get-tuple-element.71), channel_id=1, source_target_pairs={{0,8},{1,9},{2,10},{3,11},{4,12},{5,13},{6,14},{7,15},{8,16},{9,17... | collective-permute-start | bytes 12296 | tf_op jit(solution)/shard_map/ppermute | solution.py:40
  150.3 3.6 %collective-permute-start.13 = (f32[1,1024]{1,0:T(1,128)}, f32[1,1024]{1,0:T(1,128)S(1)}, u32[]{:S(2)}, u32[]{:S(2)}) collective-permute-start(f32[1,1024]{1,0:T(1,128)} %get-tuple-element.72), channel_id=1, source_target_pairs={{0,9},{1,8},{2,11},{3,10},{4,13},{5,12},{6,15},{7,14},{8,17},{9,16... | collective-permute-start | bytes 12296 | tf_op jit(solution)/shard_map/ppermute | solution.py:40
  153.9 9.0 %collective-permute-start.14 = (f32[1,1024]{1,0:T(1,128)}, f32[1,1024]{1,0:T(1,128)S(1)}, u32[]{:S(2)}, u32[]{:S(2)}) collective-permute-start(f32[1,1024]{1,0:T(1,128)} %get-tuple-element.73), channel_id=1, source_target_pairs={{0,16},{1,17},{2,18},{3,19},{4,20},{5,21},{6,22},{7,23},{8,24},{9,... | collective-permute-start | bytes 12296 | tf_op jit(solution)/shard_map/ppermute | solution.py:40
  163.0 1.9 %collective-permute-start.15 = (f32[1,1024]{1,0:T(1,128)}, f32[1,1024]{1,0:T(1,128)S(1)}, u32[]{:S(2)}, u32[]{:S(2)}) collective-permute-start(f32[1,1024]{1,0:T(1,128)} %get-tuple-element.74), channel_id=1, source_target_pairs={{0,17},{1,16},{2,19},{3,18},{4,21},{5,20},{6,23},{7,22},{8,25},{9,... | collective-permute-start | bytes 12296 | tf_op jit(solution)/shard_map/ppermute | solution.py:40
  164.9 0.0 all-to-all-done.1
  164.9 0.6 copy.10
  165.5 0.0 collective-permute-done.12.refs_0_
  165.5 0.0 collective-permute-done.13.refs_1_
  165.5 0.0 copy-start.2
  165.5 0.0 collective-permute-done.14.refs_2_
  165.6 0.0 copy-start.3
  165.6 4.9 %collective-permute-done.15.refs_3_ = f32[1,1024]{1,0:T(1,128)S(1)} collective-permute-done((f32[1,1024]{1,0:T(1,128)}, f32[1,1024]{1,0:T(1,128)S(1)}, u32[]{:S(2)}, u32[]{:S(2)}) %collective-permute-start.15) | collective-permute-done | bytes 4128 | tf_op jit(solution)/shard_map/ppermute | solution.py:40
  170.5 0.0 copy-done.3
  170.5 0.6 copy-done.4
  171.1 1.4 last_sum.1
  (13 shorter events, 0.1 us)
Async XLA Ops:
  4.7 51.8 %collective-permute-start = (bf16[512,1024]{1,0:T(8,128)(2,1)}, bf16[512,1024]{1,0:T(8,128)(2,1)}, u32[]{:S(2)}, u32[]{:S(2)}) collective-permute-start(bf16[512,1024]{1,0:T(8,128)(2,1)} %get-tuple-element.52), channel_id=1, source_target_pairs={{0,8},{1,9},{2,10},{3,11},{4,12},{5,13},{6,14},{7,15},{8,16},{9,17... | collective-permute-start | bytes 3145736 | tf_op jit(solution)/shard_map/ppermute | solution.py:40
  6.0 76.5 %collective-permute-start.3 = (bf16[1024,1024]{1,0:T(8,128)(2,1)}, bf16[1024,1024]{1,0:T(8,128)(2,1)}, u32[]{:S(2)}, u32[]{:S(2)}) collective-permute-start(bf16[1024,1024]{1,0:T(8,128)(2,1)} %get-tuple-element.53.refs_0_.refs_1_.refs_3_.refs_5_), channel_id=1, source_target_pairs={{8,0},{9,1},{10,2},{11,3},{12,4},{13,5},{14,6},{15,7},{16,8},{17,9... | collective-permute-start | bytes 6291464 | tf_op jit(solution)/shard_map/ppermute | solution.py:40
  8.9 73.6 %collective-permute-start.2 = (bf16[1024,1024]{1,0:T(8,128)(2,1)}, bf16[1024,1024]{1,0:T(8,128)(2,1)}, u32[]{:S(2)}, u32[]{:S(2)}) collective-permute-start(bf16[1024,1024]{1,0:T(8,128)(2,1)} %get-tuple-element.53.refs_0_.refs_1_.refs_3_.refs_5_), channel_id=1, source_target_pairs={{0,6},{1,7},{2,0},{3,1},{4,2},{5,3},{6,4},{7,5},{8,14},{9,15},{10,... | collective-permute-start | bytes 6291464 | tf_op jit(solution)/shard_map/ppermute | solution.py:40
  9.2 73.3 %collective-permute-start.1 = (bf16[1024,1024]{1,0:T(8,128)(2,1)}, bf16[1024,1024]{1,0:T(8,128)(2,1)}, u32[]{:S(2)}, u32[]{:S(2)}) collective-permute-start(bf16[1024,1024]{1,0:T(8,128)(2,1)} %get-tuple-element.53.refs_0_.refs_1_.refs_3_.refs_5_), channel_id=1, source_target_pairs={{0,2},{1,3},{2,4},{3,5},{4,6},{5,7},{6,0},{7,1},{8,10},{9,11},{10,... | collective-permute-start | bytes 6291464 | tf_op jit(solution)/shard_map/ppermute | solution.py:40
  11.7 8.4 %copy-start.5 = (s32[1,13]{1,0:T(1,128)S(1)}, s32[1,13]{1,0:T(1,128)}, u32[]{:S(2)}) copy-start(s32[1,13]{1,0:T(1,128)} %param.8) | copy-start | bytes 160
  56.6 26.0 %collective-permute-start.4 = (bf16[512,1024]{1,0:T(8,128)(2,1)}, bf16[512,1024]{1,0:T(8,128)(2,1)}, u32[]{:S(2)}, u32[]{:S(2)}) collective-permute-start(bf16[512,1024]{1,0:T(8,128)(2,1)} %collective-permute-done), channel_id=1, source_target_pairs={{24,0},{25,1},{26,2},{27,3},{28,4},{29,5},{30,6},{31,7},{0,8},{1,9... | collective-permute-start | bytes 3145736 | tf_op jit(solution)/shard_map/ppermute | solution.py:40
  58.9 37.9 %collective-permute-start.8 = (bf16[1024,1024]{1,0:T(8,128)(2,1)}, bf16[1024,1024]{1,0:T(8,128)(2,1)}, u32[]{:S(2)}, u32[]{:S(2)}) collective-permute-start(bf16[1024,1024]{1,0:T(8,128)(2,1)} %get-tuple-element.53.refs_0_.refs_1_.refs_3_.refs_5_), channel_id=1, source_target_pairs={{0,1},{1,0},{2,3},{3,2},{4,5},{5,4},{6,7},{7,6},{8,9},{9,8},{10,11... | collective-permute-start | bytes 6291464 | tf_op jit(solution)/shard_map/ppermute | solution.py:40
  82.5 14.8 %collective-permute-start.9 = (bf16[1024,1024]{1,0:T(8,128)(2,1)}, bf16[1024,1024]{1,0:T(8,128)(2,1)}, u32[]{:S(2)}, u32[]{:S(2)}) collective-permute-start(bf16[1024,1024]{1,0:T(8,128)(2,1)} %collective-permute-done.3.refs_5_.refs_7_), channel_id=1, source_target_pairs={{0,1},{1,0},{2,3},{3,2},{4,5},{5,4},{6,7},{7,6},{8,9},{9,8},{10,11... | collective-permute-start | bytes 6291464 | tf_op jit(solution)/shard_map/ppermute | solution.py:40
  85.6 9.3 %copy-start = (f32[1,1024]{1,0:T(1,128)S(1)}, f32[1,1024]{1,0:T(1,128)}, u32[]{:S(2)}) copy-start(f32[1,1024]{1,0:T(1,128)} %get-tuple-element.54) | copy-start | bytes 12292
  89.2 25.3 %collective-permute-start.7 = (bf16[512,1024]{1,0:T(8,128)(2,1)}, bf16[512,1024]{1,0:T(8,128)(2,1)}, u32[]{:S(2)}, u32[]{:S(2)}) collective-permute-start(bf16[512,1024]{1,0:T(8,128)(2,1)} %slice.48), channel_id=1, source_target_pairs={{0,6},{1,7},{2,0},{3,1},{4,2},{5,3},{6,4},{7,5},{8,14},{9,15},{10,... | collective-permute-start | bytes 3145736 | tf_op jit(solution)/shard_map/ppermute | solution.py:40
  91.6 24.6 %collective-permute-start.6 = (bf16[512,1024]{1,0:T(8,128)(2,1)S(1)}, bf16[512,1024]{1,0:T(8,128)(2,1)}, u32[]{:S(2)}, u32[]{:S(2)}) collective-permute-start(bf16[512,1024]{1,0:T(8,128)(2,1)S(1)} %slice.47), channel_id=1, source_target_pairs={{0,2},{1,3},{2,4},{3,5},{4,6},{5,7},{6,0},{7,1},{8,10},{9,11},{10,... | collective-permute-start | bytes 3145736 | tf_op jit(solution)/shard_map/ppermute | solution.py:40
  91.6 28.2 %collective-permute-start.5 = (bf16[512,1024]{1,0:T(8,128)(2,1)}, bf16[512,1024]{1,0:T(8,128)(2,1)}, u32[]{:S(2)}, u32[]{:S(2)}) collective-permute-start(bf16[512,1024]{1,0:T(8,128)(2,1)} %get-tuple-element.60), channel_id=1, source_target_pairs={{16,0},{17,1},{18,2},{19,3},{20,4},{21,5},{22,6},{23,7},{24,8},{25... | collective-permute-start | bytes 3145736 | tf_op jit(solution)/shard_map/ppermute | solution.py:40
  96.7 27.8 %collective-permute-start.11 = (bf16[512,1024]{1,0:T(8,128)(2,1)}, bf16[512,1024]{1,0:T(8,128)(2,1)}, u32[]{:S(2)}, u32[]{:S(2)}) collective-permute-start(bf16[512,1024]{1,0:T(8,128)(2,1)} %collective-permute-done.4.refs_10_), channel_id=1, source_target_pairs={{0,1},{1,0},{2,3},{3,2},{4,5},{5,4},{6,7},{7,6},{8,9},{9,8},{10,11... | collective-permute-start | bytes 3145736 | tf_op jit(solution)/shard_map/ppermute | solution.py:40
  119.7 4.9 %collective-permute-start.10 = (bf16[512,1024]{1,0:T(8,128)(2,1)}, bf16[512,1024]{1,0:T(8,128)(2,1)}, u32[]{:S(2)}, u32[]{:S(2)}) collective-permute-start(bf16[512,1024]{1,0:T(8,128)(2,1)} %collective-permute-done.5.refs_9_), channel_id=1, source_target_pairs={{0,1},{1,0},{2,3},{3,2},{4,5},{5,4},{6,7},{7,6},{8,9},{9,8},{10,11... | collective-permute-start | bytes 3145736 | tf_op jit(solution)/shard_map/ppermute | solution.py:40
  135.1 29.8 %all-to-all-start.1 = ((f32[8,1,1024]{2,1,0:T(1,128)}), f32[8,1,1024]{2,1,0:T(1,128)S(1)}, u32[]{:S(2)}, u32[]{:S(2)}) async-start(f32[8,1,1024]{2,1,0:T(1,128)} %copy.7), calls=%async_computation.1 | async-start | bytes 65536 | tf_op jit(solution)/shard_map/all_to_all | solution.py:401
  148.4 17.2 %collective-permute-start.12 = (f32[1,1024]{1,0:T(1,128)}, f32[1,1024]{1,0:T(1,128)S(1)}, u32[]{:S(2)}, u32[]{:S(2)}) collective-permute-start(f32[1,1024]{1,0:T(1,128)} %get-tuple-element.71), channel_id=1, source_target_pairs={{0,8},{1,9},{2,10},{3,11},{4,12},{5,13},{6,14},{7,15},{8,16},{9,17... | collective-permute-start | bytes 12296 | tf_op jit(solution)/shard_map/ppermute | solution.py:40
  150.3 15.2 %collective-permute-start.13 = (f32[1,1024]{1,0:T(1,128)}, f32[1,1024]{1,0:T(1,128)S(1)}, u32[]{:S(2)}, u32[]{:S(2)}) collective-permute-start(f32[1,1024]{1,0:T(1,128)} %get-tuple-element.72), channel_id=1, source_target_pairs={{0,9},{1,8},{2,11},{3,10},{4,13},{5,12},{6,15},{7,14},{8,17},{9,16... | collective-permute-start | bytes 12296 | tf_op jit(solution)/shard_map/ppermute | solution.py:40
  153.9 11.7 %collective-permute-start.14 = (f32[1,1024]{1,0:T(1,128)}, f32[1,1024]{1,0:T(1,128)S(1)}, u32[]{:S(2)}, u32[]{:S(2)}) collective-permute-start(f32[1,1024]{1,0:T(1,128)} %get-tuple-element.73), channel_id=1, source_target_pairs={{0,16},{1,17},{2,18},{3,19},{4,20},{5,21},{6,22},{7,23},{8,24},{9,... | collective-permute-start | bytes 12296 | tf_op jit(solution)/shard_map/ppermute | solution.py:40
  163.0 7.5 %collective-permute-start.15 = (f32[1,1024]{1,0:T(1,128)}, f32[1,1024]{1,0:T(1,128)S(1)}, u32[]{:S(2)}, u32[]{:S(2)}) collective-permute-start(f32[1,1024]{1,0:T(1,128)} %get-tuple-element.74), channel_id=1, source_target_pairs={{0,17},{1,16},{2,19},{3,18},{4,21},{5,20},{6,23},{7,22},{8,25},{9,... | collective-permute-start | bytes 12296 | tf_op jit(solution)/shard_map/ppermute | solution.py:40
  165.5 5.0 %copy-start.1 = (f32[1,1024]{1,0:T(1,128)}, f32[1,1024]{1,0:T(1,128)S(1)}, u32[]{:S(2)}) copy-start(f32[1,1024]{1,0:T(1,128)S(1)} %collective-permute-done.12.refs_0_) | copy-start | bytes 12292
  165.5 5.0 %copy-start.2 = (f32[1,1024]{1,0:T(1,128)}, f32[1,1024]{1,0:T(1,128)S(1)}, u32[]{:S(2)}) copy-start(f32[1,1024]{1,0:T(1,128)S(1)} %collective-permute-done.13.refs_1_) | copy-start | bytes 12292
  165.6 4.9 %copy-start.3 = (f32[1,1024]{1,0:T(1,128)}, f32[1,1024]{1,0:T(1,128)S(1)}, u32[]{:S(2)}) copy-start(f32[1,1024]{1,0:T(1,128)S(1)} %collective-permute-done.14.refs_2_) | copy-start | bytes 12292
  170.5 0.6 copy-start.4

commit v4 on v3

v4 whole, which is shorter than its diff:
```python
import functools

import jax
import jax.numpy as jnp
from jax import lax
from jax.experimental import pallas as pl
from jax.experimental.pallas import tpu as pltpu
from jax.sharding import PartitionSpec as P

SCALE = 256.0
LOG2E = 1.4426950408889634
LN2 = 0.6931471805599453
GAIN = SCALE * LOG2E
PLAIN = 78.0 / SCALE
FLOOR = -1e30
MASKED = -1e27
SCRATCH = 17
PLACES = [(0, 0), (0, 1), (3, 0), (1, 0), (3, 1), (1, 1), (2, 0), (2, 1)]
B = 1024
D = 1024
CH = 256
G = 32
COUNT = 128
RING = 8
HALVES = B // 2 // CH
LIST = 16
GRANT = 62 * 2**20


def around(dx):
    moves = []
    for d in range(COUNT):
        core, x, rest = d % 2, (d // 2) % 4, d // RING
        moves.append((d, rest * RING + ((x + dx) % 4) * 2 + core))
    return moves


def along(steps, flip=0):
    return [(d, (d + steps) ^ flip) for d in range(COUNT) if 0 <= d + steps < COUNT]


def send(value, moves):
    return lax.ppermute(value, "dp", moves)


def unit_kernel(list_ref, count_ref, x_ref, o_ref, top_ref, low_ref, x, o, in_sem, out_sem):
    def rows(i):
        return pl.ds(i * CH, CH)

    loads = [pltpu.make_async_copy(x_ref.at[rows(i), :], x.at[rows(i), :], in_sem.at[i]) for i in range(B // CH)]
    for load in loads:
        load.start()
    lane = lax.broadcasted_iota(jnp.int32, (LIST, D), 1)
    pairs = jnp.full((LIST, D), -1.0, jnp.float32)
    for k in range(list_ref.shape[1]):
        entry = jnp.where(k < count_ref[0], list_ref[0, k], -1).astype(jnp.float32)
        pairs = jnp.where(lane == k, entry, pairs)
    o[B : B + LIST, :] = pairs.astype(jnp.bfloat16)
    stores = [pltpu.make_async_copy(o.at[pl.ds(B, LIST), :], o_ref.at[pl.ds(B, LIST), :], out_sem.at[0])]
    stores[0].start()
    for i in range(B // CH):
        loads[i].wait()
        for g in range(CH // G):
            at = slice(i * CH + g * G, i * CH + (g + 1) * G)
            v = x[at, :].astype(jnp.float32)
            size = jnp.sum(v * v, -1, keepdims=True)
            o[at, :] = (v * lax.rsqrt(size + 1e-06)).astype(jnp.bfloat16)
        stores.append(pltpu.make_async_copy(o.at[rows(i), :], o_ref.at[rows(i), :], out_sem.at[2 * i + 1]))
        half = top_ref.at[rows(i), :] if i < HALVES else low_ref.at[rows(i - HALVES), :]
        stores.append(pltpu.make_async_copy(o.at[rows(i), :], half, out_sem.at[2 * i + 2]))
        stores[-2].start()
        stores[-1].start()
    for store in stores:
        store.wait()


def normalize(embeddings, partners, pair_count):
    bf16 = jnp.bfloat16
    smem, anywhere = pl.BlockSpec(memory_space=pltpu.SMEM), pl.BlockSpec(memory_space=pl.ANY)
    return pl.pallas_call(
        unit_kernel,
        in_specs=[smem, smem, anywhere],
        out_specs=[anywhere] * 3,
        out_shape=[
            jax.ShapeDtypeStruct((B + LIST, D), bf16),
            jax.ShapeDtypeStruct((B // 2, D), bf16),
            jax.ShapeDtypeStruct((B // 2, D), bf16),
        ],
        scratch_shapes=[
            pltpu.VMEM((B, D), bf16),
            pltpu.VMEM((B + LIST, D), bf16),
            pltpu.SemaphoreType.DMA((B // CH,)),
            pltpu.SemaphoreType.DMA((2 * (B // CH) + 1,)),
        ],
        compiler_params=pltpu.CompilerParams(vmem_limit_bytes=GRANT),
        name="unit_rows",
    )(partners, pair_count, embeddings)


def halves_kernel(a_ref, b_ref, top_ref, low_ref, sem):
    copies = [
        pltpu.make_async_copy(a_ref.at[pl.ds(0, B // 2), :], top_ref, sem.at[0]),
        pltpu.make_async_copy(b_ref.at[pl.ds(B // 2, B // 2 + LIST), :], low_ref, sem.at[1]),
    ]
    for copy in copies:
        copy.start()
    for copy in copies:
        copy.wait()


def halves(a, b):
    bf16, anywhere = jnp.bfloat16, pl.BlockSpec(memory_space=pl.ANY)
    return pl.pallas_call(
        halves_kernel,
        in_specs=[anywhere] * 2,
        out_specs=[anywhere] * 2,
        out_shape=[jax.ShapeDtypeStruct((B // 2, D), bf16), jax.ShapeDtypeStruct((B // 2 + LIST, D), bf16)],
        scratch_shapes=[pltpu.SemaphoreType.DMA((2,))],
        compiler_params=pltpu.CompilerParams(vmem_limit_bytes=GRANT),
        name="halves",
    )(a, b)


def lanes(value, op):
    return functools.reduce(op, [value[:, q * 128 : (q + 1) * 128] for q in range(value.shape[1] // 128)])


def rows8(value, op):
    return functools.reduce(op, [value[q * 8 : (q + 1) * 8, :] for q in range(value.shape[0] // 8)])


def fold(m, s, f, axis):
    top = jnp.max(m, axis, keepdims=True)
    plain = jnp.sum(f, axis, keepdims=True)
    top = jnp.maximum(top, jnp.where(plain > 0.0, 0.0, FLOOR))
    total = jnp.sum(s * jnp.exp2(m - top), axis, keepdims=True)
    total = total + plain * jnp.exp2(jnp.minimum(-top, 0.0))
    return jnp.maximum(top + jnp.log2(total), FLOOR)


def log2_add(a, b):
    top = jnp.maximum(a, b)
    return top + jnp.log2(jnp.exp2(a - top) + jnp.exp2(b - top))


def stage_kernel(plan, live, *refs):
    nl, nr, lefts, rights, widths, nrow, ncol, own_first, last = plan
    prevs, refs = refs[:2], refs[2:]
    blocks, refs = refs[: len(lefts) + len(rights)], refs[len(lefts) + len(rights) :]
    outs, refs = refs[:-SCRATCH], refs[-SCRATCH:]
    row_out, col_out = refs[-2:] if last else outs
    (lbuf, rbuf, sc, row_t, col_t, chk, row_f, row_m, row_s, col_f, col_m, col_s, waited, lsem, rsem) = refs[:-2]

    def copies(side, slot):
        pieces = lefts if side == 0 else rights
        base = 0 if side == 0 else len(lefts)
        buf, sem = (lbuf, lsem) if side == 0 else (rbuf, rsem)
        made = []
        for i, (s, row, count) in enumerate(pieces):
            if s == slot:
                made.append(
                    pltpu.make_async_copy(
                        blocks[base + i].at[pl.ds(0, count), :], buf.at[slot, pl.ds(row, count), :], sem.at[slot]
                    )
                )
        return made

    def used(flags):
        return functools.reduce(jnp.logical_or, [f > 0 for f in flags])

    need_l = [used([live[q * nr + r] for r in range(nr)]) for q in range(nl)]
    need_r = [used([live[q * nr + r] for q in range(nl)]) for r in range(nr)]
    for r in range(nr):
        waited[r] = 0

        @pl.when(need_r[r])
        def _(r=r):
            for c in copies(1, r):
                c.start()

    for q in range(nl):

        @pl.when(need_l[q])
        def _(q=q):
            for c in copies(0, q):
                c.start()

    col_f[...] = jnp.zeros_like(col_f)
    col_s[...] = jnp.zeros_like(col_s)
    col_m[...] = jnp.full_like(col_m, FLOOR)

    def pair(q, r, width, diag):
        def dot(i):
            sc[i * CH : (i + 1) * CH, :width] = lax.dot_general(
                lbuf[q, i * CH : (i + 1) * CH, :],
                rbuf[r, :width, :],
                (((1,), (1,)), ((), ())),
                preferred_element_type=jnp.float32,
            )

        def sums(i):
            cols = jnp.zeros((8, width), jnp.float32)
            size = jnp.zeros((8, 128), jnp.float32)
            for g in range(CH // G):
                at = i * CH + g * G
                v = sc[at : at + G, :width]
                if diag:
                    r_at = lax.broadcasted_iota(jnp.int32, (G, width), 0) + at
                    c_at = lax.broadcasted_iota(jnp.int32, (G, width), 1)
                    eye = r_at == c_at
                    absv = jnp.where(eye, 0.0, jnp.abs(v))
                    v = jnp.where(eye, MASKED, v)
                    sc[at : at + G, :width] = v
                else:
                    absv = jnp.abs(v)
                e = jnp.exp2(v * GAIN)
                row_t[at : at + G, :] = lanes(e, jnp.add)
                if not diag:
                    cols = cols + rows8(e, jnp.add)
                size = jnp.maximum(size, rows8(lanes(absv, jnp.maximum), jnp.maximum))
            if not diag:
                col_t[:, :width] = cols if i == 0 else col_t[:, :width] + cols
            chk[...] = size if i == 0 else jnp.maximum(chk[...], size)

        n = B // CH
        dot(0)
        for i in range(n):
            if i + 1 < n:
                dot(i + 1)
            sums(i)
        plain = jnp.max(chk[...]) <= PLAIN

        @pl.when(plain)
        def _():
            row_f[...] += row_t[...]
            if not diag:
                col_f[r, :, :width] += col_t[:, :width]

        @pl.when(jnp.logical_not(plain))
        def _():
            def group(g, _):
                at = pl.multiple_of(g * G, G)
                w = sc[pl.ds(at, G), :width] * GAIN
                old = row_m[pl.ds(at, G), :]
                top = jnp.maximum(old, lanes(w, jnp.maximum))
                total = row_s[pl.ds(at, G), :] * jnp.exp2(old - top)
                for k in range(width // 128):
                    total = total + jnp.exp2(w[:, k * 128 : (k + 1) * 128] - top)
                row_m[pl.ds(at, G), :] = top
                row_s[pl.ds(at, G), :] = total
                if not diag:
                    old = col_m[r, :, :width]
                    top = jnp.maximum(old, rows8(w, jnp.maximum))
                    total = col_s[r, :, :width] * jnp.exp2(old - top)
                    for k in range(G // 8):
                        total = total + jnp.exp2(w[k * 8 : (k + 1) * 8, :] - top)
                    col_m[r, :, :width] = top
                    col_s[r, :, :width] = total
                return 0

            lax.fori_loop(0, B // G, group, 0)

    def arrive(r):
        @pl.when(waited[r] == 0)
        def _():
            for s in range(nr):

                @pl.when(r == s)
                def _(s=s):
                    for c in copies(1, s):
                        c.wait()

            waited[r] = 1

    def runs():
        start = 0
        for r in range(1, nr + 1):
            if r == nr or widths[r] != widths[start]:
                yield start, r, widths[start]
                start = r

    def left(q, _):
        needed = functools.reduce(jnp.logical_or, [live[q * nr + r] > 0 for r in range(nr)])
        row_out[pl.ds(q, 1), :] = jnp.full((1, B), FLOOR, jnp.float32)

        @pl.when(needed)
        def _():
            row_f[...] = jnp.zeros_like(row_f)
            row_s[...] = jnp.zeros_like(row_s)
            row_m[...] = jnp.full_like(row_m, FLOOR)
            for s in range(nl):

                @pl.when(q == s)
                def _(s=s):
                    for c in copies(0, s):
                        c.wait()

            if own_first:

                @pl.when(q == 0)
                def _():
                    arrive(0)
                    pair(0, 0, B, True)

            for start, stop, width in runs():

                def step(r, _, width=width):
                    go = live[q * nr + r] > 0
                    if own_first:
                        go = jnp.logical_and(go, q + r > 0)

                    @pl.when(go)
                    def _():
                        arrive(r)
                        pair(q, r, width, False)

                    return 0

                lax.fori_loop(start, stop, step, 0)
            row_out[pl.ds(q, 1), :] = fold(row_m[...].T, row_s[...].T, row_f[...].T, 0)

        return 0

    lax.fori_loop(0, nl, left, 0)
    for q in range(nrow):
        row_out[q : q + 1, :] = log2_add(row_out[q : q + 1, :], prevs[0][q : q + 1, :])
    for r in range(nr):
        col_out[r : r + 1, :] = jnp.full((1, B), FLOOR, jnp.float32)

        @pl.when(need_r[r])
        def _(r=r):
            col_out[r : r + 1, :] = fold(col_m[r], col_s[r], col_f[r], 0)

        if r < ncol:
            col_out[r : r + 1, :] = log2_add(col_out[r : r + 1, :], prevs[1][r : r + 1, :])

    if last:
        ring_out, next_out, after_out = outs
        chip, core = live[nl * nr], live[nl * nr + 1]
        for q in range(nl):
            at = (chip + PLACES[q][0]) % 4 * 2 + (core + PLACES[q][1]) % 2
            row = row_out[q : q + 1, :]
            ring_out[at] = row if q else log2_add(row, col_out[0:1, :])
        next_out[...] = col_out[1:2, :]
        after_out[:, : B // 2] = col_out[3:4, : B // 2]
        after_out[:, B // 2 :] = col_out[2:3, : B // 2]


def stage(name, live, lefts, rights, row_prev=None, col_prev=None, own_first=False, last=False):
    nl, nr = len(lefts), len(rights)
    flat, tables = [], []
    for side in (lefts, rights):
        table = []
        for slot, pieces in enumerate(side):
            for array, row, count in pieces:
                flat.append(array)
                table.append((slot, row, count))
        tables.append(tuple(table))
    widths = tuple(sum(piece[2] for piece in pieces) for pieces in rights)
    prevs = [jnp.zeros((1, B), jnp.float32) if p is None else p for p in (row_prev, col_prev)]
    nrow, ncol = (0 if p is None else p.shape[0] for p in (row_prev, col_prev))
    plan = (nl, nr, tables[0], tables[1], widths, nrow, ncol, own_first, last)
    f32 = jnp.float32
    shapes = [(RING, 1, B), (1, B), (1, B)] if last else [(nl, B), (nr, B)]
    shapes = [jax.ShapeDtypeStruct(shape, f32) for shape in shapes]
    return pl.pallas_call(
        functools.partial(stage_kernel, plan),
        out_shape=shapes,
        in_specs=[pl.BlockSpec(memory_space=pltpu.SMEM)]
        + [pl.BlockSpec(memory_space=pltpu.VMEM)] * 2
        + [pl.BlockSpec(memory_space=pl.ANY)] * len(flat),
        out_specs=[pl.BlockSpec(memory_space=pltpu.VMEM)] * len(shapes),
        scratch_shapes=[
            pltpu.VMEM((nl, B, D), jnp.bfloat16),
            pltpu.VMEM((nr, B, D), jnp.bfloat16),
            pltpu.VMEM((B, B), f32),
            pltpu.VMEM((B, 128), f32),
            pltpu.VMEM((8, B), f32),
            pltpu.VMEM((8, 128), f32),
            pltpu.VMEM((B, 128), f32),
            pltpu.VMEM((B, 128), f32),
            pltpu.VMEM((B, 128), f32),
            pltpu.VMEM((nr, 8, B), f32),
            pltpu.VMEM((nr, 8, B), f32),
            pltpu.VMEM((nr, 8, B), f32),
            pltpu.SMEM((nr,), jnp.int32),
            pltpu.SemaphoreType.DMA((nl,)),
            pltpu.SemaphoreType.DMA((nr,)),
            pltpu.VMEM((nl, B), f32),
            pltpu.VMEM((nr, B), f32),
        ],
        compiler_params=pltpu.CompilerParams(vmem_limit_bytes=GRANT),
        cost_estimate=pl.CostEstimate(
            flops=2 * B * B * D * max(1, nl * nr // 4), bytes_accessed=2 * B * D * (nl + nr), transcendentals=0
        ),
        name=name,
    )(live, *prevs, *flat)


def last_kernel(row_ref, ring_ref, *refs):
    parts, o_ref = refs[:-1], refs[-1]
    row = row_ref[0]
    got = [ring_ref[k] for k in range(RING)]
    for k, part in enumerate(parts):
        got.append(jnp.where(row > k, part[...], FLOOR))
    got = jnp.concatenate(got, 0)
    best = jnp.max(got, 0, keepdims=True)
    total = jnp.sum(jnp.exp2(got - best), 0, keepdims=True)
    o_ref[...] = (best + jnp.log2(total)) * (LN2 / SCALE)


def body(embeddings, partners, pair_count):
    unit, top, low = normalize(embeddings, partners, pair_count)
    me = lax.axis_index("dp")
    column = me % RING
    half = B // 2
    swap = along(0, 1)

    sib = send(unit, swap)
    a = send(unit, around(1))
    b = send(unit, around(-1))
    c = send(unit, along(-RING))
    over = [(d, d - d % 32 + (d + RING) % 32) for d in range(COUNT)]
    relay = dict(over)
    mid = send(low, over)

    targets = me + RING * jnp.array([0, 1, 2, 2], jnp.int32)

    def pairs_of(*arrays):
        lists = jnp.concatenate([x[-LIST : 1 - LIST, :16] for x in arrays], 0).astype(jnp.int32)
        return jnp.any(lists[:, None, :] == targets[None, :, None], -1).astype(jnp.int32)

    def whole(array):
        return [(array, 0, B)]

    near_pairs = pairs_of(unit, sib)
    rights = [whole(unit)]
    row_0, col_0 = stage("own", near_pairs[:, 0], [whole(unit), whole(sib)], rights, own_first=True)

    mid, row_0 = lax.optimization_barrier((mid, row_0))
    d_low = send(mid, [(relay[d], d - 2 * RING) for d in range(2 * RING, COUNT)])
    a, b, c, d_low = lax.optimization_barrier((a, b, c, d_low))

    a_top, b_low = halves(a, b)
    f_top = send(a_top, around(1))
    f_low = send(b_low, around(-1))
    late, _ = lax.optimization_barrier((top, a_top))
    d_top = send(late, along(-2 * RING))
    a_sib = send(a, swap)
    b_sib = send(b, swap)

    rights = [whole(unit), whole(c), [(d_low, 0, half)]]
    live = jnp.concatenate([near_pairs.at[:, 0].set(0), pairs_of(a, b)], 0)[:, :3]
    lefts = [whole(unit), whole(sib), whole(a), whole(b)]
    row_1, col_1 = stage("near", live.reshape(-1), lefts, rights, row_0, col_0)
    a_sib, b_sib, row_1 = lax.optimization_barrier((a_sib, b_sib, row_1))
    more = pairs_of(a_sib, b_sib)
    row_2, col_2 = stage("mid", more[:, :3].reshape(-1), [whole(a_sib), whole(b_sib)], rights, None, col_1)
    f_top, f_low, d_top, row_2 = lax.optimization_barrier((f_top, f_low, d_top, row_2))
    f_top_sib = send(f_top, swap)
    f_low_sib = send(f_low, swap)

    rights.append([(d_top, 0, half)])
    lefts += [whole(a_sib), whole(b_sib)]
    lefts += [[(f_top, 0, half), (f_low, half, half)], [(f_top_sib, 0, half), (f_low_sib, half, half)]]
    early = jnp.concatenate([near_pairs, pairs_of(a, b), more], 0).at[:, :3].set(0)
    live = jnp.concatenate([early, pairs_of(f_low, f_low_sib)], 0)
    place = jnp.stack([column // 2, column % 2]).astype(jnp.int32)
    live = jnp.concatenate([live.reshape(-1), place])
    row_prev = jnp.concatenate([row_1, row_2], 0)
    ring_part, next_part, after_part = stage("far", live, lefts, rights, row_prev, col_2, last=True)

    next_got = send(next_part, along(RING))
    after_got = send(after_part, along(2 * RING))
    groups = [[r * RING + k for k in range(RING)] for r in range(COUNT // RING)]
    ring_got = lax.all_to_all(ring_part, "dp", 0, 0, axis_index_groups=groups, tiled=True)
    out = pl.pallas_call(
        last_kernel,
        in_specs=[pl.BlockSpec(memory_space=pltpu.SMEM)] + [pl.BlockSpec(memory_space=pltpu.VMEM)] * 3,
        out_shape=jax.ShapeDtypeStruct((1, B), jnp.float32),
        name="last_sum",
    )((me // RING)[None].astype(jnp.int32), ring_got, next_got, after_got)
    return out.reshape(B)


def solution(mesh):
    placed = (P("dp", None), P("dp", None), P("dp"))
    return jax.shard_map(body, mesh=mesh, in_specs=placed, out_specs=P("dp"), check_vma=False)
```

time: 173 us -> 222 us (1.28)
  the two profiles are of different devices: /device:TPU:67 before, /device:TPU:34 now
where the time goes in v4:
time: 222 us; the launch traced here: 218 us
  Pallas kernels  117 us (53%)
  waiting for transfers between devices  50.2 us (23%)
  starting transfers between devices  35.3 us (16%)
  local copies, waits for them, and re-layouts  9.9 us (4%)
  other arithmetic  5.4 us (2%)
    pallas_call x1, Pallas kernels, halves(): pl.pallas_call(halves_kernel, in_specs=[anywhere] * 2, out_specs=[anywher...  65.6 us
    ppermute x15, waiting for transfers between devices, send(): return lax.ppermute(value, 'dp', moves)  50.2 us
    pallas_call x4, Pallas kernels, stage(): pl.pallas_call(functools.partial(stage_kernel, plan), out_shape=shapes, i...  45.6 us
    ppermute x15, starting transfers between devices, send(): return lax.ppermute(value, 'dp', moves)  27.9 us
    all_to_all x1, starting transfers between devices, body(): lax.all_to_all(ring_part, 'dp', 0, 0, axis_index_groups=groups, tiled=True)  7.34 us
  transfers between devices with their start and end apart: 16, of which 5 were waited for; matrix products, arithmetic and copies ran while one was open for 5% of the time, Pallas kernels for 47%

profile of v4, /device:TPU:34, one launch (start us, length us, event | category | flops | bytes accessed | tf_op | source)
XLA Modules:
  0.0 218.4 jit_solution(12532176747288682829)
XLA Ops:
  0.7 4.0 %unit_rows.1 = (bf16[1040,1024]{1,0:T(8,128)(2,1)}, bf16[512,1024]{1,0:T(8,128)(2,1)}, bf16[512,1024]{1,0:T(8,128)(2,1)}) custom-call(s32[1,13]{1,0:T(1,128)} %list_ref.1, s32[1]{0:T(128)S(6)} %copy.7.count_ref, bf16[1024,1024]{1,0:T(8,128)(2,1)} %x_ref.1), custom_call_target="tpu_custom_call" | custom-call | tf_op jit(solution)/shard_map/unit_rows/pallas_call | solution.py:80
  4.7 0.1 collective-permute-start
  4.8 4.5 %collective-permute-start.3 = (bf16[1040,1024]{1,0:T(8,128)(2,1)}, bf16[1040,1024]{1,0:T(8,128)(2,1)}, u32[]{:S(2)}, u32[]{:S(2)}) collective-permute-start(bf16[1040,1024]{1,0:T(8,128)(2,1)} %get-tuple-element.57.refs_2_.refs_4_.refs_6_.refs_12_), channel_id=1, source_target_pairs={{8,0},{9,1},{10,2},{11,3},{12,4},{13,5},{14,6},{15,7},{16,8},{17,9... | collective-permute-start | bytes 6389768 | tf_op jit(solution)/shard_map/ppermute | solution.py:43
  9.3 0.6 collective-permute-start.2
  9.9 1.5 collective-permute-start.1
  11.3 0.0 collective-permute-start.4
  11.4 0.7 slice.67
  12.1 0.6 compare_reduce_fusion.4
  12.7 0.7 broadcast_add_fusion
  13.4 0.0 collective-permute-done.refs_3_
  13.4 0.2 compare_reduce_fusion.3
  13.6 1.2 copy-done.5
  14.8 1.3 broadcast_select_fusion
  16.0 0.6 broadcast_6_refs_0__refs_1_.2.refs_0_.refs_1_
  16.6 8.3 %own.1 = (f32[2,1024]{1,0:T(2,128)}, f32[1,1024]{1,0:T(1,128)}) custom-call(s32[2]{0:T(128)} %get-tuple-element.86.live, f32[1,1024]{1,0:T(1,128)} %broadcast_6_refs_0__refs_1_.2.refs_0_.refs_1_, f32[1,1024]{1,0:T(1,128)} %broadcast_6_refs_0__refs_1_.2.refs_0_.refs_1_, bf16[1040,1024]{1,0:T(8,128)(2,1)} %get-tuple-element.57.refs_2_.refs_4_.refs_6_.refs_12_, ...), custom_call_target="tpu_custom_call" | custom-call | flops 2147483648 | bytes 6291456 | tf_op jit(solution)/shard_map/own/pallas_call | solution.py:366
  24.9 12.6 %collective-permute-done.4 = bf16[512,1024]{1,0:T(8,128)(2,1)S(1)} collective-permute-done((bf16[512,1024]{1,0:T(8,128)(2,1)}, bf16[512,1024]{1,0:T(8,128)(2,1)S(1)}, u32[]{:S(2)}, u32[]{:S(2)}) %collective-permute-start.4) | collective-permute-done | bytes 1048608 | tf_op jit(solution)/shard_map/ppermute | solution.py:43
  37.5 1.0 copy-done.8
  38.5 1.9 collective-permute-start.5
  40.4 26.0 %collective-permute-done.3.refs_7_.refs_5_.refs_13_ = bf16[1040,1024]{1,0:T(8,128)(2,1)} collective-permute-done((bf16[1040,1024]{1,0:T(8,128)(2,1)}, bf16[1040,1024]{1,0:T(8,128)(2,1)}, u32[]{:S(2)}, u32[]{:S(2)}) %collective-permute-start.3) | collective-permute-done | bytes 2129952 | tf_op jit(solution)/shard_map/ppermute | solution.py:43
  66.4 0.0 collective-permute-done.2.refs_5_.b_ref
  66.4 0.0 collective-permute-done.1.refs_4_.a_ref
  66.4 0.0 collective-permute-done.5.refs_8_.refs_6_.refs_14_
  66.4 0.1 collective-permute-start.6
  66.5 0.5 collective-permute-start.7
  67.0 0.7 slice.70
  67.7 0.7 slice.71
  68.3 65.6 %halves.1 = (bf16[512,1024]{1,0:T(8,128)(2,1)}, bf16[528,1024]{1,0:T(8,128)(2,1)}) custom-call(bf16[1040,1024]{1,0:T(8,128)(2,1)} %collective-permute-done.1.refs_4_.a_ref, bf16[1040,1024]{1,0:T(8,128)(2,1)} %collective-permute-done.2.refs_5_.b_ref), custom_call_target="tpu_custom_call" | custom-call | tf_op jit(solution)/shard_map/halves/pallas_call | solution.py:113
  134.0 0.2 compare_reduce_fusion.2
  134.2 1.6 collective-permute-start.8
  135.8 1.9 collective-permute-start.10
  137.7 0.8 collective-permute-start.9
  138.5 0.7 reshape.117.live
  139.1 20.0 %near.1 = (f32[4,1024]{1,0:T(4,128)}, f32[3,1024]{1,0:T(4,128)}) custom-call(s32[12]{0:T(128)} %reshape.117.live, f32[2,1024]{1,0:T(2,128)} %get-tuple-element.63.refs_0_, f32[1,1024]{1,0:T(1,128)} %get-tuple-element.64.refs_1_, bf16[1040,1024]{1,0:T(8,128)(2,1)} %get-tuple-element.57.refs_2_.refs_4_.refs_6_.refs_12_, bf16[1040,1024]{1,0:T(8,128)(2,1)} %copy-done.5, ...), custom_call_target="tpu_custom_call" | custom-call | flops 6442450944 | bytes 14680064 | tf_op jit(solution)/shard_map/near/pallas_call | solution.py:366
  159.1 0.0 collective-permute-done.6.refs_2_.refs_6_
  159.1 0.0 collective-permute-done.7.refs_3_.refs_7_
  159.1 0.7 slice.73
  159.8 0.6 slice.74
  160.4 0.2 compare_reduce_fusion.1
  160.6 0.6 reshape.118.live
  161.3 9.0 %mid.1 = (f32[2,1024]{1,0:T(2,128)}, f32[3,1024]{1,0:T(4,128)}) custom-call(s32[6]{0:T(128)} %reshape.118.live, f32[1,1024]{1,0:T(1,128)} %broadcast_6_refs_0__refs_1_.2.refs_0_.refs_1_, f32[3,1024]{1,0:T(4,128)} %get-tuple-element.74.refs_1_, bf16[1040,1024]{1,0:T(8,128)(2,1)} %collective-permute-done.6.refs_2_.refs_6_, ...), custom_call_target="tpu_custom_call" | custom-call | flops 2147483648 | bytes 10485760 | tf_op jit(solution)/shard_map/mid/pallas_call | solution.py:366
  170.2 5.2 %collective-permute-done.10.refs_15_ = bf16[512,1024]{1,0:T(8,128)(2,1)} collective-permute-done((bf16[512,1024]{1,0:T(8,128)(2,1)}, bf16[512,1024]{1,0:T(8,128)(2,1)}, u32[]{:S(2)}, u32[]{:S(2)}) %collective-permute-start.10) | collective-permute-done | bytes 1048608 | tf_op jit(solution)/shard_map/ppermute | solution.py:43
  175.4 0.0 collective-permute-done.8.refs_8_
  175.4 0.0 collective-permute-done.9.refs_9_
  175.4 0.1 collective-permute-start.11
  175.5 0.5 collective-permute-start.12
  176.0 0.6 slice.76
  176.7 0.2 scatter.9
  176.9 1.3 pad_maximum_fusion.refs_0_
  178.2 0.2 collective-permute-done.11.refs_11_
  178.4 1.0 copy-done.6
  179.4 0.2 compare_reduce_fusion
  179.6 0.1 reshape.119
  179.7 0.7 pad_add_fusion.3.live
  180.4 0.0 collective-permute-done.12.refs_10_
  180.4 8.4 %far.1 = (f32[8,1,1024]{2,1,0:T(1,128)}, f32[1,1024]{1,0:T(1,128)}, f32[1,1024]{1,0:T(1,128)}) custom-call(s32[34]{0:T(128)} %pad_add_fusion.3.live, f32[6,1024]{1,0:T(8,128)} %pad_maximum_fusion.refs_0_, f32[3,1024]{1,0:T(4,128)} %get-tuple-element.79.refs_1_, bf16[1040,1024]{1,0:T(8,128)(2,1)} %get-tuple-element.57.refs_2_.refs_4_.refs_6_.refs_12_, ...), custom_call_target="tpu_custom_call" | custom-call | flops 17179869184 | bytes 25165824 | tf_op jit(solution)/shard_map/far/pallas_call | solution.py:366
  188.8 7.3 %all-to-all-start = ((f32[8,1,1024]{2,1,0:T(1,128)}), f32[8,1,1024]{2,1,0:T(1,128)S(1)}, u32[]{:S(2)}, u32[]{:S(2)}) async-start(f32[8,1,1024]{2,1,0:T(1,128)} %get-tuple-element.82), calls=%async_computation | async-start | bytes 65536 | tf_op jit(solution)/shard_map/all_to_all | solution.py:476
  196.2 12.0 %collective-permute-start.13 = (f32[1,1024]{1,0:T(1,128)}, f32[1,1024]{1,0:T(1,128)S(1)}, u32[]{:S(2)}, u32[]{:S(2)}) collective-permute-start(f32[1,1024]{1,0:T(1,128)} %get-tuple-element.83), channel_id=1, source_target_pairs={{0,8},{1,9},{2,10},{3,11},{4,12},{5,13},{6,14},{7,15},{8,16},{9,17... | collective-permute-start | bytes 12296 | tf_op jit(solution)/shard_map/ppermute | solution.py:43
  208.2 1.9 collective-permute-start.14
  210.2 0.0 collective-permute-done.13.refs_0_
  210.2 6.2 %collective-permute-done.14.refs_1_ = f32[1,1024]{1,0:T(1,128)S(1)} collective-permute-done((f32[1,1024]{1,0:T(1,128)}, f32[1,1024]{1,0:T(1,128)S(1)}, u32[]{:S(2)}, u32[]{:S(2)}) %collective-permute-start.14) | collective-permute-done | bytes 4128 | tf_op jit(solution)/shard_map/ppermute | solution.py:43
  216.3 0.0 all-to-all-done.ring_ref
  216.3 0.6 copy-done.4
  216.9 0.0 copy-done.1
  216.9 1.4 last_sum.1
  (29 shorter events, 0.2 us)
Async XLA Ops:
  4.7 8.7 %collective-permute-start = (bf16[1040,1024]{1,0:T(8,128)(2,1)}, bf16[1040,1024]{1,0:T(8,128)(2,1)S(1)}, u32[]{:S(2)}, u32[]{:S(2)}) collective-permute-start(bf16[1040,1024]{1,0:T(8,128)(2,1)} %get-tuple-element.57.refs_2_.refs_4_.refs_6_.refs_12_), channel_id=1, source_target_pairs={{0,1},{1,0},{2,3},{3,2},{4,5},{5,4},{6,7},{7,6},{8,9},{9,8},{10,11... | collective-permute-start | bytes 6389768 | tf_op jit(solution)/shard_map/ppermute | solution.py:43
  4.8 61.6 %collective-permute-start.3 = (bf16[1040,1024]{1,0:T(8,128)(2,1)}, bf16[1040,1024]{1,0:T(8,128)(2,1)}, u32[]{:S(2)}, u32[]{:S(2)}) collective-permute-start(bf16[1040,1024]{1,0:T(8,128)(2,1)} %get-tuple-element.57.refs_2_.refs_4_.refs_6_.refs_12_), channel_id=1, source_target_pairs={{8,0},{9,1},{10,2},{11,3},{12,4},{13,5},{14,6},{15,7},{16,8},{17,9... | collective-permute-start | bytes 6389768 | tf_op jit(solution)/shard_map/ppermute | solution.py:43
  9.3 57.1 %collective-permute-start.2 = (bf16[1040,1024]{1,0:T(8,128)(2,1)}, bf16[1040,1024]{1,0:T(8,128)(2,1)}, u32[]{:S(2)}, u32[]{:S(2)}) collective-permute-start(bf16[1040,1024]{1,0:T(8,128)(2,1)} %get-tuple-element.57.refs_2_.refs_4_.refs_6_.refs_12_), channel_id=1, source_target_pairs={{0,6},{1,7},{2,0},{3,1},{4,2},{5,3},{6,4},{7,5},{8,14},{9,15},{10,... | collective-permute-start | bytes 6389768 | tf_op jit(solution)/shard_map/ppermute | solution.py:43
  9.9 56.5 %collective-permute-start.1 = (bf16[1040,1024]{1,0:T(8,128)(2,1)}, bf16[1040,1024]{1,0:T(8,128)(2,1)}, u32[]{:S(2)}, u32[]{:S(2)}) collective-permute-start(bf16[1040,1024]{1,0:T(8,128)(2,1)} %get-tuple-element.57.refs_2_.refs_4_.refs_6_.refs_12_), channel_id=1, source_target_pairs={{0,2},{1,3},{2,4},{3,5},{4,6},{5,7},{6,0},{7,1},{8,10},{9,11},{10,... | collective-permute-start | bytes 6389768 | tf_op jit(solution)/shard_map/ppermute | solution.py:43
  11.3 26.1 %collective-permute-start.4 = (bf16[512,1024]{1,0:T(8,128)(2,1)}, bf16[512,1024]{1,0:T(8,128)(2,1)S(1)}, u32[]{:S(2)}, u32[]{:S(2)}) collective-permute-start(bf16[512,1024]{1,0:T(8,128)(2,1)} %get-tuple-element.58), channel_id=1, source_target_pairs={{0,8},{1,9},{2,10},{3,11},{4,12},{5,13},{6,14},{7,15},{8,16},{9,17... | collective-permute-start | bytes 3145736 | tf_op jit(solution)/shard_map/ppermute | solution.py:43
  13.4 1.4 copy-start.5
  37.5 1.0 copy-start.8
  38.5 27.9 %collective-permute-start.5 = (bf16[512,1024]{1,0:T(8,128)(2,1)}, bf16[512,1024]{1,0:T(8,128)(2,1)S(1)}, u32[]{:S(2)}, u32[]{:S(2)}) collective-permute-start(bf16[512,1024]{1,0:T(8,128)(2,1)} %copy-done.8), channel_id=1, source_target_pairs={{24,0},{25,1},{26,2},{27,3},{28,4},{29,5},{30,6},{31,7},{0,8},{1,9... | collective-permute-start | bytes 3145736 | tf_op jit(solution)/shard_map/ppermute | solution.py:43
  66.4 67.6 %copy-start = (bf16[512,1024]{1,0:T(8,128)(2,1)}, bf16[512,1024]{1,0:T(8,128)(2,1)S(1)}, u32[]{:S(2)}) copy-start(bf16[512,1024]{1,0:T(8,128)(2,1)S(1)} %collective-permute-done.5.refs_8_.refs_6_.refs_14_) | copy-start | bytes 3145732
  66.4 92.7 %collective-permute-start.6 = (bf16[1040,1024]{1,0:T(8,128)(2,1)}, bf16[1040,1024]{1,0:T(8,128)(2,1)}, u32[]{:S(2)}, u32[]{:S(2)}) collective-permute-start(bf16[1040,1024]{1,0:T(8,128)(2,1)} %collective-permute-done.1.refs_4_.a_ref), channel_id=1, source_target_pairs={{0,1},{1,0},{2,3},{3,2},{4,5},{5,4},{6,7},{7,6},{8,9},{9,8},{10,11... | collective-permute-start | bytes 6389768 | tf_op jit(solution)/shard_map/ppermute | solution.py:43
  66.5 92.6 %collective-permute-start.7 = (bf16[1040,1024]{1,0:T(8,128)(2,1)}, bf16[1040,1024]{1,0:T(8,128)(2,1)}, u32[]{:S(2)}, u32[]{:S(2)}) collective-permute-start(bf16[1040,1024]{1,0:T(8,128)(2,1)} %collective-permute-done.2.refs_5_.b_ref), channel_id=1, source_target_pairs={{0,1},{1,0},{2,3},{3,2},{4,5},{5,4},{6,7},{7,6},{8,9},{9,8},{10,11... | collective-permute-start | bytes 6389768 | tf_op jit(solution)/shard_map/ppermute | solution.py:43
  134.2 41.2 %collective-permute-start.8 = (bf16[512,1024]{1,0:T(8,128)(2,1)}, bf16[512,1024]{1,0:T(8,128)(2,1)S(1)}, u32[]{:S(2)}, u32[]{:S(2)}) collective-permute-start(bf16[512,1024]{1,0:T(8,128)(2,1)} %get-tuple-element.70), channel_id=1, source_target_pairs={{0,2},{1,3},{2,4},{3,5},{4,6},{5,7},{6,0},{7,1},{8,10},{9,11},{10,... | collective-permute-start | bytes 3145736 | tf_op jit(solution)/shard_map/ppermute | solution.py:43
  135.8 39.7 %collective-permute-start.10 = (bf16[512,1024]{1,0:T(8,128)(2,1)}, bf16[512,1024]{1,0:T(8,128)(2,1)}, u32[]{:S(2)}, u32[]{:S(2)}) collective-permute-start(bf16[512,1024]{1,0:T(8,128)(2,1)} %get-tuple-element.73), channel_id=1, source_target_pairs={{16,0},{17,1},{18,2},{19,3},{20,4},{21,5},{22,6},{23,7},{24,8},{25... | collective-permute-start | bytes 3145736 | tf_op jit(solution)/shard_map/ppermute | solution.py:43
  137.7 37.8 %collective-permute-start.9 = (bf16[528,1024]{1,0:T(8,128)(2,1)}, bf16[528,1024]{1,0:T(8,128)(2,1)}, u32[]{:S(2)}, u32[]{:S(2)}) collective-permute-start(bf16[528,1024]{1,0:T(8,128)(2,1)} %get-tuple-element.71), channel_id=1, source_target_pairs={{0,6},{1,7},{2,0},{3,1},{4,2},{5,3},{6,4},{7,5},{8,14},{9,15},{10,... | collective-permute-start | bytes 3244040 | tf_op jit(solution)/shard_map/ppermute | solution.py:43
  161.3 15.6 %copy-start.2 = (f32[4,1024]{1,0:T(4,128)S(1)}, f32[4,1024]{1,0:T(4,128)}, u32[]{:S(2)}) copy-start(f32[4,1024]{1,0:T(4,128)} %get-tuple-element.77) | copy-start | bytes 49156
  175.4 5.0 %copy-start.7 = (bf16[512,1024]{1,0:T(8,128)(2,1)}, bf16[512,1024]{1,0:T(8,128)(2,1)S(1)}, u32[]{:S(2)}) copy-start(bf16[512,1024]{1,0:T(8,128)(2,1)S(1)} %collective-permute-done.8.refs_8_) | copy-start | bytes 3145732
  175.4 3.0 %collective-permute-start.11 = (bf16[528,1024]{1,0:T(8,128)(2,1)}, bf16[528,1024]{1,0:T(8,128)(2,1)S(1)}, u32[]{:S(2)}, u32[]{:S(2)}) collective-permute-start(bf16[528,1024]{1,0:T(8,128)(2,1)} %collective-permute-done.9.refs_9_), channel_id=1, source_target_pairs={{0,1},{1,0},{2,3},{3,2},{4,5},{5,4},{6,7},{7,6},{8,9},{9,8},{10,11... | collective-permute-start | bytes 3244040 | tf_op jit(solution)/shard_map/ppermute | solution.py:43
  175.5 4.9 %collective-permute-start.12 = (bf16[512,1024]{1,0:T(8,128)(2,1)S(1)}, bf16[512,1024]{1,0:T(8,128)(2,1)}, u32[]{:S(2)}, u32[]{:S(2)}) collective-permute-start(bf16[512,1024]{1,0:T(8,128)(2,1)S(1)} %collective-permute-done.8.refs_8_), channel_id=1, source_target_pairs={{0,1},{1,0},{2,3},{3,2},{4,5},{5,4},{6,7},{7,6},{8,9},{9,8},{10,11... | collective-permute-start | bytes 3145736 | tf_op jit(solution)/shard_map/ppermute | solution.py:43
  178.4 1.0 copy-start.6
  188.8 27.5 %all-to-all-start = ((f32[8,1,1024]{2,1,0:T(1,128)}), f32[8,1,1024]{2,1,0:T(1,128)S(1)}, u32[]{:S(2)}, u32[]{:S(2)}) async-start(f32[8,1,1024]{2,1,0:T(1,128)} %get-tuple-element.82), calls=%async_computation | async-start | bytes 65536 | tf_op jit(solution)/shard_map/all_to_all | solution.py:476
  196.2 14.0 %collective-permute-start.13 = (f32[1,1024]{1,0:T(1,128)}, f32[1,1024]{1,0:T(1,128)S(1)}, u32[]{:S(2)}, u32[]{:S(2)}) collective-permute-start(f32[1,1024]{1,0:T(1,128)} %get-tuple-element.83), channel_id=1, source_target_pairs={{0,8},{1,9},{2,10},{3,11},{4,12},{5,13},{6,14},{7,15},{8,16},{9,17... | collective-permute-start | bytes 12296 | tf_op jit(solution)/shard_map/ppermute | solution.py:43
  208.2 8.1 %collective-permute-start.14 = (f32[1,1024]{1,0:T(1,128)}, f32[1,1024]{1,0:T(1,128)S(1)}, u32[]{:S(2)}, u32[]{:S(2)}) collective-permute-start(f32[1,1024]{1,0:T(1,128)} %get-tuple-element.84), channel_id=1, source_target_pairs={{0,16},{1,17},{2,18},{3,19},{4,20},{5,21},{6,22},{7,23},{8,24},{9,... | collective-permute-start | bytes 12296 | tf_op jit(solution)/shard_map/ppermute | solution.py:43
  210.2 6.2 %copy-start.3 = (f32[1,1024]{1,0:T(1,128)}, f32[1,1024]{1,0:T(1,128)S(1)}, u32[]{:S(2)}) copy-start(f32[1,1024]{1,0:T(1,128)S(1)} %collective-permute-done.13.refs_0_) | copy-start | bytes 12292
  216.3 0.6 copy-start.4
  216.3 0.6 copy-start.1
